TPU v7x, 512 devices: a whole 4x8x8 slice. The times are simulated.
512 devices in a mesh: sky: 32 (over y_hi, z, core), chan: 16 (over x, y_lo).
Axes of the slice: x: 4, y: 8 (y_hi: 2, y_lo: 4; y = y_hi * 4 + y_lo), z: 8, core: 2. Of those that a mesh axis runs over, the one named last changes fastest.
Arguments:
- cube: float32 [16, 768, 8192], P('chan', 'sky')
- noise_weight: float32 [16, 768, 8192], P('chan', 'sky'), may hold values from 0.25 to 4
- spectral_halo: float32 [8, 768, 8192], P(None, 'sky', 'chan'), may hold values from -6 to 6
- source_mask: int32 [768, 8192], P('sky', 'chan'), may hold values from 0 to 1, as said below
- tile_flags: int32 [96, 16], P('sky', 'chan'), may hold values from 0 to 1, as said below
- halo_width: int32 [2, 16], P(None, 'chan'), may hold values from 0 to 4, as said below
Outputs:
- normalized: float32 [3, 16, 768, 8192], P(None, None, 'sky', 'chan')
Inputs may be any that keep to these rules, and one draw needn't show every extreme that they name: `halo_width`: in every column of tiles both entries lie in 0 .. 4, and one of them equals 4. `source_mask`: some noise tiles lie wholly in sources. A noise tile whose pixels all have source_mask 1 has tile_flags 0.
All inputs are finite; a program needn't handle non-finite values.
Results may differ from a plain program's by a relative error of at most 0.0001.
Values sent between devices are 32-bit elements; how exact they have to be, the bound alone decides.
No kernel may reach another device: no remote copies, remote signals or barrier semaphores. Data moves between devices by JAX's collectives and lax.ppermute only.
A program may use at most 64 MiB of HBM per device.

v0:
```python
import math

import jax
import jax.numpy as jnp
from jax import lax
from jax.sharding import PartitionSpec as P

RAD = 8
HW = 4
TILE_R = 8
TILE_C = 512


def padded_2(block, sides, width):
    for axis, dim in sides:
        count = lax.axis_size(axis)
        forward = [(i, i + 1) for i in range(count - 1)]
        backward = [(target, source) for source, target in forward]
        low = lax.ppermute(
            lax.slice_in_dim(block, block.shape[dim] - width, None, axis=dim), axis, forward
        )
        high = lax.ppermute(lax.slice_in_dim(block, 0, width, axis=dim), axis, backward)
        block = jnp.concatenate([low, block, high], axis=dim)
    return block


def tap_list():
    sigma = RAD / 2.5
    return [math.exp(-((shift - RAD) ** 2) / (2.0 * sigma * sigma)) for shift in range(2 * RAD + 1)]


def smooth_along(padded, axis, taps, length):
    total = taps[0] * lax.slice_in_dim(padded, 0, length, axis=axis)
    for shift in range(1, 2 * RAD + 1):
        total = total + taps[shift] * lax.slice_in_dim(padded, shift, shift + length, axis=axis)
    return total


def local(cube, noise_weight, spectral_halo, source_mask, tile_flags, halo_width):
    taps = tap_list()
    stacked = jnp.stack([noise_weight * cube, noise_weight])
    rows = cube.shape[1]
    moved = lax.all_to_all(stacked, "chan", split_axis=3, concat_axis=1, tiled=True)
    cols = moved.shape[3]
    wide = padded_2(moved, (("chan", 3),), RAD)
    across = smooth_along(wide, 3, taps, cols)
    tall = padded_2(across, (("sky", 2),), RAD)
    both = smooth_along(tall, 2, taps, rows)
    smoothed = both[0] / both[1]
    channels, cols = (smoothed.shape[0], smoothed.shape[2])
    place = jnp.arange(HW, dtype=jnp.int32)[:, None]
    lower_keep = (place >= HW - halo_width[0][None, :]).astype(jnp.float32)
    upper_keep = (place < halo_width[1][None, :]).astype(jnp.float32)
    lower_keep = jnp.repeat(lower_keep, TILE_C, axis=1)
    upper_keep = jnp.repeat(upper_keep, TILE_C, axis=1)
    extended = jnp.concatenate(
        [
            spectral_halo[:HW] * lower_keep[:, None, :],
            smoothed,
            spectral_halo[HW:] * upper_keep[:, None, :],
        ],
        0,
    )
    keep = (source_mask == 0).astype(jnp.float32)
    tiles_r, tiles_c = (rows // TILE_R, cols // TILE_C)
    count = jnp.sum(keep.reshape(tiles_r, TILE_R, tiles_c, TILE_C), axis=(1, 3)) * channels
    flags = tile_flags.astype(jnp.float32)
    results = []
    for width in (3, 5, 9):
        half = width // 2
        boxcar = extended[HW - half : HW - half + channels]
        for shift in range(1, width):
            boxcar = boxcar + extended[HW - half + shift : HW - half + shift + channels]
        boxcar = boxcar / width
        squares = (boxcar * boxcar * keep[None]).reshape(channels, tiles_r, TILE_R, tiles_c, TILE_C)
        total = jnp.sum(squares, axis=(0, 2, 4))
        spread = jnp.sqrt(total / jnp.maximum(count, 1.0) + 1e-06)
        factor = flags / spread
        factor = jnp.repeat(jnp.repeat(factor, TILE_R, axis=0), TILE_C, axis=1)
        results.append(boxcar * factor[None])
    return jnp.stack(results)


def solution(mesh):
    placed = (
        P("chan", "sky", None),
        P("chan", "sky", None),
        P(None, "sky", "chan"),
        P("sky", "chan"),
        P("sky", "chan"),
        P(None, "chan"),
    )
    return jax.shard_map(
        local, mesh=mesh, in_specs=placed, out_specs=P(None, None, "sky", "chan"), check_vma=False
    )
```

profile of v0, /device:TPU:48, one launch (start us, length us, event | category | flops | bytes accessed | tf_op | source)
XLA Modules:
  0.0 206.1 jit_solution(13508743781086674498)
XLA Ops:
  0.0 1.5 multiply_bitcast_fusion.3
  1.6 0.1 pad_maximum_fusion.5
  1.7 12.7 %copy.18 = f32[2,1,24,8192]{2,1,0,3:T(1,128)} copy(f32[2,1,24,8192]{3,2,1,0:T(8,128)S(1)} %pad_maximum_fusion.5) | data formatting | bytes 3145728 | tf_op jit(solution)/shard_map/stack | solution.py:41
  14.4 0.5 broadcast.210
  14.9 30.5 %reduce.12 = f32[8192,2,24]{2,1,0:T(2,128)} reduce(f32[8192,2,1,24]{3,2,1,0:T(1,128)} %bitcast.45, f32[]{:T(128)} %broadcast.210), dimensions={2}, to_apply=%bitcast.41.reduce_sub_computation | reduce | bytes 3145732
  45.4 15.4 %reshape.137 = f32[16,1,24576]{2,1,0:T(1,128)} reshape(f32[8192,2,24]{2,1,0:T(2,128)} %reduce.12) | data formatting | bytes 3145728
  60.8 6.9 %all-to-all-start = ((f32[16,1,24576]{2,1,0:T(1,128)}), f32[16,1,24576]{2,1,0:T(1,128)S(1)}, u32[]{:S(2)}, u32[]{:S(2)}) async-start(f32[16,1,24576]{2,1,0:T(1,128)} %reshape.137), calls=%async_computation | async-start | bytes 3145728 | tf_op jit(solution)/shard_map/all_to_all | solution.py:43
  67.7 0.6 fusion.120
  69.0 0.1 fusion.113
  69.1 0.6 compare_convert_fusion
  69.7 31.7 %all-to-all-done = f32[16,1,24576]{2,1,0:T(1,128)S(1)} async-done(((f32[16,1,24576]{2,1,0:T(1,128)}), f32[16,1,24576]{2,1,0:T(1,128)S(1)}, u32[]{:S(2)}, u32[]{:S(2)}) %all-to-all-start) | async-done | bytes 1572896 | tf_op jit(solution)/shard_map/all_to_all | solution.py:43
  101.4 4.3 %reduce.13 = f32[16,24576]{1,0:T(8,128)S(1)} reduce(f32[16,1,24576]{2,1,0:T(1,128)S(1)} %all-to-all-done, f32[]{:T(128)} %broadcast.210), dimensions={1}, to_apply=%all_to_all.13.reduce_sub_computation | reduce | bytes 3145732 | tf_op jit(solution)/shard_map/all_to_all | solution.py:43
  105.8 18.6 %reshape.138 = f32[8192,2,1,24]{3,2,1,0:T(1,128)} reshape(f32[16,24576]{1,0:T(8,128)S(1)} %reduce.13) | data formatting | bytes 3145728
  124.4 6.8 %copy.22 = f32[2,1,24,16,512]{4,3,2,0,1:T(8,128)S(1)} copy(f32[2,1,24,16,512]{2,0,4,3,1:T(2,128)} %bitcast.46) | data formatting | bytes 3145728 | tf_op jit(solution)/shard_map/all_to_all | solution.py:43
  131.2 0.2 fusion.118
  131.4 5.0 %collective-permute-start = (f32[2,16,24,8]{3,1,2,0:T(8,128)S(1)}, f32[2,16,24,8]{3,1,2,0:T(8,128)S(1)}, u32[]{:S(2)}, u32[]{:S(2)}) collective-permute-start(f32[2,16,24,8]{3,1,2,0:T(8,128)S(1)} %get-tuple-element.14), channel_id=1, source_target_pairs={{0,1},{1,2},{2,3},{3,4},{4,5},{5,6},{6,7},{7,8},{8,9},{9,10},{10,1... | collective-permute-start | bytes 73736 | tf_op jit(solution)/shard_map/ppermute | solution.py:19
  136.5 1.9 collective-permute-start.1
  138.4 6.6 %collective-permute-done = f32[2,16,24,8]{3,1,2,0:T(8,128)S(1)} collective-permute-done((f32[2,16,24,8]{3,1,2,0:T(8,128)S(1)}, f32[2,16,24,8]{3,1,2,0:T(8,128)S(1)}, u32[]{:S(2)}, u32[]{:S(2)}) %collective-permute-start) | collective-permute-done | bytes 24608 | tf_op jit(solution)/shard_map/ppermute | solution.py:19
  145.0 10.2 %collective-permute-done.1 = f32[2,16,24,8]{3,1,2,0:T(8,128)S(1)} collective-permute-done((f32[2,16,24,8]{3,1,2,0:T(8,128)S(1)}, f32[2,16,24,8]{3,1,2,0:T(8,128)S(1)}, u32[]{:S(2)}, u32[]{:S(2)}) %collective-permute-start.1) | collective-permute-done | bytes 24608 | tf_op jit(solution)/shard_map/ppermute | solution.py:22
  155.2 9.5 %fusion.3 = f32[2,16,24,512]{3,1,2,0:T(8,128)S(1)} fusion(f32[2,16,24,512]{3,1,2,0:T(8,128)S(1)} %bitcast.48, f32[2,16,24,8]{3,1,2,0:T(8,128)S(1)} %collective-permute-done.1, f32[2,16,24,8]{3,1,2,0:T(8,128)S(1)} %collective-permute-done), kind=kLoop, calls=%fused_computation.66 | loop fusion | flops 18874368 | bytes 3194880 | tf_op jit(solution)/shard_map/add | solution.py:35
  164.7 0.1 fusion.117
  164.8 1.9 collective-permute-start.2
  166.8 11.8 %collective-permute-start.3 = (f32[2,16,8,512]{3,1,2,0:T(8,128)S(1)}, f32[2,16,8,512]{3,1,2,0:T(8,128)}, u32[]{:S(2)}, u32[]{:S(2)}) collective-permute-start(f32[2,16,8,512]{3,1,2,0:T(8,128)S(1)} %get-tuple-element.13), channel_id=1, source_target_pairs={{16,0},{32,16},{48,32},{64,48},{80,64},{96,80},{112,96},{128,112},... | collective-permute-start | bytes 1572872 | tf_op jit(solution)/shard_map/ppermute | solution.py:22
  178.5 0.6 compare_convert_fusion.1
  179.2 0.1 reduce_sum.53
  179.3 0.1 reduce_sum.54
  179.4 0.3 copy_multiply_fusion
  179.7 9.5 %collective-permute-done.2 = f32[2,16,8,512]{3,1,2,0:T(8,128)} collective-permute-done((f32[2,16,8,512]{3,1,2,0:T(8,128)S(1)}, f32[2,16,8,512]{3,1,2,0:T(8,128)}, u32[]{:S(2)}, u32[]{:S(2)}) %collective-permute-start.2) | collective-permute-done | bytes 524320 | tf_op jit(solution)/shard_map/ppermute | solution.py:19
  189.2 1.7 collective-permute-done.3
  190.8 5.6 %fusion.47 = f32[2,16,24,512]{3,1,2,0:T(8,128)S(1)} fusion(f32[2,16,24,512]{3,1,2,0:T(8,128)S(1)} %fusion.3, f32[2,16,8,512]{3,1,2,0:T(8,128)} %collective-permute-done.3, f32[2,16,8,512]{3,1,2,0:T(8,128)} %collective-permute-done.2), kind=kLoop, calls=%fused_computation.110 | loop fusion | flops 18874368 | bytes 4194304 | tf_op jit(solution)/shard_map/add | solution.py:35
  196.5 0.2 fusion.106
  196.7 0.6 copy-done.4
  197.3 2.9 %multiply_reduce_fusion.2 = (f32[24]{0:T(128)S(1)}, f32[24]{0:T(128)S(1)}, f32[24]{0:T(128)S(1)}, f32[16,24,512]{2,0,1:T(8,128)S(1)}, f32[16,24,512]{2,0,1:T(8,1...) fusion(f32[24,512]{1,0:T(8,128)S(1)} %copy-done.4, f32[16,24,512]{2,0,1:T(8,128)S(1)} %fusion.106, ...), kind=kLoop, calls=%fused_computation.190 | loop fusion | flops 7077816 | bytes 4374816 | tf_op jit(solution)/shard_map/reduce_sum | solution.py:76
  200.2 0.1 reduce_sum.47
  200.3 0.1 reduce_sum.51
  200.5 0.1 reduce_sum.72
  200.6 0.1 reduce_sum.74
  200.7 0.1 reduce_sum.75
  200.9 0.1 mul.244
  201.1 0.1 mul.252
  201.2 0.1 mul.260
  201.3 0.1 multiply_bitcast_fusion.1
  201.5 0.1 multiply_bitcast_fusion
  201.6 0.9 copy-done
  202.5 0.2 copy-done.1
  202.7 0.2 multiply_bitcast_fusion.2
  202.9 0.4 pad_maximum_fusion
  203.3 2.8 %copy.21 = f32[3,16,24,512]{3,2,1,0:T(8,128)} copy(f32[3,16,24,512]{3,1,2,0:T(8,128)S(1)} %pad_maximum_fusion) | data formatting | bytes 4718592 | tf_op jit(solution)/shard_map/stack | solution.py:81
  (20 shorter events, 0.4 us)
Async XLA Ops:
  0.0 1.6 copy-start.2
  60.8 6.9 %copy-start.6 = (s32[2,1]{0,1:T(1,128)S(1)}, s32[2,1]{0,1:T(1,128)}, u32[]{:S(2)}) copy-start(s32[2,1]{0,1:T(1,128)} %param.11) | copy-start | bytes 28
  60.8 8.2 %copy-start.5 = (s32[24,512]{1,0:T(8,128)S(1)}, s32[24,512]{1,0:T(8,128)}, u32[]{:S(2)}) copy-start(s32[24,512]{1,0:T(8,128)} %param.9) | copy-start | bytes 147460
  60.8 40.6 %all-to-all-start = ((f32[16,1,24576]{2,1,0:T(1,128)}), f32[16,1,24576]{2,1,0:T(1,128)S(1)}, u32[]{:S(2)}, u32[]{:S(2)}) async-start(f32[16,1,24576]{2,1,0:T(1,128)} %reshape.137), calls=%async_computation | async-start | bytes 3145728 | tf_op jit(solution)/shard_map/all_to_all | solution.py:43
  131.4 13.6 %collective-permute-start = (f32[2,16,24,8]{3,1,2,0:T(8,128)S(1)}, f32[2,16,24,8]{3,1,2,0:T(8,128)S(1)}, u32[]{:S(2)}, u32[]{:S(2)}) collective-permute-start(f32[2,16,24,8]{3,1,2,0:T(8,128)S(1)} %get-tuple-element.14), channel_id=1, source_target_pairs={{0,1},{1,2},{2,3},{3,4},{4,5},{5,6},{6,7},{7,8},{8,9},{9,10},{10,1... | collective-permute-start | bytes 73736 | tf_op jit(solution)/shard_map/ppermute | solution.py:19
  136.5 18.7 %collective-permute-start.1 = (f32[2,16,24,8]{3,1,2,0:T(8,128)S(1)}, f32[2,16,24,8]{3,1,2,0:T(8,128)S(1)}, u32[]{:S(2)}, u32[]{:S(2)}) collective-permute-start(f32[2,16,24,8]{3,1,2,0:T(8,128)S(1)} %get-tuple-element.15), channel_id=1, source_target_pairs={{1,0},{2,1},{3,2},{4,3},{5,4},{6,5},{7,6},{8,7},{9,8},{10,9},{11,1... | collective-permute-start | bytes 73736 | tf_op jit(solution)/shard_map/ppermute | solution.py:22
  164.7 14.7 %copy-start.3 = (f32[8,24,512]{2,1,0:T(8,128)S(1)}, f32[8,24,512]{2,1,0:T(8,128)}, u32[]{:S(2)}) copy-start(f32[8,24,512]{2,1,0:T(8,128)} %param.8) | copy-start | bytes 1179652
  164.8 24.3 %collective-permute-start.2 = (f32[2,16,8,512]{3,1,2,0:T(8,128)S(1)}, f32[2,16,8,512]{3,1,2,0:T(8,128)}, u32[]{:S(2)}, u32[]{:S(2)}) collective-permute-start(f32[2,16,8,512]{3,1,2,0:T(8,128)S(1)} %get-tuple-element.12), channel_id=1, source_target_pairs={{0,16},{16,32},{32,48},{48,64},{64,80},{80,96},{96,112},{112,128},... | collective-permute-start | bytes 1572872 | tf_op jit(solution)/shard_map/ppermute | solution.py:19
  166.8 24.1 %collective-permute-start.3 = (f32[2,16,8,512]{3,1,2,0:T(8,128)S(1)}, f32[2,16,8,512]{3,1,2,0:T(8,128)}, u32[]{:S(2)}, u32[]{:S(2)}) collective-permute-start(f32[2,16,8,512]{3,1,2,0:T(8,128)S(1)} %get-tuple-element.13), channel_id=1, source_target_pairs={{16,0},{32,16},{48,32},{64,48},{80,64},{96,80},{112,96},{128,112},... | collective-permute-start | bytes 1572872 | tf_op jit(solution)/shard_map/ppermute | solution.py:22
  196.5 0.8 copy-start.4
  197.3 3.6 %copy-start.7 = (s32[3,1]{0,1:T(1,128)S(1)}, s32[3,1]{0,1:T(1,128)}, u32[]{:S(2)}) copy-start(s32[3,1]{0,1:T(1,128)} %param.10) | copy-start | bytes 40
  201.3 1.1 copy-start
  201.3 1.4 copy-start.1
where the time goes:
time: 207 us; the launch traced here: 206 us
  local copies, waits for them, and re-layouts  60.4 us (29%)
  waiting for transfers between devices  59.6 us (29%)
  other arithmetic  57.6 us (28%)
  starting transfers between devices  27.5 us (13%)
    unnamed x19, local copies, waits for them, and re-layouts  36.4 us
    all_to_all x1, waiting for transfers between devices, local(): lax.all_to_all(stacked, 'chan', split_axis=3, concat_axis=1, tiled=True)  31.7 us
    unnamed x1, other arithmetic  30.5 us
    ppermute x2, waiting for transfers between devices, padded_2(): lax.ppermute(lax.slice_in_dim(block, block.shape[dim] - width, None, axis...  16.1 us
    add x2, other arithmetic, smooth_along(): total + taps[shift] * lax.slice_in_dim(padded, shift, shift + length, axi...  15.2 us
    ppermute x2, starting transfers between devices, padded_2(): lax.ppermute(lax.slice_in_dim(block, 0, width, axis=dim), axis, backward)  13.7 us
    another operation x1, local copies, waits for them, and re-layouts, local(): stacked = jnp.stack([noise_weight * cube, noise_weight])  12.7 us
    ppermute x2, waiting for transfers between devices, padded_2(): lax.ppermute(lax.slice_in_dim(block, 0, width, axis=dim), axis, backward)  11.8 us
  transfers between devices with their start and end apart: 5, of which 5 were waited for; matrix products, arithmetic and copies ran while one was open for 1% of the time, Pallas kernels for 0%

commit v1 on v0

v1 whole, which is shorter than its diff:
```python
import functools
import math

import jax
import jax.numpy as jnp
import ml_dtypes
import numpy as np
from jax import lax
from jax.experimental import pallas as pl
from jax.experimental.pallas import tpu as pltpu
from jax.sharding import PartitionSpec as P

RAD = 8
HW = 4
TILE_R = 8
TILE_C = 512
BLK = 256
LANES = 128


def tap_list():
    sigma = RAD / 2.5
    return [math.exp(-((shift - RAD) ** 2) / (2.0 * sigma * sigma)) for shift in range(2 * RAD + 1)]


TAPS = tap_list()[RAD:]


def band_matrices():
    source = np.concatenate([np.arange(BLK), np.arange(-LANES, 0), np.arange(BLK, BLK + LANES)])
    reach = np.abs(source[:, None] - np.arange(BLK)[None, :])
    band = np.where(reach <= RAD, np.asarray(TAPS + [0.0])[np.minimum(reach, RAD + 1)], 0.0)
    high = band.astype(np.float32).astype(ml_dtypes.bfloat16)
    low = (band - high.astype(np.float64)).astype(np.float32).astype(ml_dtypes.bfloat16)
    return np.concatenate([high, high], axis=0), low


def column_taps(tiles):
    count, width = len(tiles), tiles[0].shape[1]
    row = lax.broadcasted_iota(jnp.int32, (TILE_R, width), 0)
    totals = [
        TAPS[RAD] * (tiles[i] + tiles[i + 2]) + TAPS[0] * tiles[i + 1] for i in range(count - 2)
    ]
    for shift in range(1, TILE_R):
        rolled = [pltpu.roll(tile, TILE_R - shift, 0) for tile in tiles]
        joined = [
            jnp.where(row < TILE_R - shift, rolled[i], rolled[i + 1]) for i in range(count - 1)
        ]
        for i in range(count - 2):
            totals[i] = totals[i] + (TAPS[TILE_R - shift] * joined[i] + TAPS[shift] * joined[i + 1])
    return totals


def smooth_kernel(late, side_ref, cube_ref, weight_ref, halo_ref, high_ref, low_ref, out_ref, split):
    side = side_ref[0]
    even = side == 0
    tiles_out = 1 if late else 2
    rows = tiles_out * TILE_R
    blocks = cube_ref.shape[2] // BLK
    split[1, :, BLK : BLK + LANES] = jnp.zeros((2 * rows, LANES), jnp.bfloat16)
    split[1, :, 3 * BLK : 3 * BLK + LANES] = jnp.zeros((2 * rows, LANES), jnp.bfloat16)
    split[blocks, :, BLK + LANES : 2 * BLK] = jnp.zeros((2 * rows, LANES), jnp.bfloat16)
    split[blocks, :, 3 * BLK + LANES :] = jnp.zeros((2 * rows, LANES), jnp.bfloat16)

    def window(ref, halo, cols):
        tile = lambda index: ref[0, pl.ds(pl.multiple_of(index * TILE_R, TILE_R), TILE_R), cols]
        if late:
            middle = tile(1)
            return [jnp.where(even, halo, middle), tile(2 * side), jnp.where(even, middle, halo)]
        return [
            jnp.where(even, tile(0), halo),
            tile(1 - side),
            tile(2 - side),
            jnp.where(even, halo, tile(2)),
        ]

    def rows_step(block, carry):
        cols = pl.ds(pl.multiple_of(block * BLK, BLK), BLK)
        weights = window(weight_ref, halo_ref[1, :, cols], cols)
        values = window(cube_ref, halo_ref[0, :, cols], cols)
        values = [value * weight for value, weight in zip(values, weights)]
        both = jnp.concatenate(column_taps(values) + column_taps(weights), axis=0)
        high = both.astype(jnp.bfloat16)
        low = (both - high.astype(jnp.float32)).astype(jnp.bfloat16)
        for part, base in ((high, 0), (low, 2 * BLK)):
            split[block + 1, :, base : base + BLK] = part
            split[block + 2, :, base + BLK : base + BLK + LANES] = part[:, LANES:]
            split[block, :, base + BLK + LANES : base + 2 * BLK] = part[:, :LANES]
        return carry

    lax.fori_loop(0, blocks, rows_step, 0)

    group = 8 if late else 4

    def columns_step(step, carry):
        part = split[pl.ds(step * group + 1, group)].reshape(group * 2 * rows, 4 * BLK)
        both = jnp.dot(part, high_ref[...], preferred_element_type=jnp.float32)
        both += jnp.dot(part[:, : 2 * BLK], low_ref[...], preferred_element_type=jnp.float32)
        both = both.reshape(group, 2 * rows, BLK)
        ratio = both[:, :rows] / both[:, rows:]
        for i in range(group):
            out_ref[step * (group // 2) + i // 2, :, (i % 2) * BLK : (i % 2 + 1) * BLK] = ratio[i]
        return carry

    lax.fori_loop(0, blocks // group, columns_step, 0)


def smooth_rows(late, side, cube, weight, halo, high, low):
    rows = TILE_R if late else 2 * TILE_R
    columns = cube.shape[2]
    blocks = columns // BLK
    whole = pl.BlockSpec(memory_space=pltpu.VMEM)
    return pl.pallas_call(
        functools.partial(smooth_kernel, late),
        out_shape=jax.ShapeDtypeStruct((columns // TILE_C, rows, TILE_C), jnp.float32),
        in_specs=[pl.BlockSpec(memory_space=pltpu.SMEM)] + [whole] * 5,
        out_specs=whole,
        scratch_shapes=[pltpu.VMEM((blocks + 2, 2 * rows, 4 * BLK), jnp.bfloat16)],
        compiler_params=pltpu.CompilerParams(vmem_limit_bytes=24 * 1024 * 1024),
        cost_estimate=pl.CostEstimate(
            flops=4 * rows * columns * 2 * BLK, bytes_accessed=16 * rows * columns, transcendentals=0
        ),
    )(side, cube, weight, halo, high, low)


def norm_kernel(base, tiles_ref, smooth_ref, halo_ref, mask_ref, flags_ref, width_ref, *rest):
    out_ref = rest[-1]
    channels = smooth_ref.shape[0]
    tile = tiles_ref[0] + pl.program_id(0)
    keep_low = [(j >= HW - width_ref[0, 0]).astype(jnp.float32) for j in range(HW)]
    keep_high = [(j < width_ref[1, 0]).astype(jnp.float32) for j in range(HW)]
    sums = [jnp.zeros((TILE_R, LANES), jnp.float32) for _ in range(3)]
    kept = jnp.zeros((TILE_R, LANES), jnp.float32)
    for strip in range(TILE_C // LANES):
        cols = slice(strip * LANES, (strip + 1) * LANES)
        keep = (mask_ref[:, cols] == 0).astype(jnp.float32)
        kept = kept + keep
        extended = [halo_ref[j, :, cols] * keep_low[j] for j in range(HW)]
        extended += [smooth_ref[c, :, cols] for c in range(channels)]
        extended += [halo_ref[HW + j, :, cols] * keep_high[j] for j in range(HW)]
        squares = [jnp.zeros((TILE_R, LANES), jnp.float32) for _ in range(3)]
        for c in range(channels):
            at = c + HW
            three = extended[at - 1] + extended[at] + extended[at + 1]
            five = three + (extended[at - 2] + extended[at + 2])
            nine = five + ((extended[at - 3] + extended[at + 3]) + (extended[at - 4] + extended[at + 4]))
            for i, (total, width) in enumerate(((three, 3), (five, 5), (nine, 9))):
                boxcar = total * (1.0 / width)
                out_ref[i, c, :, cols] = boxcar
                squares[i] = squares[i] + boxcar * boxcar
        sums = [total + square * keep for total, square in zip(sums, squares)]

    def whole(x):
        return jnp.sum(jnp.sum(x, axis=1, keepdims=True), axis=0, keepdims=True)

    count = jnp.maximum(whole(kept) * channels, 1.0)
    flag = flags_ref[tile, 0].astype(jnp.float32)
    for i in range(3):
        factor = flag / jnp.sqrt(whole(sums[i]) / count + 1e-06)
        factor = jnp.broadcast_to(factor, (TILE_R, TILE_C))
        for c in range(channels):
            out_ref[i, c] = out_ref[i, c] * factor


def normalize(first, smoothed, halo, mask, flags, widths, before=None):
    channels, rows, columns = smoothed.shape
    steps = rows // TILE_R
    out = jax.ShapeDtypeStruct((3, channels) + mask.shape, jnp.float32)
    in_specs = [
        pl.BlockSpec((channels, TILE_R, columns), lambda i, at: (0, i, 0)),
        pl.BlockSpec((2 * HW, TILE_R, columns), lambda i, at: (0, at[0] + i, 0)),
        pl.BlockSpec((TILE_R, columns), lambda i, at: (at[0] + i, 0)),
        pl.BlockSpec(memory_space=pltpu.SMEM),
        pl.BlockSpec(memory_space=pltpu.SMEM),
    ]
    operands = [first, smoothed, halo, mask, flags, widths]
    aliases = {}
    if before is not None:
        in_specs.append(pl.BlockSpec(memory_space=pl.ANY))
        operands.append(before)
        aliases = {6: 0}
    return pl.pallas_call(
        functools.partial(norm_kernel, None),
        out_shape=out,
        grid_spec=pltpu.PrefetchScalarGridSpec(
            num_scalar_prefetch=1,
            grid=(steps,),
            in_specs=in_specs,
            out_specs=pl.BlockSpec(
                (3, channels, TILE_R, columns), lambda i, at: (0, 0, at[0] + i, 0)
            ),
        ),
        input_output_aliases=aliases,
        compiler_params=pltpu.CompilerParams(vmem_limit_bytes=16 * 1024 * 1024),
        cost_estimate=pl.CostEstimate(
            flops=30 * smoothed.size, bytes_accessed=20 * smoothed.size, transcendentals=0
        ),
    )(*operands)


def local(cube, noise_weight, spectral_halo, source_mask, tile_flags, halo_width):
    high, low = (jnp.asarray(part) for part in band_matrices())
    sky = lax.axis_size("sky")
    side = lax.axis_index("sky") % 2
    last = cube.shape[1] - TILE_R
    near = [(i, i ^ 1) for i in range(sky)]
    far = [(i, i + 1) for i in range(1, sky - 1, 2)]
    far = far + [(target, source) for source, target in far]

    def edge(start):
        return jnp.concatenate(
            [lax.dynamic_slice_in_dim(part, start, TILE_R, axis=1) for part in (cube, noise_weight)], axis=0
        )

    far_halo = lax.ppermute(edge(side * last), "sky", far)
    near_halo = lax.ppermute(edge((1 - side) * last), "sky", near)
    sides = jnp.reshape(side, (1,))
    early = smooth_rows(False, sides, cube, noise_weight, near_halo, high, low)
    early = lax.all_to_all(early, "chan", split_axis=0, concat_axis=0, tiled=True)
    late = smooth_rows(True, sides, cube, noise_weight, far_halo, high, low)
    late = lax.all_to_all(late, "chan", split_axis=0, concat_axis=0, tiled=True)
    rest = (spectral_halo, source_mask, tile_flags, halo_width)
    result = normalize(1 - sides, early, *rest)
    return normalize(2 * sides, late, *rest, before=result)


def solution(mesh):
    placed = (
        P("chan", "sky", None),
        P("chan", "sky", None),
        P(None, "sky", "chan"),
        P("sky", "chan"),
        P("sky", "chan"),
        P(None, "chan"),
    )
    return jax.shard_map(
        local, mesh=mesh, in_specs=placed, out_specs=P(None, None, "sky", "chan"), check_vma=False
    )
```

time: 207 us -> 69.6 us (0.34)
  the two profiles are of different devices: /device:TPU:48 before, /device:TPU:40 now
where the time goes in v1:
time: 69.6 us; the launch traced here: 69.3 us
  starting transfers between devices  26.9 us (39%)
  waiting for transfers between devices  25.9 us (37%)
  Pallas kernels  12.7 us (18%)
  local copies, waits for them, and re-layouts  2.43 us (3%)
  other arithmetic  1.15 us (2%)
    ppermute x1, waiting for transfers between devices, local(): far_halo = lax.ppermute(edge(side * last), 'sky', far)  18 us
    ppermute x1, starting transfers between devices, local(): far_halo = lax.ppermute(edge(side * last), 'sky', far)  12.4 us
    pallas_call x2, Pallas kernels, smooth_rows(): pl.pallas_call(functools.partial(smooth_kernel, late), out_shape=jax.Shap...  8.86 us
    all_to_all x1, starting transfers between devices, local(): late = lax.all_to_all(late, 'chan', split_axis=0, concat_axis=0, tiled=True)  6.65 us
    all_to_all x1, starting transfers between devices, local(): lax.all_to_all(early, 'chan', split_axis=0, concat_axis=0, tiled=True)  6.01 us
    all_to_all x1, waiting for transfers between devices, local(): late = lax.all_to_all(late, 'chan', split_axis=0, concat_axis=0, tiled=True)  5.99 us
    pallas_call x2, Pallas kernels, normalize(): pl.pallas_call(functools.partial(norm_kernel, None), out_shape=out, grid_...  3.88 us
    dynamic_slice x1, local copies, waits for them, and re-layouts, edge(): lax.dynamic_slice_in_dim(part, start, TILE_R, axis=1)  2.2 us
  transfers between devices with their start and end apart: 4, of which 3 were waited for; matrix products, arithmetic and copies ran while one was open for 2% of the time, Pallas kernels for 8%

profile of v1, /device:TPU:40, one launch (start us, length us, event | category | flops | bytes accessed | tf_op | source)
XLA Modules:
  0.0 69.3 jit_solution(6382470085528688093)
XLA Ops:
  0.0 0.0 copy-start.4
  0.0 0.0 copy-start.2
  0.0 0.0 copy-start.1
  0.0 0.0 copy-start
  0.0 2.2 %constant_dynamic-slice_fusion = (f32[1,8,8192]{2,1,0:T(8,128)S(1)}, f32[1,8,8192]{2,1,0:T(8,128)}, f32[1,8,8192]{2,1,0:T(8,128)}, f32[1,8,8192]{2,1,0:T(8,128)S(1)}) fusion(f32[1,24,8192]{2,1,0:T(8,128)} %weight_ref.3, s32[]{:T(128)S(6)} %select_n.17, s32[]{:T(128)S(6)} %select_n.16, f32[1,24,8192]{2,1,0:T(8,128)} %cube_ref.3), kind=kLoop, calls=%fused_computation.2 | loop fusion | bytes 2097160 | tf_op jit(solution)/shard_map/dynamic_slice | solution.py:212
  2.3 1.9 %collective-permute-start.1 = (f32[2,8,8192]{2,1,0:T(8,128)S(1)}, f32[2,8,8192]{2,1,0:T(8,128)S(1)}, u32[]{:S(2)}, u32[]{:S(2)}) collective-permute-start(f32[2,8,8192]{2,1,0:T(8,128)S(1)} %pad_maximum_fusion.1), channel_id=1, source_target_pairs={{0,16},{16,0},{32,48},{48,32},{64,80},{80,64},{96,112},{112,96},{1... | collective-permute-start | bytes 1572872 | tf_op jit(solution)/shard_map/ppermute | solution.py:216
  4.2 1.9 %collective-permute-done.1.halo_ref = f32[2,8,8192]{2,1,0:T(8,128)S(1)} collective-permute-done((f32[2,8,8192]{2,1,0:T(8,128)S(1)}, f32[2,8,8192]{2,1,0:T(8,128)S(1)}, u32[]{:S(2)}, u32[]{:S(2)}) %collective-permute-start.1) | collective-permute-done | bytes 524320 | tf_op jit(solution)/shard_map/ppermute | solution.py:216
  6.1 0.0 copy-done.4
  6.1 0.0 copy-done.2
  6.1 0.0 copy-done.1
  6.1 0.0 copy-done
  6.1 5.4 %shard_map.83 = f32[16,16,512]{2,1,0:T(8,128)} custom-call(s32[1]{0:T(128)} %bitcast.side_ref, f32[1,24,8192]{2,1,0:T(8,128)S(1)} %copy-done, f32[1,24,8192]{2,1,0:T(8,128)S(1)} %copy-done.1, f32[2,8,8192]{2,1,0:T(8,128)S(1)} %collective-permute-done.1.halo_ref, bf16[1024,256]{1,0:T(8,128)(2,1)S(1)} %copy-done.2, bf16[512,256]{1,0:T(8,128)(2,1)S(1)} %copy-done.4), custom_call_target="tpu_custom_call" | custom-call | flops 268435456 | bytes 2097152 | tf_op jit(solution)/shard_map/pallas_call | solution.py:113
  11.5 6.0 %all-to-all-start.1 = ((f32[16,16,512]{2,1,0:T(8,128)}), f32[16,16,512]{2,1,0:T(8,128)S(1)}, u32[]{:S(2)}, u32[]{:S(2)}) async-start(f32[16,16,512]{2,1,0:T(8,128)} %shard_map.83), calls=%async_computation.1 | async-start | bytes 1048576 | tf_op jit(solution)/shard_map/all_to_all | solution.py:219
  17.5 0.0 copy-start.7
  17.6 0.0 copy-start.6
  17.6 0.0 copy-start.3
  17.6 0.0 copy-start.5
  17.6 1.1 %pad_maximum_fusion = f32[2,8,8192]{2,1,0:T(8,128)S(1)} fusion(f32[1,8,8192]{2,1,0:T(8,128)} %get-tuple-element.8, f32[1,8,8192]{2,1,0:T(8,128)} %get-tuple-element.9), kind=kLoop, calls=%fused_computation | loop fusion | flops 131072 | bytes 1048576 | tf_op jit(solution)/shard_map/concatenate | solution.py:211
  18.7 12.4 %collective-permute-start = (f32[2,8,8192]{2,1,0:T(8,128)S(1)}, f32[2,8,8192]{2,1,0:T(8,128)S(1)}, u32[]{:S(2)}, u32[]{:S(2)}) collective-permute-start(f32[2,8,8192]{2,1,0:T(8,128)S(1)} %pad_maximum_fusion), channel_id=1, source_target_pairs={{16,32},{48,64},{80,96},{112,128},{144,160},{176,192},{208,224},{2... | collective-permute-start | bytes 1572872 | tf_op jit(solution)/shard_map/ppermute | solution.py:215
  31.1 18.0 %collective-permute-done.halo_ref = f32[2,8,8192]{2,1,0:T(8,128)S(1)} collective-permute-done((f32[2,8,8192]{2,1,0:T(8,128)S(1)}, f32[2,8,8192]{2,1,0:T(8,128)S(1)}, u32[]{:S(2)}, u32[]{:S(2)}) %collective-permute-start) | collective-permute-done | bytes 524320 | tf_op jit(solution)/shard_map/ppermute | solution.py:215
  49.1 3.4 %shard_map.82 = f32[16,8,512]{2,1,0:T(8,128)} custom-call(s32[1]{0:T(128)} %bitcast.side_ref, f32[1,24,8192]{2,1,0:T(8,128)S(1)} %copy-done, f32[1,24,8192]{2,1,0:T(8,128)S(1)} %copy-done.1, f32[2,8,8192]{2,1,0:T(8,128)S(1)} %collective-permute-done.halo_ref, bf16[1024,256]{1,0:T(8,128)(2,1)S(1)} %copy-done.2, bf16[512,256]{1,0:T(8,128)(2,1)S(1)} %copy-done.4), custom_call_target="tpu_custom_call" | custom-call | flops 134217728 | bytes 1048576 | tf_op jit(solution)/shard_map/pallas_call | solution.py:113
  52.5 0.0 all-to-all-done.1.smooth_ref
  52.5 6.7 %all-to-all-start = ((f32[16,8,512]{2,1,0:T(8,128)}), f32[16,8,512]{2,1,0:T(8,128)S(1)}, u32[]{:S(2)}, u32[]{:S(2)}) async-start(f32[16,8,512]{2,1,0:T(8,128)} %shard_map.82), calls=%async_computation | async-start | bytes 524288 | tf_op jit(solution)/shard_map/all_to_all | solution.py:221
  59.2 0.0 copy-done.7
  59.2 0.1 copy.13.width_ref
  59.3 0.0 copy-done.6
  59.3 0.1 copy.12.flags_ref
  59.4 0.0 copy-done.3
  59.4 0.0 copy-done.5
  59.4 2.1 %shard_map.84.rest_0_ = f32[3,16,24,512]{3,2,1,0:T(8,128)} custom-call(s32[1]{0:T(128)S(6)} %sub.6.tiles_ref, f32[16,16,512]{2,1,0:T(8,128)S(1)} %all-to-all-done.1.smooth_ref, f32[8,24,512]{2,1,0:T(8,128)S(1)} %copy-done.3, s32[24,512]{1,0:T(8,128)S(1)} %copy-done.5, s32[3,1]{1,0:T(4,128)S(1)} %copy.12.flags_ref, s32[2,1]{1,0:T(2,128)S(1)} %copy.13.width_ref), custom_call_target="tpu_custom_call" | custom-call | flops 3932160 | bytes 2621440 | tf_op jit(solution)/shard_map/pallas_call | solution.py:182
  61.5 6.0 %all-to-all-done.smooth_ref = f32[16,8,512]{2,1,0:T(8,128)S(1)} async-done(((f32[16,8,512]{2,1,0:T(8,128)}), f32[16,8,512]{2,1,0:T(8,128)S(1)}, u32[]{:S(2)}, u32[]{:S(2)}) %all-to-all-start) | async-done | bytes 262176 | tf_op jit(solution)/shard_map/all_to_all | solution.py:221
  67.5 1.7 %shard_map.85 = f32[3,16,24,512]{3,2,1,0:T(8,128)} custom-call(s32[1]{0:T(128)S(6)} %mul.9.tiles_ref, f32[16,8,512]{2,1,0:T(8,128)S(1)} %all-to-all-done.smooth_ref, f32[8,24,512]{2,1,0:T(8,128)S(1)} %copy-done.3, s32[24,512]{1,0:T(8,128)S(1)} %copy-done.5, s32[3,1]{1,0:T(4,128)S(1)} %copy.12.flags_ref, ...), custom_call_target="tpu_custom_call", output_to_operand_aliasing={{}: (6, {})} | custom-call | flops 1966080 | bytes 1310720 | tf_op jit(solution)/shard_map/pallas_call | solution.py:182
  (1 shorter events, 0.0 us)
Async XLA Ops:
  0.0 6.1 %copy-start.4 = (bf16[512,256]{1,0:T(8,128)(2,1)S(1)}, bf16[512,256]{1,0:T(8,128)(2,1)}, u32[]{:S(2)}) copy-start(bf16[512,256]{1,0:T(8,128)(2,1)} %constant.34.clone.low_ref) | copy-start | bytes 786436
  0.0 6.1 %copy-start.2 = (bf16[1024,256]{1,0:T(8,128)(2,1)S(1)}, bf16[1024,256]{1,0:T(8,128)(2,1)}, u32[]{:S(2)}) copy-start(bf16[1024,256]{1,0:T(8,128)(2,1)} %constant.33.clone.high_ref) | copy-start | bytes 1572868
  0.0 6.1 %copy-start.1 = (f32[1,24,8192]{2,1,0:T(8,128)S(1)}, f32[1,24,8192]{2,1,0:T(8,128)}, u32[]{:S(2)}) copy-start(f32[1,24,8192]{2,1,0:T(8,128)} %weight_ref.3) | copy-start | bytes 2359300
  0.0 6.1 %copy-start = (f32[1,24,8192]{2,1,0:T(8,128)S(1)}, f32[1,24,8192]{2,1,0:T(8,128)}, u32[]{:S(2)}) copy-start(f32[1,24,8192]{2,1,0:T(8,128)} %cube_ref.3) | copy-start | bytes 2359300
  2.3 3.8 %collective-permute-start.1 = (f32[2,8,8192]{2,1,0:T(8,128)S(1)}, f32[2,8,8192]{2,1,0:T(8,128)S(1)}, u32[]{:S(2)}, u32[]{:S(2)}) collective-permute-start(f32[2,8,8192]{2,1,0:T(8,128)S(1)} %pad_maximum_fusion.1), channel_id=1, source_target_pairs={{0,16},{16,0},{32,48},{48,32},{64,80},{80,64},{96,112},{112,96},{1... | collective-permute-start | bytes 1572872 | tf_op jit(solution)/shard_map/ppermute | solution.py:216
  11.5 41.0 %all-to-all-start.1 = ((f32[16,16,512]{2,1,0:T(8,128)}), f32[16,16,512]{2,1,0:T(8,128)S(1)}, u32[]{:S(2)}, u32[]{:S(2)}) async-start(f32[16,16,512]{2,1,0:T(8,128)} %shard_map.83), calls=%async_computation.1 | async-start | bytes 1048576 | tf_op jit(solution)/shard_map/all_to_all | solution.py:219
  17.5 41.7 %copy-start.7 = (s32[2,1]{0,1:T(1,128)S(1)}, s32[2,1]{0,1:T(1,128)}, u32[]{:S(2)}) copy-start(s32[2,1]{0,1:T(1,128)} %param.13) | copy-start | bytes 28
  17.6 41.7 %copy-start.6 = (s32[3,1]{0,1:T(1,128)S(1)}, s32[3,1]{0,1:T(1,128)}, u32[]{:S(2)}) copy-start(s32[3,1]{0,1:T(1,128)} %param.12) | copy-start | bytes 40
  17.6 41.8 %copy-start.3 = (f32[8,24,512]{2,1,0:T(8,128)S(1)}, f32[8,24,512]{2,1,0:T(8,128)}, u32[]{:S(2)}) copy-start(f32[8,24,512]{2,1,0:T(8,128)} %halo_ref.3) | copy-start | bytes 1179652
  17.6 41.8 %copy-start.5 = (s32[24,512]{1,0:T(8,128)S(1)}, s32[24,512]{1,0:T(8,128)}, u32[]{:S(2)}) copy-start(s32[24,512]{1,0:T(8,128)} %mask_ref.3) | copy-start | bytes 147460
  18.7 30.4 %collective-permute-start = (f32[2,8,8192]{2,1,0:T(8,128)S(1)}, f32[2,8,8192]{2,1,0:T(8,128)S(1)}, u32[]{:S(2)}, u32[]{:S(2)}) collective-permute-start(f32[2,8,8192]{2,1,0:T(8,128)S(1)} %pad_maximum_fusion), channel_id=1, source_target_pairs={{16,32},{48,64},{80,96},{112,128},{144,160},{176,192},{208,224},{2... | collective-permute-start | bytes 1572872 | tf_op jit(solution)/shard_map/ppermute | solution.py:215
  52.5 15.0 %all-to-all-start = ((f32[16,8,512]{2,1,0:T(8,128)}), f32[16,8,512]{2,1,0:T(8,128)S(1)}, u32[]{:S(2)}, u32[]{:S(2)}) async-start(f32[16,8,512]{2,1,0:T(8,128)} %shard_map.82), calls=%async_computation | async-start | bytes 524288 | tf_op jit(solution)/shard_map/all_to_all | solution.py:221

commit v2 on v1

--- a/solution.py
+++ b/solution.py
@@ -3,8 +3,6 @@
 
 import jax
 import jax.numpy as jnp
-import ml_dtypes
-import numpy as np
 from jax import lax
 from jax.experimental import pallas as pl
 from jax.experimental.pallas import tpu as pltpu
@@ -16,6 +14,7 @@
 TILE_C = 512
 BLK = 256
 LANES = 128
+CHUNKS = 4
 
 
 def tap_list():
@@ -26,13 +25,18 @@
 TAPS = tap_list()[RAD:]
 
 
-def band_matrices():
-    source = np.concatenate([np.arange(BLK), np.arange(-LANES, 0), np.arange(BLK, BLK + LANES)])
-    reach = np.abs(source[:, None] - np.arange(BLK)[None, :])
-    band = np.where(reach <= RAD, np.asarray(TAPS + [0.0])[np.minimum(reach, RAD + 1)], 0.0)
-    high = band.astype(np.float32).astype(ml_dtypes.bfloat16)
-    low = (band - high.astype(np.float64)).astype(np.float32).astype(ml_dtypes.bfloat16)
-    return np.concatenate([high, high], axis=0), low
+def band_matrices(high_ref, low_ref):
+    shape = (LANES, BLK)
+    target = lax.broadcasted_iota(jnp.int32, shape, 1)
+    for part, first in enumerate((0, LANES, -LANES, BLK)):
+        reach = jnp.abs(lax.broadcasted_iota(jnp.int32, shape, 0) + first - target)
+        band = jnp.zeros(shape, jnp.float32)
+        for shift in range(RAD + 1):
+            band = jnp.where(reach == shift, TAPS[shift], band)
+        high = band.astype(jnp.bfloat16)
+        rows = slice(part * LANES, (part + 1) * LANES)
+        high_ref[rows] = high
+        low_ref[rows] = (band - high.astype(jnp.float32)).astype(jnp.bfloat16)
 
 
 def column_taps(tiles):
@@ -51,12 +55,15 @@
     return totals
 
 
-def smooth_kernel(late, side_ref, cube_ref, weight_ref, halo_ref, high_ref, low_ref, out_ref, split):
+def smooth_kernel(
+    late, side_ref, cube_ref, weight_ref, halo_ref, out_hbm, split, lines, high_ref, low_ref, out_ref, sent
+):
     side = side_ref[0]
     even = side == 0
     tiles_out = 1 if late else 2
     rows = tiles_out * TILE_R
     blocks = cube_ref.shape[2] // BLK
+    band_matrices(high_ref, low_ref)
     split[1, :, BLK : BLK + LANES] = jnp.zeros((2 * rows, LANES), jnp.bfloat16)
     split[1, :, 3 * BLK : 3 * BLK + LANES] = jnp.zeros((2 * rows, LANES), jnp.bfloat16)
     split[blocks, :, BLK + LANES : 2 * BLK] = jnp.zeros((2 * rows, LANES), jnp.bfloat16)
@@ -79,7 +86,23 @@
         weights = window(weight_ref, halo_ref[1, :, cols], cols)
         values = window(cube_ref, halo_ref[0, :, cols], cols)
         values = [value * weight for value, weight in zip(values, weights)]
-        both = jnp.concatenate(column_taps(values) + column_taps(weights), axis=0)
+        sides = []
+        for slot, half in enumerate((0, LANES)):
+            for kind, tiles in enumerate((values, weights)):
+                at = 2 * slot + kind
+                for i, tile in enumerate(tiles):
+                    lines[at, TILE_R * i : TILE_R * (i + 1)] = tile[:, half : half + LANES]
+        for slot in range(2):
+            made = []
+            for kind in range(2):
+                at = 2 * slot + kind
+                line = lambda start: lines[at, start : start + rows]
+                total = TAPS[0] * line(RAD)
+                for shift in range(1, RAD + 1):
+                    total = total + TAPS[shift] * (line(RAD - shift) + line(RAD + shift))
+                made.append(total)
+            sides.append(jnp.concatenate(made, axis=0))
+        both = jnp.concatenate(sides, axis=1)
         high = both.astype(jnp.bfloat16)
         low = (both - high.astype(jnp.float32)).astype(jnp.bfloat16)
         for part, base in ((high, 0), (low, 2 * BLK)):
@@ -88,42 +111,82 @@
             split[block, :, base + BLK + LANES : base + 2 * BLK] = part[:, :LANES]
         return carry
 
-    lax.fori_loop(0, blocks, rows_step, 0)
-
-    group = 8 if late else 4
-
-    def columns_step(step, carry):
-        part = split[pl.ds(step * group + 1, group)].reshape(group * 2 * rows, 4 * BLK)
-        both = jnp.dot(part, high_ref[...], preferred_element_type=jnp.float32)
+    lax.fori_loop(0, blocks, rows_step, 0, unroll=2)
+    group = blocks // CHUNKS
+    parts = []
+    for step in range(CHUNKS):
+        part = split[step * group + 1 : (step + 1) * group + 1].reshape(group * 2 * rows, 4 * BLK)
+        both = jnp.dot(part[:, : 2 * BLK], high_ref[...], preferred_element_type=jnp.float32)
+        both += jnp.dot(part[:, 2 * BLK :], high_ref[...], preferred_element_type=jnp.float32)
         both += jnp.dot(part[:, : 2 * BLK], low_ref[...], preferred_element_type=jnp.float32)
         both = both.reshape(group, 2 * rows, BLK)
         ratio = both[:, :rows] / both[:, rows:]
+        first = step * (group // 2)
         for i in range(group):
-            out_ref[step * (group // 2) + i // 2, :, (i % 2) * BLK : (i % 2 + 1) * BLK] = ratio[i]
-        return carry
-
-    lax.fori_loop(0, blocks // group, columns_step, 0)
-
-
-def smooth_rows(late, side, cube, weight, halo, high, low):
+            out_ref[first + i // 2, :, (i % 2) * BLK : (i % 2 + 1) * BLK] = ratio[i]
+        piece = pl.ds(first, group // 2)
+        parts.append(pltpu.make_async_copy(out_ref.at[piece], out_hbm.at[piece], sent.at[step]))
+        parts[-1].start()
+    for copy in parts:
+        copy.wait()
+
+
+def edge_kernel(side_ref, cube_ref, weight_ref, far_ref, near_ref, done):
+    side = side_ref[0]
+    last = cube_ref.shape[1] - TILE_R
+    copies = []
+    for k, (out_ref, start) in enumerate(((far_ref, side * last), (near_ref, (1 - side) * last))):
+        rows = pl.ds(pl.multiple_of(start, TILE_R), TILE_R)
+        for j, ref in enumerate((cube_ref, weight_ref)):
+            copies.append(
+                pltpu.make_async_copy(ref.at[0, rows], out_ref.at[j], done.at[2 * k + j])
+            )
+    for copy in copies:
+        copy.start()
+    for copy in copies:
+        copy.wait()
+
+
+def edge_rows(side, cube, weight):
+    edge = pltpu.VMEM((2, TILE_R, cube.shape[2]), cube.dtype)
+    whole = pl.BlockSpec(memory_space=pltpu.VMEM)
+    return pl.pallas_call(
+        edge_kernel,
+        out_shape=[edge, edge],
+        in_specs=[pl.BlockSpec(memory_space=pltpu.SMEM)] + [pl.BlockSpec(memory_space=pl.ANY)] * 2,
+        out_specs=[whole, whole],
+        scratch_shapes=[pltpu.SemaphoreType.DMA((4,))],
+        compiler_params=pltpu.CompilerParams(vmem_limit_bytes=8 * 1024 * 1024),
+        cost_estimate=pl.CostEstimate(
+            flops=10**11, bytes_accessed=64 * TILE_R * cube.shape[2], transcendentals=0
+        ),
+    )(side, cube, weight)
+
+
+def smooth_rows(late, side, cube, weight, halo):
     rows = TILE_R if late else 2 * TILE_R
     columns = cube.shape[2]
     blocks = columns // BLK
     whole = pl.BlockSpec(memory_space=pltpu.VMEM)
     return pl.pallas_call(
         functools.partial(smooth_kernel, late),
-        out_shape=jax.ShapeDtypeStruct((columns // TILE_C, rows, TILE_C), jnp.float32),
-        in_specs=[pl.BlockSpec(memory_space=pltpu.SMEM)] + [whole] * 5,
-        out_specs=whole,
-        scratch_shapes=[pltpu.VMEM((blocks + 2, 2 * rows, 4 * BLK), jnp.bfloat16)],
+        out_shape=pltpu.HBM((columns // TILE_C, rows, TILE_C), jnp.float32),
+        in_specs=[pl.BlockSpec(memory_space=pltpu.SMEM)] + [whole] * 3,
+        out_specs=pl.BlockSpec(memory_space=pl.ANY),
+        scratch_shapes=[pltpu.VMEM((blocks + 2, 2 * rows, 4 * BLK), jnp.bfloat16), pltpu.VMEM((4, rows + 2 * TILE_R, LANES), jnp.float32),
+            pltpu.VMEM((2 * BLK, BLK), jnp.bfloat16),
+            pltpu.VMEM((2 * BLK, BLK), jnp.bfloat16),
+            pltpu.VMEM((columns // TILE_C, rows, TILE_C), jnp.float32),
+            pltpu.SemaphoreType.DMA((CHUNKS,)),
+        ],
         compiler_params=pltpu.CompilerParams(vmem_limit_bytes=24 * 1024 * 1024),
         cost_estimate=pl.CostEstimate(
-            flops=4 * rows * columns * 2 * BLK, bytes_accessed=16 * rows * columns, transcendentals=0
-        ),
-    )(side, cube, weight, halo, high, low)
-
-
-def norm_kernel(base, tiles_ref, smooth_ref, halo_ref, mask_ref, flags_ref, width_ref, *rest):
+            flops=10**11, bytes_accessed=16 * rows * columns, transcendentals=0
+        ),
+    )(side, cube, weight, halo)
+
+
+def norm_kernel(tiles_ref, smooth_ref, halo_ref, mask_ref, flags_ref, width_ref, *rest):
     out_ref = rest[-1]
     channels = smooth_ref.shape[0]
     tile = tiles_ref[0] + pl.program_id(0)
@@ -180,7 +243,7 @@
         operands.append(before)
         aliases = {6: 0}
     return pl.pallas_call(
-        functools.partial(norm_kernel, None),
+        norm_kernel,
         out_shape=out,
         grid_spec=pltpu.PrefetchScalarGridSpec(
             num_scalar_prefetch=1,
@@ -199,25 +262,21 @@
 
 
 def local(cube, noise_weight, spectral_halo, source_mask, tile_flags, halo_width):
-    high, low = (jnp.asarray(part) for part in band_matrices())
     sky = lax.axis_size("sky")
-    side = lax.axis_index("sky") % 2
-    last = cube.shape[1] - TILE_R
+    side = lax.axis_index("sky") & 1
     near = [(i, i ^ 1) for i in range(sky)]
     far = [(i, i + 1) for i in range(1, sky - 1, 2)]
     far = far + [(target, source) for source, target in far]
 
-    def edge(start):
-        return jnp.concatenate(
-            [lax.dynamic_slice_in_dim(part, start, TILE_R, axis=1) for part in (cube, noise_weight)], axis=0
-        )
-
-    far_halo = lax.ppermute(edge(side * last), "sky", far)
-    near_halo = lax.ppermute(edge((1 - side) * last), "sky", near)
     sides = jnp.reshape(side, (1,))
-    early = smooth_rows(False, sides, cube, noise_weight, near_halo, high, low)
+    stay = [pltpu.with_memory_space_constraint(part, pltpu.HBM) for part in (cube, noise_weight)]
+    far_edge, near_edge = edge_rows(sides, *stay)
+    far_halo = lax.ppermute(far_edge, "sky", far)
+    near_halo = lax.ppermute(near_edge, "sky", near)
+    early = smooth_rows(False, sides, cube, noise_weight, near_halo)
     early = lax.all_to_all(early, "chan", split_axis=0, concat_axis=0, tiled=True)
-    late = smooth_rows(True, sides, cube, noise_weight, far_halo, high, low)
+    far_halo = pltpu.with_memory_space_constraint(far_halo, pltpu.VMEM)
+    late = smooth_rows(True, sides, cube, noise_weight, far_halo)
     late = lax.all_to_all(late, "chan", split_axis=0, concat_axis=0, tiled=True)
     rest = (spectral_halo, source_mask, tile_flags, halo_width)
     result = normalize(1 - sides, early, *rest)

time: 69.6 us -> 56.2 us (0.81)
  the two profiles are of different devices: /device:TPU:40 before, /device:TPU:1 now
where the time goes in v2:
time: 56.2 us; the launch traced here: 55.8 us
  waiting for transfers between devices  25.5 us (45%)
  starting transfers between devices  18 us (32%)
  Pallas kernels  12 us (21%)
    all_to_all x1, waiting for transfers between devices, local(): lax.all_to_all(early, 'chan', split_axis=0, concat_axis=0, tiled=True)  16.6 us
    ppermute x1, starting transfers between devices, local(): near_halo = lax.ppermute(near_edge, 'sky', near)  8.79 us
    all_to_all x1, waiting for transfers between devices, local(): late = lax.all_to_all(late, 'chan', split_axis=0, concat_axis=0, tiled=True)  7.51 us
    pallas_call x2, Pallas kernels, smooth_rows(): pl.pallas_call(functools.partial(smooth_kernel, late), out_shape=pltpu.HB...  6.74 us
    pallas_call x2, Pallas kernels, normalize(): pl.pallas_call(norm_kernel, out_shape=out, grid_spec=pltpu.PrefetchScalar...  3.88 us
    all_to_all x1, starting transfers between devices, local(): lax.all_to_all(early, 'chan', split_axis=0, concat_axis=0, tiled=True)  3.78 us
    all_to_all x1, starting transfers between devices, local(): late = lax.all_to_all(late, 'chan', split_axis=0, concat_axis=0, tiled=True)  3.53 us
    ppermute x1, starting transfers between devices, local(): far_halo = lax.ppermute(far_edge, 'sky', far)  1.92 us
  transfers between devices with their start and end apart: 4, of which 3 were waited for; matrix products, arithmetic and copies ran while one was open for 0% of the time, Pallas kernels for 16%

profile of v2, /device:TPU:1, one launch (start us, length us, event | category | flops | bytes accessed | tf_op | source)
XLA Modules:
  0.0 55.8 jit_solution(13063879271652491571)
XLA Ops:
  0.0 0.0 copy-start.2
  0.0 0.0 copy-start.3
  0.0 1.3 %shard_map.64 = (f32[2,8,8192]{2,1,0:T(8,128)S(1)}, f32[2,8,8192]{2,1,0:T(8,128)S(1)}) custom-call(s32[1]{0:T(128)} %bitcast.side_ref, f32[1,24,8192]{2,1,0:T(8,128)} %cube_ref.5, f32[1,24,8192]{2,1,0:T(8,128)} %weight_ref.5), custom_call_target="tpu_custom_call" | custom-call | flops 99999997952 | bytes 4194304 | tf_op jit(solution)/shard_map/pallas_call | solution.py:153
  1.4 8.8 %collective-permute-start.1 = (f32[2,8,8192]{2,1,0:T(8,128)S(1)}, f32[2,8,8192]{2,1,0:T(8,128)S(1)}, u32[]{:S(2)}, u32[]{:S(2)}) collective-permute-start(f32[2,8,8192]{2,1,0:T(8,128)S(1)} %get-tuple-element.8), channel_id=1, source_target_pairs={{0,16},{16,0},{32,48},{48,32},{64,80},{80,64},{96,112},{112,96},{1... | collective-permute-start | bytes 1572872 | tf_op jit(solution)/shard_map/ppermute | solution.py:275
  10.1 1.9 %collective-permute-start = (f32[2,8,8192]{2,1,0:T(8,128)S(1)}, f32[2,8,8192]{2,1,0:T(8,128)}, u32[]{:S(2)}, u32[]{:S(2)}) collective-permute-start(f32[2,8,8192]{2,1,0:T(8,128)S(1)} %get-tuple-element.7), channel_id=1, source_target_pairs={{16,32},{48,64},{80,96},{112,128},{144,160},{176,192},{208,224},{2... | collective-permute-start | bytes 1572872 | tf_op jit(solution)/shard_map/ppermute | solution.py:274
  12.1 0.0 collective-permute-done.1.halo_ref
  12.1 0.0 copy-done.2
  12.1 0.0 copy-done.3
  12.1 3.4 %shard_map.66 = f32[16,16,512]{2,1,0:T(8,128)} custom-call(s32[1]{0:T(128)} %bitcast.side_ref, f32[1,24,8192]{2,1,0:T(8,128)S(1)} %copy-done.2, f32[1,24,8192]{2,1,0:T(8,128)S(1)} %copy-done.3, f32[2,8,8192]{2,1,0:T(8,128)S(1)} %collective-permute-done.1.halo_ref), custom_call_target="tpu_custom_call" | custom-call | flops 99999997952 | bytes 2097152 | tf_op jit(solution)/shard_map/pallas_call | solution.py:171
  15.5 3.8 %all-to-all-start.1 = ((f32[16,16,512]{2,1,0:T(8,128)}), f32[16,16,512]{2,1,0:T(8,128)S(1)}, u32[]{:S(2)}, u32[]{:S(2)}) async-start(f32[16,16,512]{2,1,0:T(8,128)} %shard_map.66), calls=%async_computation.1 | async-start | bytes 1048576 | tf_op jit(solution)/shard_map/all_to_all | solution.py:277
  19.3 0.0 copy-start.5
  19.3 0.0 copy-start.4
  19.3 0.0 copy-start
  19.3 0.0 copy-start.1
  19.3 1.4 %collective-permute-done.halo_ref = f32[2,8,8192]{2,1,0:T(8,128)} collective-permute-done((f32[2,8,8192]{2,1,0:T(8,128)S(1)}, f32[2,8,8192]{2,1,0:T(8,128)}, u32[]{:S(2)}, u32[]{:S(2)}) %collective-permute-start) | collective-permute-done | bytes 524320 | tf_op jit(solution)/shard_map/ppermute | solution.py:274
  20.8 3.4 %shard_map.65 = f32[16,8,512]{2,1,0:T(8,128)} custom-call(s32[1]{0:T(128)} %bitcast.side_ref, f32[1,24,8192]{2,1,0:T(8,128)S(1)} %copy-done.2, f32[1,24,8192]{2,1,0:T(8,128)S(1)} %copy-done.3, f32[2,8,8192]{2,1,0:T(8,128)} %collective-permute-done.halo_ref), custom_call_target="tpu_custom_call" | custom-call | flops 99999997952 | bytes 1048576 | tf_op jit(solution)/shard_map/pallas_call | solution.py:171
  24.1 16.6 %all-to-all-done.1.smooth_ref = f32[16,16,512]{2,1,0:T(8,128)S(1)} async-done(((f32[16,16,512]{2,1,0:T(8,128)}), f32[16,16,512]{2,1,0:T(8,128)S(1)}, u32[]{:S(2)}, u32[]{:S(2)}) %all-to-all-start.1) | async-done | bytes 524320 | tf_op jit(solution)/shard_map/all_to_all | solution.py:277
  40.7 3.5 %all-to-all-start = ((f32[16,8,512]{2,1,0:T(8,128)}), f32[16,8,512]{2,1,0:T(8,128)S(1)}, u32[]{:S(2)}, u32[]{:S(2)}) async-start(f32[16,8,512]{2,1,0:T(8,128)} %shard_map.65), calls=%async_computation | async-start | bytes 524288 | tf_op jit(solution)/shard_map/all_to_all | solution.py:280
  44.2 0.0 copy-done.5
  44.2 0.1 copy.11.width_ref
  44.3 0.0 copy-done.4
  44.3 0.1 copy.10.flags_ref
  44.4 0.0 copy-done
  44.4 0.0 copy-done.1
  44.4 2.1 %shard_map.67.rest_0_ = f32[3,16,24,512]{3,2,1,0:T(8,128)} custom-call(s32[1]{0:T(128)S(6)} %sub.3.tiles_ref, f32[16,16,512]{2,1,0:T(8,128)S(1)} %all-to-all-done.1.smooth_ref, f32[8,24,512]{2,1,0:T(8,128)S(1)} %copy-done, s32[24,512]{1,0:T(8,128)S(1)} %copy-done.1, s32[3,1]{1,0:T(4,128)S(1)} %copy.10.flags_ref, s32[2,1]{1,0:T(2,128)S(1)} %copy.11.width_ref), custom_call_target="tpu_custom_call" | custom-call | flops 3932160 | bytes 2621440 | tf_op jit(solution)/shard_map/pallas_call | solution.py:245
  46.6 7.5 %all-to-all-done.smooth_ref = f32[16,8,512]{2,1,0:T(8,128)S(1)} async-done(((f32[16,8,512]{2,1,0:T(8,128)}), f32[16,8,512]{2,1,0:T(8,128)S(1)}, u32[]{:S(2)}, u32[]{:S(2)}) %all-to-all-start) | async-done | bytes 262176 | tf_op jit(solution)/shard_map/all_to_all | solution.py:280
  54.1 1.7 %shard_map.68 = f32[3,16,24,512]{3,2,1,0:T(8,128)} custom-call(s32[1]{0:T(128)S(6)} %mul.3.tiles_ref, f32[16,8,512]{2,1,0:T(8,128)S(1)} %all-to-all-done.smooth_ref, f32[8,24,512]{2,1,0:T(8,128)S(1)} %copy-done, s32[24,512]{1,0:T(8,128)S(1)} %copy-done.1, s32[3,1]{1,0:T(4,128)S(1)} %copy.10.flags_ref, ...), custom_call_target="tpu_custom_call", output_to_operand_aliasing={{}: (6, {})} | custom-call | flops 1966080 | bytes 1310720 | tf_op jit(solution)/shard_map/pallas_call | solution.py:245
Async XLA Ops:
  0.0 12.1 %copy-start.2 = (f32[1,24,8192]{2,1,0:T(8,128)S(1)}, f32[1,24,8192]{2,1,0:T(8,128)}, u32[]{:S(2)}) copy-start(f32[1,24,8192]{2,1,0:T(8,128)} %cube_ref.5) | copy-start | bytes 2359300
  0.0 12.1 %copy-start.3 = (f32[1,24,8192]{2,1,0:T(8,128)S(1)}, f32[1,24,8192]{2,1,0:T(8,128)}, u32[]{:S(2)}) copy-start(f32[1,24,8192]{2,1,0:T(8,128)} %weight_ref.5) | copy-start | bytes 2359300
  1.4 10.7 %collective-permute-start.1 = (f32[2,8,8192]{2,1,0:T(8,128)S(1)}, f32[2,8,8192]{2,1,0:T(8,128)S(1)}, u32[]{:S(2)}, u32[]{:S(2)}) collective-permute-start(f32[2,8,8192]{2,1,0:T(8,128)S(1)} %get-tuple-element.8), channel_id=1, source_target_pairs={{0,16},{16,0},{32,48},{48,32},{64,80},{80,64},{96,112},{112,96},{1... | collective-permute-start | bytes 1572872 | tf_op jit(solution)/shard_map/ppermute | solution.py:275
  10.1 10.6 %collective-permute-start = (f32[2,8,8192]{2,1,0:T(8,128)S(1)}, f32[2,8,8192]{2,1,0:T(8,128)}, u32[]{:S(2)}, u32[]{:S(2)}) collective-permute-start(f32[2,8,8192]{2,1,0:T(8,128)S(1)} %get-tuple-element.7), channel_id=1, source_target_pairs={{16,32},{48,64},{80,96},{112,128},{144,160},{176,192},{208,224},{2... | collective-permute-start | bytes 1572872 | tf_op jit(solution)/shard_map/ppermute | solution.py:274
  15.5 25.2 %all-to-all-start.1 = ((f32[16,16,512]{2,1,0:T(8,128)}), f32[16,16,512]{2,1,0:T(8,128)S(1)}, u32[]{:S(2)}, u32[]{:S(2)}) async-start(f32[16,16,512]{2,1,0:T(8,128)} %shard_map.66), calls=%async_computation.1 | async-start | bytes 1048576 | tf_op jit(solution)/shard_map/all_to_all | solution.py:277
  19.3 25.0 %copy-start.5 = (s32[2,1]{0,1:T(1,128)S(1)}, s32[2,1]{0,1:T(1,128)}, u32[]{:S(2)}) copy-start(s32[2,1]{0,1:T(1,128)} %param.11) | copy-start | bytes 28
  19.3 25.1 %copy-start.4 = (s32[3,1]{0,1:T(1,128)S(1)}, s32[3,1]{0,1:T(1,128)}, u32[]{:S(2)}) copy-start(s32[3,1]{0,1:T(1,128)} %param.10) | copy-start | bytes 40
  19.3 25.1 %copy-start = (f32[8,24,512]{2,1,0:T(8,128)S(1)}, f32[8,24,512]{2,1,0:T(8,128)}, u32[]{:S(2)}) copy-start(f32[8,24,512]{2,1,0:T(8,128)} %halo_ref.3) | copy-start | bytes 1179652
  19.3 25.1 %copy-start.1 = (s32[24,512]{1,0:T(8,128)S(1)}, s32[24,512]{1,0:T(8,128)}, u32[]{:S(2)}) copy-start(s32[24,512]{1,0:T(8,128)} %mask_ref.3) | copy-start | bytes 147460
  40.7 13.4 %all-to-all-start = ((f32[16,8,512]{2,1,0:T(8,128)}), f32[16,8,512]{2,1,0:T(8,128)S(1)}, u32[]{:S(2)}, u32[]{:S(2)}) async-start(f32[16,8,512]{2,1,0:T(8,128)} %shard_map.65), calls=%async_computation | async-start | bytes 524288 | tf_op jit(solution)/shard_map/all_to_all | solution.py:280

commit v3 on v2

--- a/solution.py
+++ b/solution.py
@@ -15,6 +15,7 @@
 BLK = 256
 LANES = 128
 CHUNKS = 4
+WIDTHS = (3, 5, 9)
 
 
 def tap_list():
@@ -56,10 +57,13 @@
 
 
 def smooth_kernel(
-    late, side_ref, cube_ref, weight_ref, halo_ref, out_hbm, split, lines, high_ref, low_ref, out_ref, sent
+    late, side_ref, cube_ref, weight_ref, *rest
 ):
-    side = side_ref[0]
+    out_hbm, split, lines, high_ref, low_ref, out_ref, sent = rest[-7:]
+    halos = rest[:-8] if late else rest[:-7]
+    side = side_ref[0] & 1
     even = side == 0
+    border = side_ref[0] > 1
     tiles_out = 1 if late else 2
     rows = tiles_out * TILE_R
     blocks = cube_ref.shape[2] // BLK
@@ -83,8 +87,12 @@
 
     def rows_step(block, carry):
         cols = pl.ds(pl.multiple_of(block * BLK, BLK), BLK)
-        weights = window(weight_ref, halo_ref[1, :, cols], cols)
-        values = window(cube_ref, halo_ref[0, :, cols], cols)
+        cube_halo, weight_halo = halos[0][0, :, cols], halos[0][1, :, cols]
+        if not late:
+            cube_halo = jnp.where(border, cube_halo, halos[1][:, cols])
+            weight_halo = jnp.where(border, weight_halo, halos[2][:, cols])
+        weights = window(weight_ref, weight_halo, cols)
+        values = window(cube_ref, cube_halo, cols)
         values = [value * weight for value, weight in zip(values, weights)]
         sides = []
         for slot, half in enumerate((0, LANES)):
@@ -113,6 +121,7 @@
 
     lax.fori_loop(0, blocks, rows_step, 0, unroll=2)
     group = blocks // CHUNKS
+    top = pl.multiple_of((2 * side if late else 1 - side) * TILE_R, TILE_R)
     parts = []
     for step in range(CHUNKS):
         part = split[step * group + 1 : (step + 1) * group + 1].reshape(group * 2 * rows, 4 * BLK)
@@ -125,14 +134,15 @@
         for i in range(group):
             out_ref[first + i // 2, :, (i % 2) * BLK : (i % 2 + 1) * BLK] = ratio[i]
         piece = pl.ds(first, group // 2)
-        parts.append(pltpu.make_async_copy(out_ref.at[piece], out_hbm.at[piece], sent.at[step]))
+        place = out_hbm.at[piece, pl.ds(top, rows)]
+        parts.append(pltpu.make_async_copy(out_ref.at[piece], place, sent.at[step]))
         parts[-1].start()
     for copy in parts:
         copy.wait()
 
 
 def edge_kernel(side_ref, cube_ref, weight_ref, far_ref, near_ref, done):
-    side = side_ref[0]
+    side = side_ref[0] & 1
     last = cube_ref.shape[1] - TILE_R
     copies = []
     for k, (out_ref, start) in enumerate(((far_ref, side * last), (near_ref, (1 - side) * last))):
@@ -163,16 +173,18 @@
     )(side, cube, weight)
 
 
-def smooth_rows(late, side, cube, weight, halo):
+def smooth_rows(side, cube, weight, *halo, before=None):
+    late = before is not None
     rows = TILE_R if late else 2 * TILE_R
     columns = cube.shape[2]
     blocks = columns // BLK
     whole = pl.BlockSpec(memory_space=pltpu.VMEM)
     return pl.pallas_call(
         functools.partial(smooth_kernel, late),
-        out_shape=pltpu.HBM((columns // TILE_C, rows, TILE_C), jnp.float32),
-        in_specs=[pl.BlockSpec(memory_space=pltpu.SMEM)] + [whole] * 3,
+        out_shape=pltpu.HBM((columns // TILE_C, cube.shape[1], TILE_C), jnp.float32),
+        in_specs=[pl.BlockSpec(memory_space=pltpu.SMEM)] + [whole] * (2 + len(halo)) + [pl.BlockSpec(memory_space=pl.ANY)] * late,
         out_specs=pl.BlockSpec(memory_space=pl.ANY),
+        input_output_aliases={4: 0} if late else {},
         scratch_shapes=[pltpu.VMEM((blocks + 2, 2 * rows, 4 * BLK), jnp.bfloat16), pltpu.VMEM((4, rows + 2 * TILE_R, LANES), jnp.float32),
             pltpu.VMEM((2 * BLK, BLK), jnp.bfloat16),
             pltpu.VMEM((2 * BLK, BLK), jnp.bfloat16),
@@ -181,106 +193,99 @@
         ],
         compiler_params=pltpu.CompilerParams(vmem_limit_bytes=24 * 1024 * 1024),
         cost_estimate=pl.CostEstimate(
-            flops=10**11, bytes_accessed=16 * rows * columns, transcendentals=0
+            flops=4 * rows * columns * 2 * BLK, bytes_accessed=16 * rows * columns, transcendentals=0
         ),
-    )(side, cube, weight, halo)
-
-
-def norm_kernel(tiles_ref, smooth_ref, halo_ref, mask_ref, flags_ref, width_ref, *rest):
-    out_ref = rest[-1]
-    channels = smooth_ref.shape[0]
-    tile = tiles_ref[0] + pl.program_id(0)
+    )(side, cube, weight, *halo, *([before] if late else []))
+
+
+def norm_kernel(smooth_ref, halo_ref, mask_ref, flags_ref, width_ref, out_hbm, out_ref, sent):
+    channels, rows, columns = smooth_ref.shape
     keep_low = [(j >= HW - width_ref[0, 0]).astype(jnp.float32) for j in range(HW)]
     keep_high = [(j < width_ref[1, 0]).astype(jnp.float32) for j in range(HW)]
-    sums = [jnp.zeros((TILE_R, LANES), jnp.float32) for _ in range(3)]
-    kept = jnp.zeros((TILE_R, LANES), jnp.float32)
-    for strip in range(TILE_C // LANES):
-        cols = slice(strip * LANES, (strip + 1) * LANES)
-        keep = (mask_ref[:, cols] == 0).astype(jnp.float32)
-        kept = kept + keep
-        extended = [halo_ref[j, :, cols] * keep_low[j] for j in range(HW)]
-        extended += [smooth_ref[c, :, cols] for c in range(channels)]
-        extended += [halo_ref[HW + j, :, cols] * keep_high[j] for j in range(HW)]
-        squares = [jnp.zeros((TILE_R, LANES), jnp.float32) for _ in range(3)]
-        for c in range(channels):
-            at = c + HW
-            three = extended[at - 1] + extended[at] + extended[at + 1]
-            five = three + (extended[at - 2] + extended[at + 2])
-            nine = five + ((extended[at - 3] + extended[at + 3]) + (extended[at - 4] + extended[at + 4]))
-            for i, (total, width) in enumerate(((three, 3), (five, 5), (nine, 9))):
-                boxcar = total * (1.0 / width)
-                out_ref[i, c, :, cols] = boxcar
-                squares[i] = squares[i] + boxcar * boxcar
-        sums = [total + square * keep for total, square in zip(sums, squares)]
 
     def whole(x):
         return jnp.sum(jnp.sum(x, axis=1, keepdims=True), axis=0, keepdims=True)
 
-    count = jnp.maximum(whole(kept) * channels, 1.0)
-    flag = flags_ref[tile, 0].astype(jnp.float32)
-    for i in range(3):
-        factor = flag / jnp.sqrt(whole(sums[i]) / count + 1e-06)
-        factor = jnp.broadcast_to(factor, (TILE_R, TILE_C))
-        for c in range(channels):
-            out_ref[i, c] = out_ref[i, c] * factor
-
-
-def normalize(first, smoothed, halo, mask, flags, widths, before=None):
-    channels, rows, columns = smoothed.shape
-    steps = rows // TILE_R
-    out = jax.ShapeDtypeStruct((3, channels) + mask.shape, jnp.float32)
-    in_specs = [
-        pl.BlockSpec((channels, TILE_R, columns), lambda i, at: (0, i, 0)),
-        pl.BlockSpec((2 * HW, TILE_R, columns), lambda i, at: (0, at[0] + i, 0)),
-        pl.BlockSpec((TILE_R, columns), lambda i, at: (at[0] + i, 0)),
-        pl.BlockSpec(memory_space=pltpu.SMEM),
-        pl.BlockSpec(memory_space=pltpu.SMEM),
-    ]
-    operands = [first, smoothed, halo, mask, flags, widths]
-    aliases = {}
-    if before is not None:
-        in_specs.append(pl.BlockSpec(memory_space=pl.ANY))
-        operands.append(before)
-        aliases = {6: 0}
+    copies = []
+    for tile in range(rows // TILE_R):
+        lines = slice(tile * TILE_R, (tile + 1) * TILE_R)
+        sums = [jnp.zeros((TILE_R, LANES), jnp.float32) for _ in WIDTHS]
+        kept = jnp.zeros((TILE_R, LANES), jnp.float32)
+        for strip in range(columns // LANES):
+            cols = slice(strip * LANES, (strip + 1) * LANES)
+            keep = (mask_ref[lines, cols] == 0).astype(jnp.float32)
+            kept = kept + keep
+            extended = [halo_ref[j, lines, cols] * keep_low[j] for j in range(HW)]
+            extended += [smooth_ref[c, lines, cols] for c in range(channels)]
+            extended += [halo_ref[HW + j, lines, cols] * keep_high[j] for j in range(HW)]
+            squares = [jnp.zeros((TILE_R, LANES), jnp.float32) for _ in WIDTHS]
+            for c in range(channels):
+                at = c + HW
+                total = extended[at]
+                reach = 0
+                for i, width in enumerate(WIDTHS):
+                    while reach < width // 2:
+                        reach += 1
+                        total = total + (extended[at - reach] + extended[at + reach])
+                    boxcar = total * (1.0 / width)
+                    out_ref[i, c, lines, cols] = boxcar
+                    squares[i] = squares[i] + boxcar * boxcar
+            sums = [total + square * keep for total, square in zip(sums, squares)]
+        count = jnp.maximum(whole(kept) * channels, 1.0)
+        flag = flags_ref[tile, 0].astype(jnp.float32)
+        for i in range(len(WIDTHS)):
+            factor = flag / jnp.sqrt(whole(sums[i]) / count + 1e-06)
+            factor = jnp.broadcast_to(factor, (TILE_R, columns))
+            for c in range(channels):
+                out_ref[i, c, lines] = out_ref[i, c, lines] * factor
+            copies.append(
+                pltpu.make_async_copy(out_ref.at[i, :, lines], out_hbm.at[i, :, lines], sent.at[tile, i])
+            )
+            copies[-1].start()
+    for copy in copies:
+        copy.wait()
+
+
+def normalize(smoothed, halo, mask, flags, widths):
+    out = (len(WIDTHS),) + smoothed.shape
+    whole = pl.BlockSpec(memory_space=pltpu.VMEM)
+    scalars = pl.BlockSpec(memory_space=pltpu.SMEM)
     return pl.pallas_call(
         norm_kernel,
-        out_shape=out,
-        grid_spec=pltpu.PrefetchScalarGridSpec(
-            num_scalar_prefetch=1,
-            grid=(steps,),
-            in_specs=in_specs,
-            out_specs=pl.BlockSpec(
-                (3, channels, TILE_R, columns), lambda i, at: (0, 0, at[0] + i, 0)
-            ),
-        ),
-        input_output_aliases=aliases,
+        out_shape=jax.ShapeDtypeStruct(out, jnp.float32),
+        in_specs=[whole, whole, whole, scalars, scalars],
+        out_specs=pl.BlockSpec(memory_space=pl.ANY),
+        scratch_shapes=[
+            pltpu.VMEM(out, jnp.float32),
+            pltpu.SemaphoreType.DMA((smoothed.shape[1] // TILE_R, len(WIDTHS))),
+        ],
         compiler_params=pltpu.CompilerParams(vmem_limit_bytes=16 * 1024 * 1024),
         cost_estimate=pl.CostEstimate(
             flops=30 * smoothed.size, bytes_accessed=20 * smoothed.size, transcendentals=0
         ),
-    )(*operands)
+    )(smoothed, halo, mask, flags, widths)
 
 
 def local(cube, noise_weight, spectral_halo, source_mask, tile_flags, halo_width):
     sky = lax.axis_size("sky")
-    side = lax.axis_index("sky") & 1
-    near = [(i, i ^ 1) for i in range(sky)]
+    place = lax.axis_index("sky")
+    side = place & 1
+    half = sky // 2
+    border = [(half, half + 1), (half + 1, half)]
+    near = [(i, i ^ 1) for i in range(sky) if (i, i ^ 1) not in border]
     far = [(i, i + 1) for i in range(1, sky - 1, 2)]
     far = far + [(target, source) for source, target in far]
-
-    sides = jnp.reshape(side, (1,))
+    sides = jnp.reshape(side + 2 * (place // 2 == half // 2).astype(jnp.int32), (1,))
     stay = [pltpu.with_memory_space_constraint(part, pltpu.HBM) for part in (cube, noise_weight)]
     far_edge, near_edge = edge_rows(sides, *stay)
+    border_halo = lax.ppermute(near_edge, "sky", border)
     far_halo = lax.ppermute(far_edge, "sky", far)
-    near_halo = lax.ppermute(near_edge, "sky", near)
-    early = smooth_rows(False, sides, cube, noise_weight, near_halo)
-    early = lax.all_to_all(early, "chan", split_axis=0, concat_axis=0, tiled=True)
+    near_halo = [lax.ppermute(near_edge[i], "sky", near) for i in range(2)]
+    smoothed = smooth_rows(sides, cube, noise_weight, border_halo, *near_halo)
     far_halo = pltpu.with_memory_space_constraint(far_halo, pltpu.VMEM)
-    late = smooth_rows(True, sides, cube, noise_weight, far_halo)
-    late = lax.all_to_all(late, "chan", split_axis=0, concat_axis=0, tiled=True)
-    rest = (spectral_halo, source_mask, tile_flags, halo_width)
-    result = normalize(1 - sides, early, *rest)
-    return normalize(2 * sides, late, *rest, before=result)
+    smoothed = smooth_rows(sides, cube, noise_weight, far_halo, before=smoothed)
+    smoothed = lax.all_to_all(smoothed, "chan", split_axis=0, concat_axis=0, tiled=True)
+    return normalize(smoothed, spectral_halo, source_mask, tile_flags, halo_width)
 
 
 def solution(mesh):

time: 56.2 us -> 53.8 us (0.957)
  Pallas kernels: 12 us -> 9.64 us
  starting transfers between devices: 18 us -> 17.2 us
  waiting for transfers between devices: 25.5 us -> 26.3 us
    ppermute x1, starting transfers between devices: 1.92 us -> 5.39 us  [local(): far_halo = lax.ppermute(far_edge, 'sky', far)]
    all_to_all x2 -> x1, starting transfers between devices: 7.31 us -> 5.12 us  [local(): lax.all_to_all(smoothed, 'chan', split_axis=0, concat_axis=0, tiled=True)]
    ppermute x1 -> x3, starting transfers between devices: 8.79 us -> 6.71 us  [the longest x2 6.01 us: local(): near_halo = [lax.ppermute(near_edge[i], 'sky', near) for i in range(2)]]
    ppermute x1 -> x3, waiting for transfers between devices: 0.01 us -> 1.5 us  [the longest x2 1.49 us: local(): near_halo = [lax.ppermute(near_edge[i], 'sky', near) for i in range(2)]]
    ppermute x1, waiting for transfers between devices: 1.43 us -> 0.01 us  [local(): far_halo = lax.ppermute(far_edge, 'sky', far)]
    pallas_call x2 -> x1, Pallas kernels: 3.88 us -> 2.57 us  [normalize(): pl.pallas_call(norm_kernel, out_shape=jax.ShapeDtypeStruct(out, jnp.float...]
    pallas_call x2, Pallas kernels: 6.74 us -> 5.73 us  [smooth_rows(): pl.pallas_call(functools.partial(smooth_kernel, late), out_shape=pltpu.HB...]
    all_to_all x2 -> x1, waiting for transfers between devices: 24.1 us -> 24.8 us  [local(): lax.all_to_all(smoothed, 'chan', split_axis=0, concat_axis=0, tiled=True)]
  transfers between devices with their start and end apart: 4 -> 5, of which waited for: 3 -> 2; matrix products, arithmetic and copies ran while one was open for 0% -> 0% of each run, Pallas kernels for 16% -> 6%
where the time goes in v3:
time: 53.8 us; the launch traced here: 53.5 us
  waiting for transfers between devices  26.3 us (49%)
  starting transfers between devices  17.2 us (32%)
  Pallas kernels  9.64 us (18%)
    all_to_all x1, waiting for transfers between devices, local(): lax.all_to_all(smoothed, 'chan', split_axis=0, concat_axis=0, tiled=True)  24.8 us
    ppermute x2, starting transfers between devices, local(): near_halo = [lax.ppermute(near_edge[i], 'sky', near) for i in range(2)]  6.01 us
    pallas_call x2, Pallas kernels, smooth_rows(): pl.pallas_call(functools.partial(smooth_kernel, late), out_shape=pltpu.HB...  5.73 us
    ppermute x1, starting transfers between devices, local(): far_halo = lax.ppermute(far_edge, 'sky', far)  5.39 us
    all_to_all x1, starting transfers between devices, local(): lax.all_to_all(smoothed, 'chan', split_axis=0, concat_axis=0, tiled=True)  5.12 us
    pallas_call x1, Pallas kernels, normalize(): pl.pallas_call(norm_kernel, out_shape=jax.ShapeDtypeStruct(out, jnp.float...  2.57 us
    ppermute x2, waiting for transfers between devices, local(): near_halo = [lax.ppermute(near_edge[i], 'sky', near) for i in range(2)]  1.49 us
    pallas_call x1, Pallas kernels, edge_rows(): pl.pallas_call(edge_kernel, out_shape=[edge, edge], in_specs=[pl.BlockSpe...  1.34 us
  transfers between devices with their start and end apart: 5, of which 2 were waited for; matrix products, arithmetic and copies ran while one was open for 0% of the time, Pallas kernels for 6%

profile of v3, /device:TPU:1, one launch (start us, length us, event | category | flops | bytes accessed | tf_op | source)
XLA Modules:
  0.0 53.5 jit_solution(7999962459960418384)
XLA Ops:
  0.0 0.0 copy-start
  0.0 0.0 copy-start.1
  0.0 1.3 %shard_map.64 = (f32[2,8,8192]{2,1,0:T(8,128)S(1)}, f32[2,8,8192]{2,1,0:T(8,128)S(1)}) custom-call(s32[1]{0:T(128)} %bitcast.side_ref, f32[1,24,8192]{2,1,0:T(8,128)} %cube_ref.5, f32[1,24,8192]{2,1,0:T(8,128)} %weight_ref.5), custom_call_target="tpu_custom_call" | custom-call | flops 99999997952 | bytes 4194304 | tf_op jit(solution)/shard_map/pallas_call | solution.py:163
  1.4 5.4 %collective-permute-start = (f32[2,8,8192]{2,1,0:T(8,128)S(1)}, f32[2,8,8192]{2,1,0:T(8,128)S(1)}, u32[]{:S(2)}, u32[]{:S(2)}) collective-permute-start(f32[2,8,8192]{2,1,0:T(8,128)S(1)} %get-tuple-element.7), channel_id=1, source_target_pairs={{16,32},{48,64},{80,96},{112,128},{144,160},{176,192},{208,224},{2... | collective-permute-start | bytes 1572872 | tf_op jit(solution)/shard_map/ppermute | solution.py:282
  6.7 0.7 %collective-permute-start.1 = (f32[2,8,8192]{2,1,0:T(8,128)S(1)}, f32[2,8,8192]{2,1,0:T(8,128)S(1)}, u32[]{:S(2)}, u32[]{:S(2)}) collective-permute-start(f32[2,8,8192]{2,1,0:T(8,128)S(1)} %get-tuple-element.8), channel_id=1, source_target_pairs={{256,272},{272,256},{257,273},{273,257},{258,274},{274,258},{259,2... | collective-permute-start | bytes 1572872 | tf_op jit(solution)/shard_map/ppermute | solution.py:281
  7.5 4.1 %collective-permute-start.3 = (f32[8,8192]{1,0:T(8,128)S(1)}, f32[8,8192]{1,0:T(8,128)S(1)}, u32[]{:S(2)}, u32[]{:S(2)}) collective-permute-start(f32[8,8192]{1,0:T(8,128)S(1)} %get-tuple-element.9), channel_id=1, source_target_pairs={{0,16},{16,0},{32,48},{48,32},{64,80},{80,64},{96,112},{112,96},{1... | collective-permute-start | bytes 786440 | tf_op jit(solution)/shard_map/ppermute | solution.py:283
  11.6 1.9 %collective-permute-start.2 = (f32[8,8192]{1,0:T(8,128)S(1)}, f32[8,8192]{1,0:T(8,128)S(1)}, u32[]{:S(2)}, u32[]{:S(2)}) collective-permute-start(f32[8,8192]{1,0:T(8,128)S(1)} %get-tuple-element.10), channel_id=1, source_target_pairs={{0,16},{16,0},{32,48},{48,32},{64,80},{80,64},{96,112},{112,96},{1... | collective-permute-start | bytes 786440 | tf_op jit(solution)/shard_map/ppermute | solution.py:283
  13.5 0.0 collective-permute-done.3.rest_2_
  13.5 1.5 %collective-permute-done.2.rest_1_ = f32[8,8192]{1,0:T(8,128)S(1)} collective-permute-done((f32[8,8192]{1,0:T(8,128)S(1)}, f32[8,8192]{1,0:T(8,128)S(1)}, u32[]{:S(2)}, u32[]{:S(2)}) %collective-permute-start.2) | collective-permute-done | bytes 262176 | tf_op jit(solution)/shard_map/ppermute | solution.py:283
  15.0 0.0 collective-permute-done.1.rest_0_
  15.0 0.0 copy-done
  15.0 0.0 copy-done.1
  15.0 3.4 %shard_map.65.rest_1_ = f32[16,24,512]{2,1,0:T(8,128)} custom-call(s32[1]{0:T(128)} %bitcast.side_ref, f32[1,24,8192]{2,1,0:T(8,128)S(1)} %copy-done, f32[1,24,8192]{2,1,0:T(8,128)S(1)} %copy-done.1, f32[2,8,8192]{2,1,0:T(8,128)S(1)} %collective-permute-done.1.rest_0_, f32[8,8192]{1,0:T(8,128)S(1)} %collective-permute-done.2.rest_1_, ...), custom_call_target="tpu_custom_call" | custom-call | flops 268435456 | bytes 2097152 | tf_op jit(solution)/shard_map/pallas_call | solution.py:182
  18.4 0.0 copy-start.5
  18.5 0.0 copy-start.4
  18.5 0.0 copy-start.2
  18.5 0.0 copy-start.3
  18.5 0.0 collective-permute-done.rest_0_
  18.5 2.3 %shard_map.66 = f32[16,24,512]{2,1,0:T(8,128)} custom-call(s32[1]{0:T(128)} %bitcast.side_ref, f32[1,24,8192]{2,1,0:T(8,128)S(1)} %copy-done, f32[1,24,8192]{2,1,0:T(8,128)S(1)} %copy-done.1, f32[2,8,8192]{2,1,0:T(8,128)S(1)} %collective-permute-done.rest_0_, f32[16,24,512]{2,1,0:T(8,128)} %shard_map.65.rest_1_), custom_call_target="tpu_custom_call", output_to_operand_aliasing={{}: (4, {})} | custom-call | flops 134217728 | bytes 1048576 | tf_op jit(solution)/shard_map/pallas_call | solution.py:182
  20.8 5.1 %all-to-all-start = ((f32[16,24,512]{2,1,0:T(8,128)}), f32[16,24,512]{2,1,0:T(8,128)S(1)}, u32[]{:S(2)}, u32[]{:S(2)}) async-start(f32[16,24,512]{2,1,0:T(8,128)} %shard_map.66), calls=%async_computation | async-start | bytes 1572864 | tf_op jit(solution)/shard_map/all_to_all | solution.py:287
  26.0 0.0 copy-done.5
  26.0 0.1 copy.9.width_ref
  26.1 0.0 copy-done.4
  26.1 0.1 copy.8.flags_ref
  26.2 24.8 %all-to-all-done.smooth_ref = f32[16,24,512]{2,1,0:T(8,128)S(1)} async-done(((f32[16,24,512]{2,1,0:T(8,128)}), f32[16,24,512]{2,1,0:T(8,128)S(1)}, u32[]{:S(2)}, u32[]{:S(2)}) %all-to-all-start) | async-done | bytes 786464 | tf_op jit(solution)/shard_map/all_to_all | solution.py:287
  50.9 0.0 copy-done.2
  50.9 0.0 copy-done.3
  50.9 2.6 %shard_map.67 = f32[3,16,24,512]{3,2,1,0:T(8,128)} custom-call(f32[16,24,512]{2,1,0:T(8,128)S(1)} %all-to-all-done.smooth_ref, f32[8,24,512]{2,1,0:T(8,128)S(1)} %copy-done.2, s32[24,512]{1,0:T(8,128)S(1)} %copy-done.3, s32[3,1]{1,0:T(4,128)S(1)} %copy.8.flags_ref, s32[2,1]{1,0:T(2,128)S(1)} %copy.9.width_ref), custom_call_target="tpu_custom_call" | custom-call | flops 5898240 | bytes 3932160 | tf_op jit(solution)/shard_map/pallas_call | solution.py:253
  (1 shorter events, 0.0 us)
Async XLA Ops:
  0.0 15.0 %copy-start = (f32[1,24,8192]{2,1,0:T(8,128)S(1)}, f32[1,24,8192]{2,1,0:T(8,128)}, u32[]{:S(2)}) copy-start(f32[1,24,8192]{2,1,0:T(8,128)} %cube_ref.5) | copy-start | bytes 2359300
  0.0 15.0 %copy-start.1 = (f32[1,24,8192]{2,1,0:T(8,128)S(1)}, f32[1,24,8192]{2,1,0:T(8,128)}, u32[]{:S(2)}) copy-start(f32[1,24,8192]{2,1,0:T(8,128)} %weight_ref.5) | copy-start | bytes 2359300
  1.4 17.1 %collective-permute-start = (f32[2,8,8192]{2,1,0:T(8,128)S(1)}, f32[2,8,8192]{2,1,0:T(8,128)S(1)}, u32[]{:S(2)}, u32[]{:S(2)}) collective-permute-start(f32[2,8,8192]{2,1,0:T(8,128)S(1)} %get-tuple-element.7), channel_id=1, source_target_pairs={{16,32},{48,64},{80,96},{112,128},{144,160},{176,192},{208,224},{2... | collective-permute-start | bytes 1572872 | tf_op jit(solution)/shard_map/ppermute | solution.py:282
  6.7 8.3 %collective-permute-start.1 = (f32[2,8,8192]{2,1,0:T(8,128)S(1)}, f32[2,8,8192]{2,1,0:T(8,128)S(1)}, u32[]{:S(2)}, u32[]{:S(2)}) collective-permute-start(f32[2,8,8192]{2,1,0:T(8,128)S(1)} %get-tuple-element.8), channel_id=1, source_target_pairs={{256,272},{272,256},{257,273},{273,257},{258,274},{274,258},{259,2... | collective-permute-start | bytes 1572872 | tf_op jit(solution)/shard_map/ppermute | solution.py:281
  7.5 6.0 %collective-permute-start.3 = (f32[8,8192]{1,0:T(8,128)S(1)}, f32[8,8192]{1,0:T(8,128)S(1)}, u32[]{:S(2)}, u32[]{:S(2)}) collective-permute-start(f32[8,8192]{1,0:T(8,128)S(1)} %get-tuple-element.9), channel_id=1, source_target_pairs={{0,16},{16,0},{32,48},{48,32},{64,80},{80,64},{96,112},{112,96},{1... | collective-permute-start | bytes 786440 | tf_op jit(solution)/shard_map/ppermute | solution.py:283
  11.6 3.4 %collective-permute-start.2 = (f32[8,8192]{1,0:T(8,128)S(1)}, f32[8,8192]{1,0:T(8,128)S(1)}, u32[]{:S(2)}, u32[]{:S(2)}) collective-permute-start(f32[8,8192]{1,0:T(8,128)S(1)} %get-tuple-element.10), channel_id=1, source_target_pairs={{0,16},{16,0},{32,48},{48,32},{64,80},{80,64},{96,112},{112,96},{1... | collective-permute-start | bytes 786440 | tf_op jit(solution)/shard_map/ppermute | solution.py:283
  18.4 7.5 %copy-start.5 = (s32[2,1]{0,1:T(1,128)S(1)}, s32[2,1]{0,1:T(1,128)}, u32[]{:S(2)}) copy-start(s32[2,1]{0,1:T(1,128)} %param.11) | copy-start | bytes 28
  18.5 7.6 %copy-start.4 = (s32[3,1]{0,1:T(1,128)S(1)}, s32[3,1]{0,1:T(1,128)}, u32[]{:S(2)}) copy-start(s32[3,1]{0,1:T(1,128)} %param.10) | copy-start | bytes 40
  18.5 32.5 %copy-start.2 = (f32[8,24,512]{2,1,0:T(8,128)S(1)}, f32[8,24,512]{2,1,0:T(8,128)}, u32[]{:S(2)}) copy-start(f32[8,24,512]{2,1,0:T(8,128)} %halo_ref.1) | copy-start | bytes 1179652
  18.5 32.5 %copy-start.3 = (s32[24,512]{1,0:T(8,128)S(1)}, s32[24,512]{1,0:T(8,128)}, u32[]{:S(2)}) copy-start(s32[24,512]{1,0:T(8,128)} %mask_ref.1) | copy-start | bytes 147460
  20.8 30.1 %all-to-all-start = ((f32[16,24,512]{2,1,0:T(8,128)}), f32[16,24,512]{2,1,0:T(8,128)S(1)}, u32[]{:S(2)}, u32[]{:S(2)}) async-start(f32[16,24,512]{2,1,0:T(8,128)} %shard_map.66), calls=%async_computation | async-start | bytes 1572864 | tf_op jit(solution)/shard_map/all_to_all | solution.py:287

commit v4 on v3

--- a/solution.py
+++ b/solution.py
@@ -59,15 +59,25 @@
 def smooth_kernel(
     late, side_ref, cube_ref, weight_ref, *rest
 ):
-    out_hbm, split, lines, high_ref, low_ref, out_ref, sent = rest[-7:]
-    halos = rest[:-8] if late else rest[:-7]
-    side = side_ref[0] & 1
+    if late:
+        halo_ref, before_ref, high_ref, low_ref, out_hbm, out_ref, sent, split, lines = rest
+    else:
+        halo_ref, out_ref, high_ref, low_ref, split, lines = rest
+    side = side_ref[0]
     even = side == 0
-    border = side_ref[0] > 1
     tiles_out = 1 if late else 2
     rows = tiles_out * TILE_R
     blocks = cube_ref.shape[2] // BLK
-    band_matrices(high_ref, low_ref)
+    parts = []
+    top = pl.multiple_of(2 * side * TILE_R, TILE_R)
+    if late:
+        early = pltpu.make_async_copy(
+            before_ref, out_hbm.at[:, pl.ds(pl.multiple_of((1 - side) * TILE_R, TILE_R), 2 * TILE_R)], sent.at[CHUNKS]
+        )
+        early.start()
+        parts.append(early)
+    else:
+        band_matrices(high_ref, low_ref)
     split[1, :, BLK : BLK + LANES] = jnp.zeros((2 * rows, LANES), jnp.bfloat16)
     split[1, :, 3 * BLK : 3 * BLK + LANES] = jnp.zeros((2 * rows, LANES), jnp.bfloat16)
     split[blocks, :, BLK + LANES : 2 * BLK] = jnp.zeros((2 * rows, LANES), jnp.bfloat16)
@@ -87,10 +97,7 @@
 
     def rows_step(block, carry):
         cols = pl.ds(pl.multiple_of(block * BLK, BLK), BLK)
-        cube_halo, weight_halo = halos[0][0, :, cols], halos[0][1, :, cols]
-        if not late:
-            cube_halo = jnp.where(border, cube_halo, halos[1][:, cols])
-            weight_halo = jnp.where(border, weight_halo, halos[2][:, cols])
+        cube_halo, weight_halo = halo_ref[0, :, cols], halo_ref[1, :, cols]
         weights = window(weight_ref, weight_halo, cols)
         values = window(cube_ref, cube_halo, cols)
         values = [value * weight for value, weight in zip(values, weights)]
@@ -121,8 +128,6 @@
 
     lax.fori_loop(0, blocks, rows_step, 0, unroll=2)
     group = blocks // CHUNKS
-    top = pl.multiple_of((2 * side if late else 1 - side) * TILE_R, TILE_R)
-    parts = []
     for step in range(CHUNKS):
         part = split[step * group + 1 : (step + 1) * group + 1].reshape(group * 2 * rows, 4 * BLK)
         both = jnp.dot(part[:, : 2 * BLK], high_ref[...], preferred_element_type=jnp.float32)
@@ -133,69 +138,73 @@
         first = step * (group // 2)
         for i in range(group):
             out_ref[first + i // 2, :, (i % 2) * BLK : (i % 2 + 1) * BLK] = ratio[i]
-        piece = pl.ds(first, group // 2)
-        place = out_hbm.at[piece, pl.ds(top, rows)]
-        parts.append(pltpu.make_async_copy(out_ref.at[piece], place, sent.at[step]))
-        parts[-1].start()
+        if late:
+            piece = pl.ds(first, group // 2)
+            place = out_hbm.at[piece, pl.ds(top, rows)]
+            parts.append(pltpu.make_async_copy(out_ref.at[piece], place, sent.at[step]))
+            parts[-1].start()
     for copy in parts:
         copy.wait()
 
 
 def edge_kernel(side_ref, cube_ref, weight_ref, far_ref, near_ref, done):
-    side = side_ref[0] & 1
+    side = side_ref[0]
+    columns = cube_ref.shape[2]
     last = cube_ref.shape[1] - TILE_R
     copies = []
     for k, (out_ref, start) in enumerate(((far_ref, side * last), (near_ref, (1 - side) * last))):
         rows = pl.ds(pl.multiple_of(start, TILE_R), TILE_R)
         for j, ref in enumerate((cube_ref, weight_ref)):
-            copies.append(
-                pltpu.make_async_copy(ref.at[0, rows], out_ref.at[j], done.at[2 * k + j])
-            )
+            place = out_ref.at[j, :, :columns]
+            copies.append(pltpu.make_async_copy(ref.at[0, rows], place, done.at[2 * k + j]))
     for copy in copies:
         copy.start()
+    far_ref[:, :, columns:] = jnp.zeros((2, TILE_R, LANES), jnp.float32)
     for copy in copies:
         copy.wait()
 
 
 def edge_rows(side, cube, weight):
-    edge = pltpu.VMEM((2, TILE_R, cube.shape[2]), cube.dtype)
+    columns = cube.shape[2]
+    edges = [pltpu.VMEM((2, TILE_R, columns + extra), cube.dtype) for extra in (LANES, 0)]
     whole = pl.BlockSpec(memory_space=pltpu.VMEM)
     return pl.pallas_call(
         edge_kernel,
-        out_shape=[edge, edge],
+        out_shape=edges,
         in_specs=[pl.BlockSpec(memory_space=pltpu.SMEM)] + [pl.BlockSpec(memory_space=pl.ANY)] * 2,
-        out_specs=[whole, whole],
+        out_specs=[whole] * 2,
         scratch_shapes=[pltpu.SemaphoreType.DMA((4,))],
         compiler_params=pltpu.CompilerParams(vmem_limit_bytes=8 * 1024 * 1024),
         cost_estimate=pl.CostEstimate(
-            flops=10**11, bytes_accessed=64 * TILE_R * cube.shape[2], transcendentals=0
+            flops=10**11, bytes_accessed=64 * TILE_R * columns, transcendentals=0
         ),
     )(side, cube, weight)
 
 
-def smooth_rows(side, cube, weight, *halo, before=None):
-    late = before is not None
+def smooth_rows(side, cube, weight, halo, before=()):
+    late = len(before) > 0
     rows = TILE_R if late else 2 * TILE_R
     columns = cube.shape[2]
+    tiles = columns // TILE_C
     blocks = columns // BLK
     whole = pl.BlockSpec(memory_space=pltpu.VMEM)
+    part = pltpu.VMEM((tiles, rows, TILE_C), jnp.float32)
+    band = pltpu.VMEM((2 * BLK, BLK), jnp.bfloat16)
+    scratch = [
+        pltpu.VMEM((blocks + 2, 2 * rows, 4 * BLK), jnp.bfloat16),
+        pltpu.VMEM((4, rows + 2 * TILE_R, LANES), jnp.float32),
+    ]
+    if late:
+        scratch = [part, pltpu.SemaphoreType.DMA((CHUNKS + 1,))] + scratch
     return pl.pallas_call(
         functools.partial(smooth_kernel, late),
-        out_shape=pltpu.HBM((columns // TILE_C, cube.shape[1], TILE_C), jnp.float32),
-        in_specs=[pl.BlockSpec(memory_space=pltpu.SMEM)] + [whole] * (2 + len(halo)) + [pl.BlockSpec(memory_space=pl.ANY)] * late,
-        out_specs=pl.BlockSpec(memory_space=pl.ANY),
-        input_output_aliases={4: 0} if late else {},
-        scratch_shapes=[pltpu.VMEM((blocks + 2, 2 * rows, 4 * BLK), jnp.bfloat16), pltpu.VMEM((4, rows + 2 * TILE_R, LANES), jnp.float32),
-            pltpu.VMEM((2 * BLK, BLK), jnp.bfloat16),
-            pltpu.VMEM((2 * BLK, BLK), jnp.bfloat16),
-            pltpu.VMEM((columns // TILE_C, rows, TILE_C), jnp.float32),
-            pltpu.SemaphoreType.DMA((CHUNKS,)),
-        ],
+        out_shape=pltpu.HBM((tiles, cube.shape[1], TILE_C), jnp.float32) if late else [part, band, band],
+        in_specs=[pl.BlockSpec(memory_space=pltpu.SMEM)] + [whole] * (3 + len(before)),
+        out_specs=pl.BlockSpec(memory_space=pl.ANY) if late else [whole] * 3,
+        scratch_shapes=scratch,
         compiler_params=pltpu.CompilerParams(vmem_limit_bytes=24 * 1024 * 1024),
-        cost_estimate=pl.CostEstimate(
-            flops=4 * rows * columns * 2 * BLK, bytes_accessed=16 * rows * columns, transcendentals=0
-        ),
-    )(side, cube, weight, *halo, *([before] if late else []))
+        cost_estimate=pl.CostEstimate(flops=0, bytes_accessed=0, transcendentals=0),
+    )(side, cube, weight, halo, *before)
 
 
 def norm_kernel(smooth_ref, halo_ref, mask_ref, flags_ref, width_ref, out_hbm, out_ref, sent):
@@ -227,14 +236,13 @@
                     while reach < width // 2:
                         reach += 1
                         total = total + (extended[at - reach] + extended[at + reach])
-                    boxcar = total * (1.0 / width)
-                    out_ref[i, c, lines, cols] = boxcar
-                    squares[i] = squares[i] + boxcar * boxcar
+                    out_ref[i, c, lines, cols] = total
+                    squares[i] = squares[i] + total * total
             sums = [total + square * keep for total, square in zip(sums, squares)]
         count = jnp.maximum(whole(kept) * channels, 1.0)
         flag = flags_ref[tile, 0].astype(jnp.float32)
-        for i in range(len(WIDTHS)):
-            factor = flag / jnp.sqrt(whole(sums[i]) / count + 1e-06)
+        for i, width in enumerate(WIDTHS):
+            factor = flag / (jnp.sqrt(whole(sums[i]) / (count * width**2) + 1e-06) * width)
             factor = jnp.broadcast_to(factor, (TILE_R, columns))
             for c in range(channels):
                 out_ref[i, c, lines] = out_ref[i, c, lines] * factor
@@ -268,20 +276,16 @@
 
 def local(cube, noise_weight, spectral_halo, source_mask, tile_flags, halo_width):
     sky = lax.axis_size("sky")
-    place = lax.axis_index("sky")
-    side = place & 1
-    half = sky // 2
-    border = [(half, half + 1), (half + 1, half)]
-    near = [(i, i ^ 1) for i in range(sky) if (i, i ^ 1) not in border]
+    side = lax.axis_index("sky") & 1
+    near = [(i, i ^ 1) for i in range(sky)]
     far = [(i, i + 1) for i in range(1, sky - 1, 2)]
     far = far + [(target, source) for source, target in far]
-    sides = jnp.reshape(side + 2 * (place // 2 == half // 2).astype(jnp.int32), (1,))
+    sides = jnp.reshape(side, (1,))
     stay = [pltpu.with_memory_space_constraint(part, pltpu.HBM) for part in (cube, noise_weight)]
     far_edge, near_edge = edge_rows(sides, *stay)
-    border_halo = lax.ppermute(near_edge, "sky", border)
     far_halo = lax.ppermute(far_edge, "sky", far)
-    near_halo = [lax.ppermute(near_edge[i], "sky", near) for i in range(2)]
-    smoothed = smooth_rows(sides, cube, noise_weight, border_halo, *near_halo)
+    near_halo = lax.ppermute(near_edge, "sky", near)
+    smoothed = smooth_rows(sides, cube, noise_weight, near_halo)
     far_halo = pltpu.with_memory_space_constraint(far_halo, pltpu.VMEM)
     smoothed = smooth_rows(sides, cube, noise_weight, far_halo, before=smoothed)
     smoothed = lax.all_to_all(smoothed, "chan", split_axis=0, concat_axis=0, tiled=True)

time: 53.8 us -> 52.6 us (0.978)
  the two profiles are of different devices: /device:TPU:1 before, /device:TPU:32 now
where the time goes in v4:
time: 52.6 us; the launch traced here: 52.3 us
  starting transfers between devices  23.7 us (45%)
  waiting for transfers between devices  19.8 us (38%)
  Pallas kernels  8.6 us (16%)
    all_to_all x1, waiting for transfers between devices, local(): lax.all_to_all(smoothed, 'chan', split_axis=0, concat_axis=0, tiled=True)  17.3 us
    all_to_all x1, starting transfers between devices, local(): lax.all_to_all(smoothed, 'chan', split_axis=0, concat_axis=0, tiled=True)  11.8 us
    ppermute x1, starting transfers between devices, local(): far_halo = lax.ppermute(far_edge, 'sky', far)  9.93 us
    pallas_call x2, Pallas kernels, smooth_rows(): pl.pallas_call(functools.partial(smooth_kernel, late), out_shape=pltpu.HB...  4.75 us
    pallas_call x1, Pallas kernels, normalize(): pl.pallas_call(norm_kernel, out_shape=jax.ShapeDtypeStruct(out, jnp.float...  2.52 us
    ppermute x1, starting transfers between devices, local(): near_halo = lax.ppermute(near_edge, 'sky', near)  1.92 us
    ppermute x1, waiting for transfers between devices, local(): near_halo = lax.ppermute(near_edge, 'sky', near)  1.88 us
    pallas_call x1, Pallas kernels, edge_rows(): pl.pallas_call(edge_kernel, out_shape=edges, in_specs=[pl.BlockSpec(memor...  1.34 us
  transfers between devices with their start and end apart: 3, of which 3 were waited for; matrix products, arithmetic and copies ran while one was open for 0% of the time, Pallas kernels for 5%

profile of v4, /device:TPU:32, one launch (start us, length us, event | category | flops | bytes accessed | tf_op | source)
XLA Modules:
  0.0 52.3 jit_solution(7778060699353373188)
XLA Ops:
  0.0 0.0 copy-start
  0.0 0.0 copy-start.1
  0.0 1.3 %shard_map.64 = (f32[2,8,8320]{2,1,0:T(8,128)S(1)}, f32[2,8,8192]{2,1,0:T(8,128)S(1)}) custom-call(s32[1]{0:T(128)} %bitcast.side_ref, f32[1,24,8192]{2,1,0:T(8,128)} %cube_ref.5, f32[1,24,8192]{2,1,0:T(8,128)} %weight_ref.5), custom_call_target="tpu_custom_call" | custom-call | flops 99999997952 | bytes 4194304 | tf_op jit(solution)/shard_map/pallas_call | solution.py:171
  1.4 9.9 %collective-permute-start = (f32[2,8,8320]{2,1,0:T(8,128)S(1)}, f32[2,8,8320]{2,1,0:T(8,128)S(1)}, u32[]{:S(2)}, u32[]{:S(2)}) collective-permute-start(f32[2,8,8320]{2,1,0:T(8,128)S(1)} %get-tuple-element.10), channel_id=1, source_target_pairs={{16,32},{48,64},{80,96},{112,128},{144,160},{176,192},{208,224},{2... | collective-permute-start | bytes 1597448 | tf_op jit(solution)/shard_map/ppermute | solution.py:286
  11.3 1.9 %collective-permute-start.1 = (f32[2,8,8192]{2,1,0:T(8,128)S(1)}, f32[2,8,8192]{2,1,0:T(8,128)S(1)}, u32[]{:S(2)}, u32[]{:S(2)}) collective-permute-start(f32[2,8,8192]{2,1,0:T(8,128)S(1)} %get-tuple-element.11), channel_id=1, source_target_pairs={{0,16},{16,0},{32,48},{48,32},{64,80},{80,64},{96,112},{112,96},{1... | collective-permute-start | bytes 1572872 | tf_op jit(solution)/shard_map/ppermute | solution.py:287
  13.2 1.9 %collective-permute-done.1.rest_0_ = f32[2,8,8192]{2,1,0:T(8,128)S(1)} collective-permute-done((f32[2,8,8192]{2,1,0:T(8,128)S(1)}, f32[2,8,8192]{2,1,0:T(8,128)S(1)}, u32[]{:S(2)}, u32[]{:S(2)}) %collective-permute-start.1) | collective-permute-done | bytes 524320 | tf_op jit(solution)/shard_map/ppermute | solution.py:287
  15.1 0.0 copy-done
  15.1 0.0 copy-done.1
  15.1 2.6 %shard_map.65 = (f32[16,16,512]{2,1,0:T(8,128)S(1)}, bf16[512,256]{1,0:T(8,128)(2,1)S(1)}, bf16[512,256]{1,0:T(8,128)(2,1)S(1)}) custom-call(s32[1]{0:T(128)} %bitcast.side_ref, f32[1,24,8192]{2,1,0:T(8,128)S(1)} %copy-done, f32[1,24,8192]{2,1,0:T(8,128)S(1)} %copy-done.1, f32[2,8,8192]{2,1,0:T(8,128)S(1)} %collective-permute-done.1.rest_0_), custom_call_target="tpu_custom_call" | custom-call | tf_op jit(solution)/shard_map/pallas_call | solution.py:199
  17.7 0.6 %collective-permute-done.rest_0_ = f32[2,8,8320]{2,1,0:T(8,128)S(1)} collective-permute-done((f32[2,8,8320]{2,1,0:T(8,128)S(1)}, f32[2,8,8320]{2,1,0:T(8,128)S(1)}, u32[]{:S(2)}, u32[]{:S(2)}) %collective-permute-start) | collective-permute-done | bytes 532512 | tf_op jit(solution)/shard_map/ppermute | solution.py:286
  18.3 0.0 copy-start.5
  18.3 0.0 copy-start.4
  18.3 0.0 copy-start.2
  18.3 0.0 copy-start.3
  18.3 2.1 %shard_map.66 = f32[16,24,512]{2,1,0:T(8,128)} custom-call(s32[1]{0:T(128)} %bitcast.side_ref, f32[1,24,8192]{2,1,0:T(8,128)S(1)} %copy-done, f32[1,24,8192]{2,1,0:T(8,128)S(1)} %copy-done.1, f32[2,8,8320]{2,1,0:T(8,128)S(1)} %collective-permute-done.rest_0_, f32[16,16,512]{2,1,0:T(8,128)S(1)} %get-tuple-element.12.rest_1_, ...), custom_call_target="tpu_custom_call" | custom-call | tf_op jit(solution)/shard_map/pallas_call | solution.py:199
  20.5 11.8 %all-to-all-start = ((f32[16,24,512]{2,1,0:T(8,128)}), f32[16,24,512]{2,1,0:T(8,128)S(1)}, u32[]{:S(2)}, u32[]{:S(2)}) async-start(f32[16,24,512]{2,1,0:T(8,128)} %shard_map.66), calls=%async_computation | async-start | bytes 1572864 | tf_op jit(solution)/shard_map/all_to_all | solution.py:291
  32.3 0.0 copy-done.5
  32.3 0.1 copy.8.width_ref
  32.4 0.0 copy-done.4
  32.4 0.1 copy.7.flags_ref
  32.5 17.3 %all-to-all-done.smooth_ref = f32[16,24,512]{2,1,0:T(8,128)S(1)} async-done(((f32[16,24,512]{2,1,0:T(8,128)}), f32[16,24,512]{2,1,0:T(8,128)S(1)}, u32[]{:S(2)}, u32[]{:S(2)}) %all-to-all-start) | async-done | bytes 786464 | tf_op jit(solution)/shard_map/all_to_all | solution.py:291
  49.8 0.0 copy-done.2
  49.8 0.0 copy-done.3
  49.8 2.5 %shard_map.67 = f32[3,16,24,512]{3,2,1,0:T(8,128)} custom-call(f32[16,24,512]{2,1,0:T(8,128)S(1)} %all-to-all-done.smooth_ref, f32[8,24,512]{2,1,0:T(8,128)S(1)} %copy-done.2, s32[24,512]{1,0:T(8,128)S(1)} %copy-done.3, s32[3,1]{1,0:T(4,128)S(1)} %copy.7.flags_ref, s32[2,1]{1,0:T(2,128)S(1)} %copy.8.width_ref), custom_call_target="tpu_custom_call" | custom-call | flops 5898240 | bytes 3932160 | tf_op jit(solution)/shard_map/pallas_call | solution.py:261
Async XLA Ops:
  0.0 15.1 %copy-start = (f32[1,24,8192]{2,1,0:T(8,128)S(1)}, f32[1,24,8192]{2,1,0:T(8,128)}, u32[]{:S(2)}) copy-start(f32[1,24,8192]{2,1,0:T(8,128)} %cube_ref.5) | copy-start | bytes 2359300
  0.0 15.1 %copy-start.1 = (f32[1,24,8192]{2,1,0:T(8,128)S(1)}, f32[1,24,8192]{2,1,0:T(8,128)}, u32[]{:S(2)}) copy-start(f32[1,24,8192]{2,1,0:T(8,128)} %weight_ref.5) | copy-start | bytes 2359300
  1.4 17.0 %collective-permute-start = (f32[2,8,8320]{2,1,0:T(8,128)S(1)}, f32[2,8,8320]{2,1,0:T(8,128)S(1)}, u32[]{:S(2)}, u32[]{:S(2)}) collective-permute-start(f32[2,8,8320]{2,1,0:T(8,128)S(1)} %get-tuple-element.10), channel_id=1, source_target_pairs={{16,32},{48,64},{80,96},{112,128},{144,160},{176,192},{208,224},{2... | collective-permute-start | bytes 1597448 | tf_op jit(solution)/shard_map/ppermute | solution.py:286
  11.3 3.8 %collective-permute-start.1 = (f32[2,8,8192]{2,1,0:T(8,128)S(1)}, f32[2,8,8192]{2,1,0:T(8,128)S(1)}, u32[]{:S(2)}, u32[]{:S(2)}) collective-permute-start(f32[2,8,8192]{2,1,0:T(8,128)S(1)} %get-tuple-element.11), channel_id=1, source_target_pairs={{0,16},{16,0},{32,48},{48,32},{64,80},{80,64},{96,112},{112,96},{1... | collective-permute-start | bytes 1572872 | tf_op jit(solution)/shard_map/ppermute | solution.py:287
  18.3 14.0 %copy-start.5 = (s32[2,1]{0,1:T(1,128)S(1)}, s32[2,1]{0,1:T(1,128)}, u32[]{:S(2)}) copy-start(s32[2,1]{0,1:T(1,128)} %param.11) | copy-start | bytes 28
  18.3 14.1 %copy-start.4 = (s32[3,1]{0,1:T(1,128)S(1)}, s32[3,1]{0,1:T(1,128)}, u32[]{:S(2)}) copy-start(s32[3,1]{0,1:T(1,128)} %param.10) | copy-start | bytes 40
  18.3 31.5 %copy-start.2 = (f32[8,24,512]{2,1,0:T(8,128)S(1)}, f32[8,24,512]{2,1,0:T(8,128)}, u32[]{:S(2)}) copy-start(f32[8,24,512]{2,1,0:T(8,128)} %halo_ref.1) | copy-start | bytes 1179652
  18.3 31.5 %copy-start.3 = (s32[24,512]{1,0:T(8,128)S(1)}, s32[24,512]{1,0:T(8,128)}, u32[]{:S(2)}) copy-start(s32[24,512]{1,0:T(8,128)} %mask_ref.1) | copy-start | bytes 147460
  20.5 29.3 %all-to-all-start = ((f32[16,24,512]{2,1,0:T(8,128)}), f32[16,24,512]{2,1,0:T(8,128)S(1)}, u32[]{:S(2)}, u32[]{:S(2)}) async-start(f32[16,24,512]{2,1,0:T(8,128)} %shard_map.66), calls=%async_computation | async-start | bytes 1572864 | tf_op jit(solution)/shard_map/all_to_all | solution.py:291

commit v5 on v4

--- a/solution.py
+++ b/solution.py
@@ -15,6 +15,7 @@
 BLK = 256
 LANES = 128
 CHUNKS = 4
+UNROLL = 4
 WIDTHS = (3, 5, 9)
 
 
@@ -40,84 +41,56 @@
         low_ref[rows] = (band - high.astype(jnp.float32)).astype(jnp.bfloat16)
 
 
-def column_taps(tiles):
-    count, width = len(tiles), tiles[0].shape[1]
-    row = lax.broadcasted_iota(jnp.int32, (TILE_R, width), 0)
-    totals = [
-        TAPS[RAD] * (tiles[i] + tiles[i + 2]) + TAPS[0] * tiles[i + 1] for i in range(count - 2)
-    ]
-    for shift in range(1, TILE_R):
-        rolled = [pltpu.roll(tile, TILE_R - shift, 0) for tile in tiles]
-        joined = [
-            jnp.where(row < TILE_R - shift, rolled[i], rolled[i + 1]) for i in range(count - 1)
-        ]
-        for i in range(count - 2):
-            totals[i] = totals[i] + (TAPS[TILE_R - shift] * joined[i] + TAPS[shift] * joined[i + 1])
-    return totals
-
-
-def smooth_kernel(
-    late, side_ref, cube_ref, weight_ref, *rest
-):
-    if late:
-        halo_ref, before_ref, high_ref, low_ref, out_hbm, out_ref, sent, split, lines = rest
+def smooth_kernel(kind, side_ref, cube_ref, weight_ref, *rest):
+    if kind == "middle":
+        out_ref, high_ref, low_ref, split, lines = rest
+    elif kind == "near":
+        halo_ref, high_ref, low_ref, out_ref, split, lines = rest
     else:
-        halo_ref, out_ref, high_ref, low_ref, split, lines = rest
-    side = side_ref[0]
-    even = side == 0
-    tiles_out = 1 if late else 2
-    rows = tiles_out * TILE_R
+        halo_ref, high_ref, low_ref, middle_ref, near_ref, out_hbm, out_ref, sent, split, lines = rest
+    side = 1 - side_ref[0] if kind == "near" else side_ref[0]
+    top = side == 0
     blocks = cube_ref.shape[2] // BLK
-    parts = []
-    top = pl.multiple_of(2 * side * TILE_R, TILE_R)
-    if late:
-        early = pltpu.make_async_copy(
-            before_ref, out_hbm.at[:, pl.ds(pl.multiple_of((1 - side) * TILE_R, TILE_R), 2 * TILE_R)], sent.at[CHUNKS]
-        )
-        early.start()
-        parts.append(early)
-    else:
+    copies = []
+    if kind == "far":
+        for slot, (ref, tile) in enumerate(((middle_ref, 1), (near_ref, 2 * (1 - side)))):
+            place = out_hbm.at[:, pl.ds(pl.multiple_of(tile * TILE_R, TILE_R), TILE_R)]
+            copies.append(pltpu.make_async_copy(ref, place, sent.at[CHUNKS + slot]))
+            copies[-1].start()
+    if kind == "middle":
         band_matrices(high_ref, low_ref)
-    split[1, :, BLK : BLK + LANES] = jnp.zeros((2 * rows, LANES), jnp.bfloat16)
-    split[1, :, 3 * BLK : 3 * BLK + LANES] = jnp.zeros((2 * rows, LANES), jnp.bfloat16)
-    split[blocks, :, BLK + LANES : 2 * BLK] = jnp.zeros((2 * rows, LANES), jnp.bfloat16)
-    split[blocks, :, 3 * BLK + LANES :] = jnp.zeros((2 * rows, LANES), jnp.bfloat16)
+    edge = jnp.zeros((2 * TILE_R, LANES), jnp.bfloat16)
+    for first in (BLK, 3 * BLK):
+        split[1, :, first : first + LANES] = edge
+        split[blocks, :, first + LANES : first + BLK] = edge
 
     def window(ref, halo, cols):
         tile = lambda index: ref[0, pl.ds(pl.multiple_of(index * TILE_R, TILE_R), TILE_R), cols]
-        if late:
-            middle = tile(1)
-            return [jnp.where(even, halo, middle), tile(2 * side), jnp.where(even, middle, halo)]
-        return [
-            jnp.where(even, tile(0), halo),
-            tile(1 - side),
-            tile(2 - side),
-            jnp.where(even, halo, tile(2)),
-        ]
+        if kind == "middle":
+            return [tile(0), tile(1), tile(2)]
+        centre = tile(1)
+        return [jnp.where(top, halo, centre), tile(2 * side), jnp.where(top, centre, halo)]
 
     def rows_step(block, carry):
         cols = pl.ds(pl.multiple_of(block * BLK, BLK), BLK)
-        cube_halo, weight_halo = halo_ref[0, :, cols], halo_ref[1, :, cols]
-        weights = window(weight_ref, weight_halo, cols)
-        values = window(cube_ref, cube_halo, cols)
-        values = [value * weight for value, weight in zip(values, weights)]
-        sides = []
-        for slot, half in enumerate((0, LANES)):
-            for kind, tiles in enumerate((values, weights)):
-                at = 2 * slot + kind
+        halo = [None, None] if kind == "middle" else [halo_ref[0, :, cols], halo_ref[1, :, cols]]
+        weights = window(weight_ref, halo[1], cols)
+        values = [value * weight for value, weight in zip(window(cube_ref, halo[0], cols), weights)]
+        for half in range(2):
+            for at, tiles in ((2 * half, values), (2 * half + 1, weights)):
                 for i, tile in enumerate(tiles):
-                    lines[at, TILE_R * i : TILE_R * (i + 1)] = tile[:, half : half + LANES]
-        for slot in range(2):
+                    lines[at, TILE_R * i : TILE_R * (i + 1)] = tile[:, half * LANES : (half + 1) * LANES]
+        halves = []
+        for half in range(2):
             made = []
-            for kind in range(2):
-                at = 2 * slot + kind
-                line = lambda start: lines[at, start : start + rows]
+            for at in (2 * half, 2 * half + 1):
+                line = lambda start: lines[at, start : start + TILE_R]
                 total = TAPS[0] * line(RAD)
                 for shift in range(1, RAD + 1):
                     total = total + TAPS[shift] * (line(RAD - shift) + line(RAD + shift))
                 made.append(total)
-            sides.append(jnp.concatenate(made, axis=0))
-        both = jnp.concatenate(sides, axis=1)
+            halves.append(jnp.concatenate(made, axis=0))
+        both = jnp.concatenate(halves, axis=1)
         high = both.astype(jnp.bfloat16)
         low = (both - high.astype(jnp.float32)).astype(jnp.bfloat16)
         for part, base in ((high, 0), (low, 2 * BLK)):
@@ -126,24 +99,25 @@
             split[block, :, base + BLK + LANES : base + 2 * BLK] = part[:, :LANES]
         return carry
 
-    lax.fori_loop(0, blocks, rows_step, 0, unroll=2)
+    lax.fori_loop(0, blocks, rows_step, 0, unroll=UNROLL)
+
     group = blocks // CHUNKS
     for step in range(CHUNKS):
-        part = split[step * group + 1 : (step + 1) * group + 1].reshape(group * 2 * rows, 4 * BLK)
+        part = split[step * group + 1 : (step + 1) * group + 1].reshape(group * 2 * TILE_R, 4 * BLK)
         both = jnp.dot(part[:, : 2 * BLK], high_ref[...], preferred_element_type=jnp.float32)
         both += jnp.dot(part[:, 2 * BLK :], high_ref[...], preferred_element_type=jnp.float32)
         both += jnp.dot(part[:, : 2 * BLK], low_ref[...], preferred_element_type=jnp.float32)
-        both = both.reshape(group, 2 * rows, BLK)
-        ratio = both[:, :rows] / both[:, rows:]
+        both = both.reshape(group, 2 * TILE_R, BLK)
+        ratio = both[:, :TILE_R] / both[:, TILE_R:]
         first = step * (group // 2)
         for i in range(group):
             out_ref[first + i // 2, :, (i % 2) * BLK : (i % 2 + 1) * BLK] = ratio[i]
-        if late:
+        if kind == "far":
             piece = pl.ds(first, group // 2)
-            place = out_hbm.at[piece, pl.ds(top, rows)]
-            parts.append(pltpu.make_async_copy(out_ref.at[piece], place, sent.at[step]))
-            parts[-1].start()
-    for copy in parts:
+            place = out_hbm.at[piece, pl.ds(pl.multiple_of(2 * side * TILE_R, TILE_R), TILE_R)]
+            copies.append(pltpu.make_async_copy(out_ref.at[piece], place, sent.at[step]))
+            copies[-1].start()
+    for copy in copies:
         copy.wait()
 
 
@@ -181,36 +155,41 @@
     )(side, cube, weight)
 
 
-def smooth_rows(side, cube, weight, halo, before=()):
-    late = len(before) > 0
-    rows = TILE_R if late else 2 * TILE_R
+def smooth_rows(kind, side, cube, weight, *rest):
     columns = cube.shape[2]
     tiles = columns // TILE_C
-    blocks = columns // BLK
     whole = pl.BlockSpec(memory_space=pltpu.VMEM)
-    part = pltpu.VMEM((tiles, rows, TILE_C), jnp.float32)
+    part = pltpu.VMEM((tiles, TILE_R, TILE_C), jnp.float32)
     band = pltpu.VMEM((2 * BLK, BLK), jnp.bfloat16)
-    scratch = [
-        pltpu.VMEM((blocks + 2, 2 * rows, 4 * BLK), jnp.bfloat16),
-        pltpu.VMEM((4, rows + 2 * TILE_R, LANES), jnp.float32),
-    ]
-    if late:
-        scratch = [part, pltpu.SemaphoreType.DMA((CHUNKS + 1,))] + scratch
+    out_shape, out_specs, scratch = part, whole, []
+    if kind == "middle":
+        out_shape, out_specs = [part, band, band], [whole] * 3
+    if kind == "far":
+        out_shape = pltpu.HBM((tiles, cube.shape[1], TILE_C), jnp.float32)
+        out_specs = pl.BlockSpec(memory_space=pl.ANY)
+        scratch = [part, pltpu.SemaphoreType.DMA((CHUNKS + 2,))]
     return pl.pallas_call(
-        functools.partial(smooth_kernel, late),
-        out_shape=pltpu.HBM((tiles, cube.shape[1], TILE_C), jnp.float32) if late else [part, band, band],
-        in_specs=[pl.BlockSpec(memory_space=pltpu.SMEM)] + [whole] * (3 + len(before)),
-        out_specs=pl.BlockSpec(memory_space=pl.ANY) if late else [whole] * 3,
-        scratch_shapes=scratch,
+        functools.partial(smooth_kernel, kind),
+        out_shape=out_shape,
+        in_specs=[pl.BlockSpec(memory_space=pltpu.SMEM)] + [whole] * (2 + len(rest)),
+        out_specs=out_specs,
+        scratch_shapes=scratch
+        + [
+            pltpu.VMEM((columns // BLK + 2, 2 * TILE_R, 4 * BLK), jnp.bfloat16),
+            pltpu.VMEM((4, 3 * TILE_R, LANES), jnp.float32),
+        ],
         compiler_params=pltpu.CompilerParams(vmem_limit_bytes=24 * 1024 * 1024),
         cost_estimate=pl.CostEstimate(flops=0, bytes_accessed=0, transcendentals=0),
-    )(side, cube, weight, halo, *before)
+    )(side, cube, weight, *rest)
 
 
 def norm_kernel(smooth_ref, halo_ref, mask_ref, flags_ref, width_ref, out_hbm, out_ref, sent):
     channels, rows, columns = smooth_ref.shape
-    keep_low = [(j >= HW - width_ref[0, 0]).astype(jnp.float32) for j in range(HW)]
-    keep_high = [(j < width_ref[1, 0]).astype(jnp.float32) for j in range(HW)]
+    shape = (TILE_R, LANES)
+    below = jnp.broadcast_to(width_ref[0:1, :], shape)
+    above = jnp.broadcast_to(width_ref[1:2, :], shape)
+    keep_low = [(below >= HW - j).astype(jnp.float32) for j in range(HW)]
+    keep_high = [(above > j).astype(jnp.float32) for j in range(HW)]
 
     def whole(x):
         return jnp.sum(jnp.sum(x, axis=1, keepdims=True), axis=0, keepdims=True)
@@ -240,7 +219,7 @@
                     squares[i] = squares[i] + total * total
             sums = [total + square * keep for total, square in zip(sums, squares)]
         count = jnp.maximum(whole(kept) * channels, 1.0)
-        flag = flags_ref[tile, 0].astype(jnp.float32)
+        flag = flags_ref[tile : tile + 1, :].astype(jnp.float32)
         for i, width in enumerate(WIDTHS):
             factor = flag / (jnp.sqrt(whole(sums[i]) / (count * width**2) + 1e-06) * width)
             factor = jnp.broadcast_to(factor, (TILE_R, columns))
@@ -257,11 +236,10 @@
 def normalize(smoothed, halo, mask, flags, widths):
     out = (len(WIDTHS),) + smoothed.shape
     whole = pl.BlockSpec(memory_space=pltpu.VMEM)
-    scalars = pl.BlockSpec(memory_space=pltpu.SMEM)
     return pl.pallas_call(
         norm_kernel,
         out_shape=jax.ShapeDtypeStruct(out, jnp.float32),
-        in_specs=[whole, whole, whole, scalars, scalars],
+        in_specs=[whole] * 5,
         out_specs=pl.BlockSpec(memory_space=pl.ANY),
         scratch_shapes=[
             pltpu.VMEM(out, jnp.float32),
@@ -285,9 +263,10 @@
     far_edge, near_edge = edge_rows(sides, *stay)
     far_halo = lax.ppermute(far_edge, "sky", far)
     near_halo = lax.ppermute(near_edge, "sky", near)
-    smoothed = smooth_rows(sides, cube, noise_weight, near_halo)
+    middle, *band = smooth_rows("middle", sides, cube, noise_weight)
+    near_part = smooth_rows("near", sides, cube, noise_weight, near_halo, *band)
     far_halo = pltpu.with_memory_space_constraint(far_halo, pltpu.VMEM)
-    smoothed = smooth_rows(sides, cube, noise_weight, far_halo, before=smoothed)
+    smoothed = smooth_rows("far", sides, cube, noise_weight, far_halo, *band, middle, near_part)
     smoothed = lax.all_to_all(smoothed, "chan", split_axis=0, concat_axis=0, tiled=True)
     return normalize(smoothed, spectral_halo, source_mask, tile_flags, halo_width)
 

time: 52.6 us -> 50.9 us (0.968)
  the two profiles are of different devices: /device:TPU:32 before, /device:TPU:1 now
where the time goes in v5:
time: 50.9 us; the launch traced here: 50.2 us
  waiting for transfers between devices  25 us (49%)
  starting transfers between devices  16.5 us (32%)
  Pallas kernels  8.37 us (16%)
    all_to_all x1, waiting for transfers between devices, local(): lax.all_to_all(smoothed, 'chan', split_axis=0, concat_axis=0, tiled=True)  25 us
    all_to_all x1, starting transfers between devices, local(): lax.all_to_all(smoothed, 'chan', split_axis=0, concat_axis=0, tiled=True)  6.98 us
    ppermute x1, starting transfers between devices, local(): far_halo = lax.ppermute(far_edge, 'sky', far)  5.39 us
    pallas_call x3, Pallas kernels, smooth_rows(): pl.pallas_call(functools.partial(smooth_kernel, kind), out_shape=out_shap...  5.02 us
    ppermute x1, starting transfers between devices, local(): near_halo = lax.ppermute(near_edge, 'sky', near)  4.09 us
    pallas_call x1, Pallas kernels, normalize(): pl.pallas_call(norm_kernel, out_shape=jax.ShapeDtypeStruct(out, jnp.float...  2.01 us
    pallas_call x1, Pallas kernels, edge_rows(): pl.pallas_call(edge_kernel, out_shape=edges, in_specs=[pl.BlockSpec(memor...  1.34 us
  transfers between devices with their start and end apart: 3, of which 1 were waited for; matrix products, arithmetic and copies ran while one was open for 0% of the time, Pallas kernels for 6%

profile of v5, /device:TPU:1, one launch (start us, length us, event | category | flops | bytes accessed | tf_op | source)
XLA Modules:
  0.0 50.2 jit_solution(3591480979618299824)
XLA Ops:
  0.0 0.0 copy-start
  0.0 0.0 copy-start.1
  0.0 1.3 %shard_map.64 = (f32[2,8,8320]{2,1,0:T(8,128)S(1)}, f32[2,8,8192]{2,1,0:T(8,128)S(1)}) custom-call(s32[1]{0:T(128)} %bitcast.side_ref, f32[1,24,8192]{2,1,0:T(8,128)} %cube_ref.7, f32[1,24,8192]{2,1,0:T(8,128)} %weight_ref.7), custom_call_target="tpu_custom_call" | custom-call | flops 99999997952 | bytes 4194304 | tf_op jit(solution)/shard_map/pallas_call | solution.py:145
  1.4 5.4 %collective-permute-start = (f32[2,8,8320]{2,1,0:T(8,128)S(1)}, f32[2,8,8320]{2,1,0:T(8,128)S(1)}, u32[]{:S(2)}, u32[]{:S(2)}) collective-permute-start(f32[2,8,8320]{2,1,0:T(8,128)S(1)} %get-tuple-element.10), channel_id=1, source_target_pairs={{16,32},{48,64},{80,96},{112,128},{144,160},{176,192},{208,224},{2... | collective-permute-start | bytes 1597448 | tf_op jit(solution)/shard_map/ppermute | solution.py:264
  6.8 4.1 %collective-permute-start.1 = (f32[2,8,8192]{2,1,0:T(8,128)S(1)}, f32[2,8,8192]{2,1,0:T(8,128)S(1)}, u32[]{:S(2)}, u32[]{:S(2)}) collective-permute-start(f32[2,8,8192]{2,1,0:T(8,128)S(1)} %get-tuple-element.14), channel_id=1, source_target_pairs={{0,16},{16,0},{32,48},{48,32},{64,80},{80,64},{96,112},{112,96},{1... | collective-permute-start | bytes 1572872 | tf_op jit(solution)/shard_map/ppermute | solution.py:265
  10.8 0.0 copy-done
  10.9 0.0 copy-done.1
  10.9 1.6 %shard_map.65 = (f32[16,8,512]{2,1,0:T(8,128)S(1)}, bf16[512,256]{1,0:T(8,128)(2,1)S(1)}, bf16[512,256]{1,0:T(8,128)(2,1)S(1)}) custom-call(s32[1]{0:T(128)} %bitcast.side_ref, f32[1,24,8192]{2,1,0:T(8,128)S(1)} %copy-done, f32[1,24,8192]{2,1,0:T(8,128)S(1)} %copy-done.1), custom_call_target="tpu_custom_call" | custom-call | tf_op jit(solution)/shard_map/pallas_call | solution.py:171
  12.4 0.0 collective-permute-done.1.rest_0_
  12.5 1.4 %shard_map.66.rest_4_ = f32[16,8,512]{2,1,0:T(8,128)S(1)} custom-call(s32[1]{0:T(128)} %bitcast.side_ref, f32[1,24,8192]{2,1,0:T(8,128)S(1)} %copy-done, f32[1,24,8192]{2,1,0:T(8,128)S(1)} %copy-done.1, f32[2,8,8192]{2,1,0:T(8,128)S(1)} %collective-permute-done.1.rest_0_, bf16[512,256]{1,0:T(8,128)(2,1)S(1)} %get-tuple-element.11.rest_1_, ...), custom_call_target="tpu_custom_call" | custom-call | tf_op jit(solution)/shard_map/pallas_call | solution.py:171
  13.8 0.0 collective-permute-done.rest_0_
  13.8 0.0 copy-start.5
  13.9 0.0 copy-start.4
  13.9 0.0 copy-start.2
  13.9 0.0 copy-start.3
  13.9 2.1 %shard_map.67 = f32[16,24,512]{2,1,0:T(8,128)} custom-call(s32[1]{0:T(128)} %bitcast.side_ref, f32[1,24,8192]{2,1,0:T(8,128)S(1)} %copy-done, f32[1,24,8192]{2,1,0:T(8,128)S(1)} %copy-done.1, f32[2,8,8320]{2,1,0:T(8,128)S(1)} %collective-permute-done.rest_0_, bf16[512,256]{1,0:T(8,128)(2,1)S(1)} %get-tuple-element.11.rest_1_, ...), custom_call_target="tpu_custom_call" | custom-call | tf_op jit(solution)/shard_map/pallas_call | solution.py:171
  16.0 7.0 %all-to-all-start = ((f32[16,24,512]{2,1,0:T(8,128)}), f32[16,24,512]{2,1,0:T(8,128)S(1)}, u32[]{:S(2)}, u32[]{:S(2)}) async-start(f32[16,24,512]{2,1,0:T(8,128)} %shard_map.67), calls=%async_computation | async-start | bytes 1572864 | tf_op jit(solution)/shard_map/all_to_all | solution.py:270
  23.0 0.0 copy-done.5
  23.0 0.1 copy.8.width_ref
  23.1 0.0 copy-done.4
  23.1 0.1 copy.7.flags_ref
  23.2 25.0 %all-to-all-done.smooth_ref = f32[16,24,512]{2,1,0:T(8,128)S(1)} async-done(((f32[16,24,512]{2,1,0:T(8,128)}), f32[16,24,512]{2,1,0:T(8,128)S(1)}, u32[]{:S(2)}, u32[]{:S(2)}) %all-to-all-start) | async-done | bytes 786464 | tf_op jit(solution)/shard_map/all_to_all | solution.py:270
  48.2 0.0 copy-done.2
  48.2 0.0 copy-done.3
  48.2 2.0 %shard_map.68 = f32[3,16,24,512]{3,2,1,0:T(8,128)} custom-call(f32[16,24,512]{2,1,0:T(8,128)S(1)} %all-to-all-done.smooth_ref, f32[8,24,512]{2,1,0:T(8,128)S(1)} %copy-done.2, s32[24,512]{1,0:T(8,128)S(1)} %copy-done.3, s32[3,1]{1,0:T(4,128)S(1)} %copy.7.flags_ref, s32[2,1]{1,0:T(2,128)S(1)} %copy.8.width_ref), custom_call_target="tpu_custom_call" | custom-call | flops 5898240 | bytes 3932160 | tf_op jit(solution)/shard_map/pallas_call | solution.py:239
Async XLA Ops:
  0.0 10.9 %copy-start = (f32[1,24,8192]{2,1,0:T(8,128)S(1)}, f32[1,24,8192]{2,1,0:T(8,128)}, u32[]{:S(2)}) copy-start(f32[1,24,8192]{2,1,0:T(8,128)} %cube_ref.7) | copy-start | bytes 2359300
  0.0 10.9 %copy-start.1 = (f32[1,24,8192]{2,1,0:T(8,128)S(1)}, f32[1,24,8192]{2,1,0:T(8,128)}, u32[]{:S(2)}) copy-start(f32[1,24,8192]{2,1,0:T(8,128)} %weight_ref.7) | copy-start | bytes 2359300
  1.4 12.5 %collective-permute-start = (f32[2,8,8320]{2,1,0:T(8,128)S(1)}, f32[2,8,8320]{2,1,0:T(8,128)S(1)}, u32[]{:S(2)}, u32[]{:S(2)}) collective-permute-start(f32[2,8,8320]{2,1,0:T(8,128)S(1)} %get-tuple-element.10), channel_id=1, source_target_pairs={{16,32},{48,64},{80,96},{112,128},{144,160},{176,192},{208,224},{2... | collective-permute-start | bytes 1597448 | tf_op jit(solution)/shard_map/ppermute | solution.py:264
  6.8 5.7 %collective-permute-start.1 = (f32[2,8,8192]{2,1,0:T(8,128)S(1)}, f32[2,8,8192]{2,1,0:T(8,128)S(1)}, u32[]{:S(2)}, u32[]{:S(2)}) collective-permute-start(f32[2,8,8192]{2,1,0:T(8,128)S(1)} %get-tuple-element.14), channel_id=1, source_target_pairs={{0,16},{16,0},{32,48},{48,32},{64,80},{80,64},{96,112},{112,96},{1... | collective-permute-start | bytes 1572872 | tf_op jit(solution)/shard_map/ppermute | solution.py:265
  13.8 9.1 %copy-start.5 = (s32[2,1]{0,1:T(1,128)S(1)}, s32[2,1]{0,1:T(1,128)}, u32[]{:S(2)}) copy-start(s32[2,1]{0,1:T(1,128)} %param.11) | copy-start | bytes 28
  13.9 9.2 %copy-start.4 = (s32[3,1]{0,1:T(1,128)S(1)}, s32[3,1]{0,1:T(1,128)}, u32[]{:S(2)}) copy-start(s32[3,1]{0,1:T(1,128)} %param.10) | copy-start | bytes 40
  13.9 34.3 %copy-start.2 = (f32[8,24,512]{2,1,0:T(8,128)S(1)}, f32[8,24,512]{2,1,0:T(8,128)}, u32[]{:S(2)}) copy-start(f32[8,24,512]{2,1,0:T(8,128)} %halo_ref.1) | copy-start | bytes 1179652
  13.9 34.3 %copy-start.3 = (s32[24,512]{1,0:T(8,128)S(1)}, s32[24,512]{1,0:T(8,128)}, u32[]{:S(2)}) copy-start(s32[24,512]{1,0:T(8,128)} %mask_ref.1) | copy-start | bytes 147460
  16.0 32.2 %all-to-all-start = ((f32[16,24,512]{2,1,0:T(8,128)}), f32[16,24,512]{2,1,0:T(8,128)S(1)}, u32[]{:S(2)}, u32[]{:S(2)}) async-start(f32[16,24,512]{2,1,0:T(8,128)} %shard_map.67), calls=%async_computation | async-start | bytes 1572864 | tf_op jit(solution)/shard_map/all_to_all | solution.py:270

commit v6 on v5

--- a/solution.py
+++ b/solution.py
@@ -16,6 +16,7 @@
 LANES = 128
 CHUNKS = 4
 UNROLL = 4
+SHARE = 2.0**-7
 WIDTHS = (3, 5, 9)
 
 
@@ -74,7 +75,7 @@
     def rows_step(block, carry):
         cols = pl.ds(pl.multiple_of(block * BLK, BLK), BLK)
         halo = [None, None] if kind == "middle" else [halo_ref[0, :, cols], halo_ref[1, :, cols]]
-        weights = window(weight_ref, halo[1], cols)
+        weights = [tile * SHARE for tile in window(weight_ref, halo[1], cols)]
         values = [value * weight for value, weight in zip(window(cube_ref, halo[0], cols), weights)]
         for half in range(2):
             for at, tiles in ((2 * half, values), (2 * half + 1, weights)):
@@ -215,13 +216,14 @@
                     while reach < width // 2:
                         reach += 1
                         total = total + (extended[at - reach] + extended[at + reach])
-                    out_ref[i, c, lines, cols] = total
-                    squares[i] = squares[i] + total * total
+                    boxcar = total * (1.0 / width)
+                    out_ref[i, c, lines, cols] = boxcar
+                    squares[i] = squares[i] + boxcar * boxcar
             sums = [total + square * keep for total, square in zip(sums, squares)]
         count = jnp.maximum(whole(kept) * channels, 1.0)
         flag = flags_ref[tile : tile + 1, :].astype(jnp.float32)
-        for i, width in enumerate(WIDTHS):
-            factor = flag / (jnp.sqrt(whole(sums[i]) / (count * width**2) + 1e-06) * width)
+        for i in range(len(WIDTHS)):
+            factor = flag / jnp.sqrt(whole(sums[i]) / count + 1e-06)
             factor = jnp.broadcast_to(factor, (TILE_R, columns))
             for c in range(channels):
                 out_ref[i, c, lines] = out_ref[i, c, lines] * factor

time: 50.9 us -> 51 us (level)
  no operation moved by 1% of the time
where the time goes in v6:
time: 51 us; the launch traced here: 50.3 us
  waiting for transfers between devices  25.1 us (49%)
  starting transfers between devices  16.4 us (32%)
  Pallas kernels  8.49 us (17%)
    all_to_all x1, waiting for transfers between devices, local(): lax.all_to_all(smoothed, 'chan', split_axis=0, concat_axis=0, tiled=True)  25.1 us
    all_to_all x1, starting transfers between devices, local(): lax.all_to_all(smoothed, 'chan', split_axis=0, concat_axis=0, tiled=True)  6.92 us
    ppermute x1, starting transfers between devices, local(): far_halo = lax.ppermute(far_edge, 'sky', far)  5.39 us
    pallas_call x3, Pallas kernels, smooth_rows(): pl.pallas_call(functools.partial(smooth_kernel, kind), out_shape=out_shap...  5.11 us
    ppermute x1, starting transfers between devices, local(): near_halo = lax.ppermute(near_edge, 'sky', near)  4.09 us
    pallas_call x1, Pallas kernels, normalize(): pl.pallas_call(norm_kernel, out_shape=jax.ShapeDtypeStruct(out, jnp.float...  2.05 us
    pallas_call x1, Pallas kernels, edge_rows(): pl.pallas_call(edge_kernel, out_shape=edges, in_specs=[pl.BlockSpec(memor...  1.34 us
  transfers between devices with their start and end apart: 3, of which 1 were waited for; matrix products, arithmetic and copies ran while one was open for 0% of the time, Pallas kernels for 6%

profile of v6, /device:TPU:1, one launch (start us, length us, event | category | flops | bytes accessed | tf_op | source)
XLA Modules:
  0.0 50.3 jit_solution(17512954400929186657)
XLA Ops:
  0.0 0.0 copy-start
  0.0 0.0 copy-start.1
  0.0 1.3 %shard_map.64 = (f32[2,8,8320]{2,1,0:T(8,128)S(1)}, f32[2,8,8192]{2,1,0:T(8,128)S(1)}) custom-call(s32[1]{0:T(128)} %bitcast.side_ref, f32[1,24,8192]{2,1,0:T(8,128)} %cube_ref.7, f32[1,24,8192]{2,1,0:T(8,128)} %weight_ref.7), custom_call_target="tpu_custom_call" | custom-call | flops 99999997952 | bytes 4194304 | tf_op jit(solution)/shard_map/pallas_call | solution.py:146
  1.4 5.4 %collective-permute-start = (f32[2,8,8320]{2,1,0:T(8,128)S(1)}, f32[2,8,8320]{2,1,0:T(8,128)S(1)}, u32[]{:S(2)}, u32[]{:S(2)}) collective-permute-start(f32[2,8,8320]{2,1,0:T(8,128)S(1)} %get-tuple-element.10), channel_id=1, source_target_pairs={{16,32},{48,64},{80,96},{112,128},{144,160},{176,192},{208,224},{2... | collective-permute-start | bytes 1597448 | tf_op jit(solution)/shard_map/ppermute | solution.py:266
  6.8 4.1 %collective-permute-start.1 = (f32[2,8,8192]{2,1,0:T(8,128)S(1)}, f32[2,8,8192]{2,1,0:T(8,128)S(1)}, u32[]{:S(2)}, u32[]{:S(2)}) collective-permute-start(f32[2,8,8192]{2,1,0:T(8,128)S(1)} %get-tuple-element.14), channel_id=1, source_target_pairs={{0,16},{16,0},{32,48},{48,32},{64,80},{80,64},{96,112},{112,96},{1... | collective-permute-start | bytes 1572872 | tf_op jit(solution)/shard_map/ppermute | solution.py:267
  10.8 0.0 copy-done
  10.9 0.0 copy-done.1
  10.9 1.6 %shard_map.65 = (f32[16,8,512]{2,1,0:T(8,128)S(1)}, bf16[512,256]{1,0:T(8,128)(2,1)S(1)}, bf16[512,256]{1,0:T(8,128)(2,1)S(1)}) custom-call(s32[1]{0:T(128)} %bitcast.side_ref, f32[1,24,8192]{2,1,0:T(8,128)S(1)} %copy-done, f32[1,24,8192]{2,1,0:T(8,128)S(1)} %copy-done.1), custom_call_target="tpu_custom_call" | custom-call | tf_op jit(solution)/shard_map/pallas_call | solution.py:172
  12.5 0.0 collective-permute-done.1.rest_0_
  12.5 1.4 %shard_map.66.rest_4_ = f32[16,8,512]{2,1,0:T(8,128)S(1)} custom-call(s32[1]{0:T(128)} %bitcast.side_ref, f32[1,24,8192]{2,1,0:T(8,128)S(1)} %copy-done, f32[1,24,8192]{2,1,0:T(8,128)S(1)} %copy-done.1, f32[2,8,8192]{2,1,0:T(8,128)S(1)} %collective-permute-done.1.rest_0_, bf16[512,256]{1,0:T(8,128)(2,1)S(1)} %get-tuple-element.11.rest_1_, ...), custom_call_target="tpu_custom_call" | custom-call | tf_op jit(solution)/shard_map/pallas_call | solution.py:172
  13.9 0.0 collective-permute-done.rest_0_
  13.9 0.0 copy-start.5
  13.9 0.0 copy-start.4
  13.9 0.0 copy-start.2
  13.9 0.0 copy-start.3
  13.9 2.1 %shard_map.67 = f32[16,24,512]{2,1,0:T(8,128)} custom-call(s32[1]{0:T(128)} %bitcast.side_ref, f32[1,24,8192]{2,1,0:T(8,128)S(1)} %copy-done, f32[1,24,8192]{2,1,0:T(8,128)S(1)} %copy-done.1, f32[2,8,8320]{2,1,0:T(8,128)S(1)} %collective-permute-done.rest_0_, bf16[512,256]{1,0:T(8,128)(2,1)S(1)} %get-tuple-element.11.rest_1_, ...), custom_call_target="tpu_custom_call" | custom-call | tf_op jit(solution)/shard_map/pallas_call | solution.py:172
  16.1 6.9 %all-to-all-start = ((f32[16,24,512]{2,1,0:T(8,128)}), f32[16,24,512]{2,1,0:T(8,128)S(1)}, u32[]{:S(2)}, u32[]{:S(2)}) async-start(f32[16,24,512]{2,1,0:T(8,128)} %shard_map.67), calls=%async_computation | async-start | bytes 1572864 | tf_op jit(solution)/shard_map/all_to_all | solution.py:272
  23.0 0.0 copy-done.5
  23.0 0.1 copy.8.width_ref
  23.1 0.0 copy-done.4
  23.1 0.1 copy.7.flags_ref
  23.2 25.1 %all-to-all-done.smooth_ref = f32[16,24,512]{2,1,0:T(8,128)S(1)} async-done(((f32[16,24,512]{2,1,0:T(8,128)}), f32[16,24,512]{2,1,0:T(8,128)S(1)}, u32[]{:S(2)}, u32[]{:S(2)}) %all-to-all-start) | async-done | bytes 786464 | tf_op jit(solution)/shard_map/all_to_all | solution.py:272
  48.3 0.0 copy-done.2
  48.3 0.0 copy-done.3
  48.3 2.0 %shard_map.68 = f32[3,16,24,512]{3,2,1,0:T(8,128)} custom-call(f32[16,24,512]{2,1,0:T(8,128)S(1)} %all-to-all-done.smooth_ref, f32[8,24,512]{2,1,0:T(8,128)S(1)} %copy-done.2, s32[24,512]{1,0:T(8,128)S(1)} %copy-done.3, s32[3,1]{1,0:T(4,128)S(1)} %copy.7.flags_ref, s32[2,1]{1,0:T(2,128)S(1)} %copy.8.width_ref), custom_call_target="tpu_custom_call" | custom-call | flops 5898240 | bytes 3932160 | tf_op jit(solution)/shard_map/pallas_call | solution.py:241
Async XLA Ops:
  0.0 10.9 %copy-start = (f32[1,24,8192]{2,1,0:T(8,128)S(1)}, f32[1,24,8192]{2,1,0:T(8,128)}, u32[]{:S(2)}) copy-start(f32[1,24,8192]{2,1,0:T(8,128)} %cube_ref.7) | copy-start | bytes 2359300
  0.0 10.9 %copy-start.1 = (f32[1,24,8192]{2,1,0:T(8,128)S(1)}, f32[1,24,8192]{2,1,0:T(8,128)}, u32[]{:S(2)}) copy-start(f32[1,24,8192]{2,1,0:T(8,128)} %weight_ref.7) | copy-start | bytes 2359300
  1.4 12.5 %collective-permute-start = (f32[2,8,8320]{2,1,0:T(8,128)S(1)}, f32[2,8,8320]{2,1,0:T(8,128)S(1)}, u32[]{:S(2)}, u32[]{:S(2)}) collective-permute-start(f32[2,8,8320]{2,1,0:T(8,128)S(1)} %get-tuple-element.10), channel_id=1, source_target_pairs={{16,32},{48,64},{80,96},{112,128},{144,160},{176,192},{208,224},{2... | collective-permute-start | bytes 1597448 | tf_op jit(solution)/shard_map/ppermute | solution.py:266
  6.8 5.7 %collective-permute-start.1 = (f32[2,8,8192]{2,1,0:T(8,128)S(1)}, f32[2,8,8192]{2,1,0:T(8,128)S(1)}, u32[]{:S(2)}, u32[]{:S(2)}) collective-permute-start(f32[2,8,8192]{2,1,0:T(8,128)S(1)} %get-tuple-element.14), channel_id=1, source_target_pairs={{0,16},{16,0},{32,48},{48,32},{64,80},{80,64},{96,112},{112,96},{1... | collective-permute-start | bytes 1572872 | tf_op jit(solution)/shard_map/ppermute | solution.py:267
  13.9 9.1 %copy-start.5 = (s32[2,1]{0,1:T(1,128)S(1)}, s32[2,1]{0,1:T(1,128)}, u32[]{:S(2)}) copy-start(s32[2,1]{0,1:T(1,128)} %param.11) | copy-start | bytes 28
  13.9 9.2 %copy-start.4 = (s32[3,1]{0,1:T(1,128)S(1)}, s32[3,1]{0,1:T(1,128)}, u32[]{:S(2)}) copy-start(s32[3,1]{0,1:T(1,128)} %param.10) | copy-start | bytes 40
  13.9 34.4 %copy-start.2 = (f32[8,24,512]{2,1,0:T(8,128)S(1)}, f32[8,24,512]{2,1,0:T(8,128)}, u32[]{:S(2)}) copy-start(f32[8,24,512]{2,1,0:T(8,128)} %halo_ref.1) | copy-start | bytes 1179652
  13.9 34.3 %copy-start.3 = (s32[24,512]{1,0:T(8,128)S(1)}, s32[24,512]{1,0:T(8,128)}, u32[]{:S(2)}) copy-start(s32[24,512]{1,0:T(8,128)} %mask_ref.1) | copy-start | bytes 147460
  16.1 32.2 %all-to-all-start = ((f32[16,24,512]{2,1,0:T(8,128)}), f32[16,24,512]{2,1,0:T(8,128)S(1)}, u32[]{:S(2)}, u32[]{:S(2)}) async-start(f32[16,24,512]{2,1,0:T(8,128)} %shard_map.67), calls=%async_computation | async-start | bytes 1572864 | tf_op jit(solution)/shard_map/all_to_all | solution.py:272

commit v7 on v6

--- a/solution.py
+++ b/solution.py
@@ -44,7 +44,7 @@
 
 def smooth_kernel(kind, side_ref, cube_ref, weight_ref, *rest):
     if kind == "middle":
-        out_ref, high_ref, low_ref, split, lines = rest
+        high_ref, low_ref, out_ref, split, lines = rest
     elif kind == "near":
         halo_ref, high_ref, low_ref, out_ref, split, lines = rest
     else:
@@ -58,8 +58,6 @@
             place = out_hbm.at[:, pl.ds(pl.multiple_of(tile * TILE_R, TILE_R), TILE_R)]
             copies.append(pltpu.make_async_copy(ref, place, sent.at[CHUNKS + slot]))
             copies[-1].start()
-    if kind == "middle":
-        band_matrices(high_ref, low_ref)
     edge = jnp.zeros((2 * TILE_R, LANES), jnp.bfloat16)
     for first in (BLK, 3 * BLK):
         split[1, :, first : first + LANES] = edge
@@ -122,7 +120,7 @@
         copy.wait()
 
 
-def edge_kernel(side_ref, cube_ref, weight_ref, far_ref, near_ref, done):
+def edge_kernel(side_ref, cube_ref, weight_ref, far_ref, near_ref, high_ref, low_ref, done):
     side = side_ref[0]
     columns = cube_ref.shape[2]
     last = cube_ref.shape[1] - TILE_R
@@ -135,6 +133,7 @@
     for copy in copies:
         copy.start()
     far_ref[:, :, columns:] = jnp.zeros((2, TILE_R, LANES), jnp.float32)
+    band_matrices(high_ref, low_ref)
     for copy in copies:
         copy.wait()
 
@@ -142,12 +141,13 @@
 def edge_rows(side, cube, weight):
     columns = cube.shape[2]
     edges = [pltpu.VMEM((2, TILE_R, columns + extra), cube.dtype) for extra in (LANES, 0)]
+    band = pltpu.VMEM((2 * BLK, BLK), jnp.bfloat16)
     whole = pl.BlockSpec(memory_space=pltpu.VMEM)
     return pl.pallas_call(
         edge_kernel,
-        out_shape=edges,
+        out_shape=edges + [band, band],
         in_specs=[pl.BlockSpec(memory_space=pltpu.SMEM)] + [pl.BlockSpec(memory_space=pl.ANY)] * 2,
-        out_specs=[whole] * 2,
+        out_specs=[whole] * 4,
         scratch_shapes=[pltpu.SemaphoreType.DMA((4,))],
         compiler_params=pltpu.CompilerParams(vmem_limit_bytes=8 * 1024 * 1024),
         cost_estimate=pl.CostEstimate(
@@ -161,10 +161,7 @@
     tiles = columns // TILE_C
     whole = pl.BlockSpec(memory_space=pltpu.VMEM)
     part = pltpu.VMEM((tiles, TILE_R, TILE_C), jnp.float32)
-    band = pltpu.VMEM((2 * BLK, BLK), jnp.bfloat16)
     out_shape, out_specs, scratch = part, whole, []
-    if kind == "middle":
-        out_shape, out_specs = [part, band, band], [whole] * 3
     if kind == "far":
         out_shape = pltpu.HBM((tiles, cube.shape[1], TILE_C), jnp.float32)
         out_specs = pl.BlockSpec(memory_space=pl.ANY)
@@ -262,10 +259,10 @@
     far = far + [(target, source) for source, target in far]
     sides = jnp.reshape(side, (1,))
     stay = [pltpu.with_memory_space_constraint(part, pltpu.HBM) for part in (cube, noise_weight)]
-    far_edge, near_edge = edge_rows(sides, *stay)
+    far_edge, near_edge, *band = edge_rows(sides, *stay)
     far_halo = lax.ppermute(far_edge, "sky", far)
     near_halo = lax.ppermute(near_edge, "sky", near)
-    middle, *band = smooth_rows("middle", sides, cube, noise_weight)
+    middle = smooth_rows("middle", sides, cube, noise_weight, *band)
     near_part = smooth_rows("near", sides, cube, noise_weight, near_halo, *band)
     far_halo = pltpu.with_memory_space_constraint(far_halo, pltpu.VMEM)
     smoothed = smooth_rows("far", sides, cube, noise_weight, far_halo, *band, middle, near_part)

time: 51 us -> 50.8 us (level)
  transfers between devices with their start and end apart: 3 -> 3, of which waited for: 1 -> 2; matrix products, arithmetic and copies ran while one was open for 0% -> 0% of each run, Pallas kernels for 6% -> 6%
where the time goes in v7:
time: 50.8 us; the launch traced here: 50.2 us
  waiting for transfers between devices  25.1 us (49%)
  starting transfers between devices  16.5 us (32%)
  Pallas kernels  8.27 us (16%)
    all_to_all x1, waiting for transfers between devices, local(): lax.all_to_all(smoothed, 'chan', split_axis=0, concat_axis=0, tiled=True)  25 us
    all_to_all x1, starting transfers between devices, local(): lax.all_to_all(smoothed, 'chan', split_axis=0, concat_axis=0, tiled=True)  7.04 us
    ppermute x1, starting transfers between devices, local(): far_halo = lax.ppermute(far_edge, 'sky', far)  5.39 us
    pallas_call x3, Pallas kernels, smooth_rows(): pl.pallas_call(functools.partial(smooth_kernel, kind), out_shape=out_shap...  4.88 us
    ppermute x1, starting transfers between devices, local(): near_halo = lax.ppermute(near_edge, 'sky', near)  4.09 us
    pallas_call x1, Pallas kernels, normalize(): pl.pallas_call(norm_kernel, out_shape=jax.ShapeDtypeStruct(out, jnp.float...  2.05 us
    pallas_call x1, Pallas kernels, edge_rows(): pl.pallas_call(edge_kernel, out_shape=edges + [band, band], in_specs=[pl....  1.34 us
  transfers between devices with their start and end apart: 3, of which 2 were waited for; matrix products, arithmetic and copies ran while one was open for 0% of the time, Pallas kernels for 6%

profile of v7, /device:TPU:1, one launch (start us, length us, event | category | flops | bytes accessed | tf_op | source)
XLA Modules:
  0.0 50.2 jit_solution(7365826422610129069)
XLA Ops:
  0.0 0.0 copy-start
  0.0 0.0 copy-start.1
  0.0 1.3 %shard_map.64 = (f32[2,8,8320]{2,1,0:T(8,128)S(1)}, f32[2,8,8192]{2,1,0:T(8,128)S(1)}, bf16[512,256]{1,0:T(8,128)(2,1)S(1)}, bf16[512,256]{1,0:T(8,128)(2,1)S(1)}) custom-call(s32[1]{0:T(128)} %bitcast.side_ref, f32[1,24,8192]{2,1,0:T(8,128)} %cube_ref.7, f32[1,24,8192]{2,1,0:T(8,128)} %weight_ref.7), custom_call_target="tpu_custom_call" | custom-call | flops 99999997952 | bytes 4194304 | tf_op jit(solution)/shard_map/pallas_call | solution.py:146
  1.4 5.4 %collective-permute-start = (f32[2,8,8320]{2,1,0:T(8,128)S(1)}, f32[2,8,8320]{2,1,0:T(8,128)S(1)}, u32[]{:S(2)}, u32[]{:S(2)}) collective-permute-start(f32[2,8,8320]{2,1,0:T(8,128)S(1)} %get-tuple-element.9), channel_id=1, source_target_pairs={{16,32},{48,64},{80,96},{112,128},{144,160},{176,192},{208,224},{2... | collective-permute-start | bytes 1597448 | tf_op jit(solution)/shard_map/ppermute | solution.py:263
  6.8 4.1 %collective-permute-start.1 = (f32[2,8,8192]{2,1,0:T(8,128)S(1)}, f32[2,8,8192]{2,1,0:T(8,128)S(1)}, u32[]{:S(2)}, u32[]{:S(2)}) collective-permute-start(f32[2,8,8192]{2,1,0:T(8,128)S(1)} %get-tuple-element.12), channel_id=1, source_target_pairs={{0,16},{16,0},{32,48},{48,32},{64,80},{80,64},{96,112},{112,96},{1... | collective-permute-start | bytes 1572872 | tf_op jit(solution)/shard_map/ppermute | solution.py:264
  10.9 0.0 copy-done
  10.9 0.0 copy-done.1
  10.9 1.4 %shard_map.65.rest_3_ = f32[16,8,512]{2,1,0:T(8,128)S(1)} custom-call(s32[1]{0:T(128)} %bitcast.side_ref, f32[1,24,8192]{2,1,0:T(8,128)S(1)} %copy-done, f32[1,24,8192]{2,1,0:T(8,128)S(1)} %copy-done.1, bf16[512,256]{1,0:T(8,128)(2,1)S(1)} %get-tuple-element.10.rest_0_.rest_1_, bf16[512,256]{1,0:T(8,128)(2,1)S(1)} %get-tuple-element.11.rest_1_.rest_2_), custom_call_target="tpu_custom_call" | custom-call | tf_op jit(solution)/shard_map/pallas_call | solution.py:169
  12.3 0.1 collective-permute-done.1.rest_0_
  12.4 1.4 %shard_map.66.rest_4_ = f32[16,8,512]{2,1,0:T(8,128)S(1)} custom-call(s32[1]{0:T(128)} %bitcast.side_ref, f32[1,24,8192]{2,1,0:T(8,128)S(1)} %copy-done, f32[1,24,8192]{2,1,0:T(8,128)S(1)} %copy-done.1, f32[2,8,8192]{2,1,0:T(8,128)S(1)} %collective-permute-done.1.rest_0_, bf16[512,256]{1,0:T(8,128)(2,1)S(1)} %get-tuple-element.10.rest_0_.rest_1_, ...), custom_call_target="tpu_custom_call" | custom-call | tf_op jit(solution)/shard_map/pallas_call | solution.py:169
  13.8 0.0 copy-start.5
  13.8 0.0 copy-start.4
  13.8 0.0 copy-start.2
  13.8 0.0 copy-start.3
  13.8 0.0 collective-permute-done.rest_0_
  13.8 2.1 %shard_map.67 = f32[16,24,512]{2,1,0:T(8,128)} custom-call(s32[1]{0:T(128)} %bitcast.side_ref, f32[1,24,8192]{2,1,0:T(8,128)S(1)} %copy-done, f32[1,24,8192]{2,1,0:T(8,128)S(1)} %copy-done.1, f32[2,8,8320]{2,1,0:T(8,128)S(1)} %collective-permute-done.rest_0_, bf16[512,256]{1,0:T(8,128)(2,1)S(1)} %get-tuple-element.10.rest_0_.rest_1_, ...), custom_call_target="tpu_custom_call" | custom-call | tf_op jit(solution)/shard_map/pallas_call | solution.py:169
  15.9 7.0 %all-to-all-start = ((f32[16,24,512]{2,1,0:T(8,128)}), f32[16,24,512]{2,1,0:T(8,128)S(1)}, u32[]{:S(2)}, u32[]{:S(2)}) async-start(f32[16,24,512]{2,1,0:T(8,128)} %shard_map.67), calls=%async_computation | async-start | bytes 1572864 | tf_op jit(solution)/shard_map/all_to_all | solution.py:269
  23.0 0.0 copy-done.5
  23.0 0.1 copy.8.width_ref
  23.1 0.0 copy-done.4
  23.1 0.1 copy.7.flags_ref
  23.2 25.0 %all-to-all-done.smooth_ref = f32[16,24,512]{2,1,0:T(8,128)S(1)} async-done(((f32[16,24,512]{2,1,0:T(8,128)}), f32[16,24,512]{2,1,0:T(8,128)S(1)}, u32[]{:S(2)}, u32[]{:S(2)}) %all-to-all-start) | async-done | bytes 786464 | tf_op jit(solution)/shard_map/all_to_all | solution.py:269
  48.1 0.0 copy-done.2
  48.2 0.0 copy-done.3
  48.2 2.0 %shard_map.68 = f32[3,16,24,512]{3,2,1,0:T(8,128)} custom-call(f32[16,24,512]{2,1,0:T(8,128)S(1)} %all-to-all-done.smooth_ref, f32[8,24,512]{2,1,0:T(8,128)S(1)} %copy-done.2, s32[24,512]{1,0:T(8,128)S(1)} %copy-done.3, s32[3,1]{1,0:T(4,128)S(1)} %copy.7.flags_ref, s32[2,1]{1,0:T(2,128)S(1)} %copy.8.width_ref), custom_call_target="tpu_custom_call" | custom-call | flops 5898240 | bytes 3932160 | tf_op jit(solution)/shard_map/pallas_call | solution.py:238
Async XLA Ops:
  0.0 10.9 %copy-start = (f32[1,24,8192]{2,1,0:T(8,128)S(1)}, f32[1,24,8192]{2,1,0:T(8,128)}, u32[]{:S(2)}) copy-start(f32[1,24,8192]{2,1,0:T(8,128)} %cube_ref.7) | copy-start | bytes 2359300
  0.0 10.9 %copy-start.1 = (f32[1,24,8192]{2,1,0:T(8,128)S(1)}, f32[1,24,8192]{2,1,0:T(8,128)}, u32[]{:S(2)}) copy-start(f32[1,24,8192]{2,1,0:T(8,128)} %weight_ref.7) | copy-start | bytes 2359300
  1.4 12.5 %collective-permute-start = (f32[2,8,8320]{2,1,0:T(8,128)S(1)}, f32[2,8,8320]{2,1,0:T(8,128)S(1)}, u32[]{:S(2)}, u32[]{:S(2)}) collective-permute-start(f32[2,8,8320]{2,1,0:T(8,128)S(1)} %get-tuple-element.9), channel_id=1, source_target_pairs={{16,32},{48,64},{80,96},{112,128},{144,160},{176,192},{208,224},{2... | collective-permute-start | bytes 1597448 | tf_op jit(solution)/shard_map/ppermute | solution.py:263
  6.8 5.6 %collective-permute-start.1 = (f32[2,8,8192]{2,1,0:T(8,128)S(1)}, f32[2,8,8192]{2,1,0:T(8,128)S(1)}, u32[]{:S(2)}, u32[]{:S(2)}) collective-permute-start(f32[2,8,8192]{2,1,0:T(8,128)S(1)} %get-tuple-element.12), channel_id=1, source_target_pairs={{0,16},{16,0},{32,48},{48,32},{64,80},{80,64},{96,112},{112,96},{1... | collective-permute-start | bytes 1572872 | tf_op jit(solution)/shard_map/ppermute | solution.py:264
  13.8 9.2 %copy-start.5 = (s32[2,1]{0,1:T(1,128)S(1)}, s32[2,1]{0,1:T(1,128)}, u32[]{:S(2)}) copy-start(s32[2,1]{0,1:T(1,128)} %param.11) | copy-start | bytes 28
  13.8 9.3 %copy-start.4 = (s32[3,1]{0,1:T(1,128)S(1)}, s32[3,1]{0,1:T(1,128)}, u32[]{:S(2)}) copy-start(s32[3,1]{0,1:T(1,128)} %param.10) | copy-start | bytes 40
  13.8 34.4 %copy-start.2 = (f32[8,24,512]{2,1,0:T(8,128)S(1)}, f32[8,24,512]{2,1,0:T(8,128)}, u32[]{:S(2)}) copy-start(f32[8,24,512]{2,1,0:T(8,128)} %halo_ref.1) | copy-start | bytes 1179652
  13.8 34.4 %copy-start.3 = (s32[24,512]{1,0:T(8,128)S(1)}, s32[24,512]{1,0:T(8,128)}, u32[]{:S(2)}) copy-start(s32[24,512]{1,0:T(8,128)} %mask_ref.1) | copy-start | bytes 147460
  15.9 32.2 %all-to-all-start = ((f32[16,24,512]{2,1,0:T(8,128)}), f32[16,24,512]{2,1,0:T(8,128)S(1)}, u32[]{:S(2)}, u32[]{:S(2)}) async-start(f32[16,24,512]{2,1,0:T(8,128)} %shard_map.67), calls=%async_computation | async-start | bytes 1572864 | tf_op jit(solution)/shard_map/all_to_all | solution.py:269

commit v8 on v7

--- a/solution.py
+++ b/solution.py
@@ -15,7 +15,7 @@
 BLK = 256
 LANES = 128
 CHUNKS = 4
-UNROLL = 4
+UNROLL = 8
 SHARE = 2.0**-7
 WIDTHS = (3, 5, 9)
 
@@ -70,7 +70,7 @@
         centre = tile(1)
         return [jnp.where(top, halo, centre), tile(2 * side), jnp.where(top, centre, halo)]
 
-    def rows_step(block, carry):
+    def rows_step(block, slot):
         cols = pl.ds(pl.multiple_of(block * BLK, BLK), BLK)
         halo = [None, None] if kind == "middle" else [halo_ref[0, :, cols], halo_ref[1, :, cols]]
         weights = [tile * SHARE for tile in window(weight_ref, halo[1], cols)]
@@ -78,12 +78,12 @@
         for half in range(2):
             for at, tiles in ((2 * half, values), (2 * half + 1, weights)):
                 for i, tile in enumerate(tiles):
-                    lines[at, TILE_R * i : TILE_R * (i + 1)] = tile[:, half * LANES : (half + 1) * LANES]
+                    lines[4 * slot + at, TILE_R * i : TILE_R * (i + 1)] = tile[:, half * LANES : (half + 1) * LANES]
         halves = []
         for half in range(2):
             made = []
             for at in (2 * half, 2 * half + 1):
-                line = lambda start: lines[at, start : start + TILE_R]
+                line = lambda start: lines[4 * slot + at, start : start + TILE_R]
                 total = TAPS[0] * line(RAD)
                 for shift in range(1, RAD + 1):
                     total = total + TAPS[shift] * (line(RAD - shift) + line(RAD + shift))
@@ -96,9 +96,13 @@
             split[block + 1, :, base : base + BLK] = part
             split[block + 2, :, base + BLK : base + BLK + LANES] = part[:, LANES:]
             split[block, :, base + BLK + LANES : base + 2 * BLK] = part[:, :LANES]
+
+    def rows_steps(step, carry):
+        for slot in range(UNROLL):
+            rows_step(step * UNROLL + slot, slot)
         return carry
 
-    lax.fori_loop(0, blocks, rows_step, 0, unroll=UNROLL)
+    lax.fori_loop(0, blocks // UNROLL, rows_steps, 0)
 
     group = blocks // CHUNKS
     for step in range(CHUNKS):
@@ -174,7 +178,7 @@
         scratch_shapes=scratch
         + [
             pltpu.VMEM((columns // BLK + 2, 2 * TILE_R, 4 * BLK), jnp.bfloat16),
-            pltpu.VMEM((4, 3 * TILE_R, LANES), jnp.float32),
+            pltpu.VMEM((4 * UNROLL, 3 * TILE_R, LANES), jnp.float32),
         ],
         compiler_params=pltpu.CompilerParams(vmem_limit_bytes=24 * 1024 * 1024),
         cost_estimate=pl.CostEstimate(flops=0, bytes_accessed=0, transcendentals=0),
@@ -205,14 +209,12 @@
             extended += [smooth_ref[c, lines, cols] for c in range(channels)]
             extended += [halo_ref[HW + j, lines, cols] * keep_high[j] for j in range(HW)]
             squares = [jnp.zeros((TILE_R, LANES), jnp.float32) for _ in WIDTHS]
+            threes = [a + b + c for a, b, c in zip(extended, extended[1:], extended[2:])]
             for c in range(channels):
-                at = c + HW
-                total = extended[at]
-                reach = 0
-                for i, width in enumerate(WIDTHS):
-                    while reach < width // 2:
-                        reach += 1
-                        total = total + (extended[at - reach] + extended[at + reach])
+                three = threes[c + HW - 1]
+                five = three + (extended[c + HW - 2] + extended[c + HW + 2])
+                nine = three + (threes[c + HW - 4] + threes[c + HW + 2])
+                for i, (total, width) in enumerate(zip((three, five, nine), WIDTHS)):
                     boxcar = total * (1.0 / width)
                     out_ref[i, c, lines, cols] = boxcar
                     squares[i] = squares[i] + boxcar * boxcar

time: 50.8 us -> 50.7 us (level)
  transfers between devices with their start and end apart: 3 -> 3, of which waited for: 2 -> 2; matrix products, arithmetic and copies ran while one was open for 0% -> 0% of each run, Pallas kernels for 6% -> 5%
where the time goes in v8:
time: 50.7 us; the launch traced here: 50.1 us
  waiting for transfers between devices  25.1 us (50%)
  starting transfers between devices  16.6 us (33%)
  Pallas kernels  8.09 us (16%)
    all_to_all x1, waiting for transfers between devices, local(): lax.all_to_all(smoothed, 'chan', split_axis=0, concat_axis=0, tiled=True)  24.9 us
    all_to_all x1, starting transfers between devices, local(): lax.all_to_all(smoothed, 'chan', split_axis=0, concat_axis=0, tiled=True)  7.09 us
    ppermute x1, starting transfers between devices, local(): far_halo = lax.ppermute(far_edge, 'sky', far)  5.39 us
    pallas_call x3, Pallas kernels, smooth_rows(): pl.pallas_call(functools.partial(smooth_kernel, kind), out_shape=out_shap...  4.74 us
    ppermute x1, starting transfers between devices, local(): near_halo = lax.ppermute(near_edge, 'sky', near)  4.09 us
    pallas_call x1, Pallas kernels, normalize(): pl.pallas_call(norm_kernel, out_shape=jax.ShapeDtypeStruct(out, jnp.float...  2.01 us
    pallas_call x1, Pallas kernels, edge_rows(): pl.pallas_call(edge_kernel, out_shape=edges + [band, band], in_specs=[pl....  1.34 us
  transfers between devices with their start and end apart: 3, of which 2 were waited for; matrix products, arithmetic and copies ran while one was open for 0% of the time, Pallas kernels for 5%

profile of v8, /device:TPU:1, one launch (start us, length us, event | category | flops | bytes accessed | tf_op | source)
XLA Modules:
  0.0 50.1 jit_solution(7339088052573286976)
XLA Ops:
  0.0 0.0 copy-start
  0.0 0.0 copy-start.1
  0.0 1.3 %shard_map.64 = (f32[2,8,8320]{2,1,0:T(8,128)S(1)}, f32[2,8,8192]{2,1,0:T(8,128)S(1)}, bf16[512,256]{1,0:T(8,128)(2,1)S(1)}, bf16[512,256]{1,0:T(8,128)(2,1)S(1)}) custom-call(s32[1]{0:T(128)} %bitcast.side_ref, f32[1,24,8192]{2,1,0:T(8,128)} %cube_ref.7, f32[1,24,8192]{2,1,0:T(8,128)} %weight_ref.7), custom_call_target="tpu_custom_call" | custom-call | flops 99999997952 | bytes 4194304 | tf_op jit(solution)/shard_map/pallas_call | solution.py:150
  1.4 5.4 %collective-permute-start = (f32[2,8,8320]{2,1,0:T(8,128)S(1)}, f32[2,8,8320]{2,1,0:T(8,128)S(1)}, u32[]{:S(2)}, u32[]{:S(2)}) collective-permute-start(f32[2,8,8320]{2,1,0:T(8,128)S(1)} %get-tuple-element.9), channel_id=1, source_target_pairs={{16,32},{48,64},{80,96},{112,128},{144,160},{176,192},{208,224},{2... | collective-permute-start | bytes 1597448 | tf_op jit(solution)/shard_map/ppermute | solution.py:265
  6.8 4.1 %collective-permute-start.1 = (f32[2,8,8192]{2,1,0:T(8,128)S(1)}, f32[2,8,8192]{2,1,0:T(8,128)S(1)}, u32[]{:S(2)}, u32[]{:S(2)}) collective-permute-start(f32[2,8,8192]{2,1,0:T(8,128)S(1)} %get-tuple-element.12), channel_id=1, source_target_pairs={{0,16},{16,0},{32,48},{48,32},{64,80},{80,64},{96,112},{112,96},{1... | collective-permute-start | bytes 1572872 | tf_op jit(solution)/shard_map/ppermute | solution.py:266
  10.9 0.0 copy-done
  10.9 0.0 copy-done.1
  10.9 1.3 %shard_map.65.rest_3_ = f32[16,8,512]{2,1,0:T(8,128)S(1)} custom-call(s32[1]{0:T(128)} %bitcast.side_ref, f32[1,24,8192]{2,1,0:T(8,128)S(1)} %copy-done, f32[1,24,8192]{2,1,0:T(8,128)S(1)} %copy-done.1, bf16[512,256]{1,0:T(8,128)(2,1)S(1)} %get-tuple-element.10.rest_0_.rest_1_, bf16[512,256]{1,0:T(8,128)(2,1)S(1)} %get-tuple-element.11.rest_1_.rest_2_), custom_call_target="tpu_custom_call" | custom-call | tf_op jit(solution)/shard_map/pallas_call | solution.py:173
  12.2 0.2 collective-permute-done.1.rest_0_
  12.4 1.3 %shard_map.66.rest_4_ = f32[16,8,512]{2,1,0:T(8,128)S(1)} custom-call(s32[1]{0:T(128)} %bitcast.side_ref, f32[1,24,8192]{2,1,0:T(8,128)S(1)} %copy-done, f32[1,24,8192]{2,1,0:T(8,128)S(1)} %copy-done.1, f32[2,8,8192]{2,1,0:T(8,128)S(1)} %collective-permute-done.1.rest_0_, bf16[512,256]{1,0:T(8,128)(2,1)S(1)} %get-tuple-element.10.rest_0_.rest_1_, ...), custom_call_target="tpu_custom_call" | custom-call | tf_op jit(solution)/shard_map/pallas_call | solution.py:173
  13.7 0.0 copy-start.5
  13.7 0.0 copy-start.4
  13.7 0.0 copy-start.2
  13.7 0.0 copy-start.3
  13.8 0.0 collective-permute-done.rest_0_
  13.8 2.1 %shard_map.67 = f32[16,24,512]{2,1,0:T(8,128)} custom-call(s32[1]{0:T(128)} %bitcast.side_ref, f32[1,24,8192]{2,1,0:T(8,128)S(1)} %copy-done, f32[1,24,8192]{2,1,0:T(8,128)S(1)} %copy-done.1, f32[2,8,8320]{2,1,0:T(8,128)S(1)} %collective-permute-done.rest_0_, bf16[512,256]{1,0:T(8,128)(2,1)S(1)} %get-tuple-element.10.rest_0_.rest_1_, ...), custom_call_target="tpu_custom_call" | custom-call | tf_op jit(solution)/shard_map/pallas_call | solution.py:173
  15.9 7.1 %all-to-all-start = ((f32[16,24,512]{2,1,0:T(8,128)}), f32[16,24,512]{2,1,0:T(8,128)S(1)}, u32[]{:S(2)}, u32[]{:S(2)}) async-start(f32[16,24,512]{2,1,0:T(8,128)} %shard_map.67), calls=%async_computation | async-start | bytes 1572864 | tf_op jit(solution)/shard_map/all_to_all | solution.py:271
  23.0 0.0 copy-done.5
  23.0 0.1 copy.8.width_ref
  23.1 0.0 copy-done.4
  23.1 0.1 copy.7.flags_ref
  23.1 24.9 %all-to-all-done.smooth_ref = f32[16,24,512]{2,1,0:T(8,128)S(1)} async-done(((f32[16,24,512]{2,1,0:T(8,128)}), f32[16,24,512]{2,1,0:T(8,128)S(1)}, u32[]{:S(2)}, u32[]{:S(2)}) %all-to-all-start) | async-done | bytes 786464 | tf_op jit(solution)/shard_map/all_to_all | solution.py:271
  48.1 0.0 copy-done.2
  48.1 0.0 copy-done.3
  48.1 2.0 %shard_map.68 = f32[3,16,24,512]{3,2,1,0:T(8,128)} custom-call(f32[16,24,512]{2,1,0:T(8,128)S(1)} %all-to-all-done.smooth_ref, f32[8,24,512]{2,1,0:T(8,128)S(1)} %copy-done.2, s32[24,512]{1,0:T(8,128)S(1)} %copy-done.3, s32[3,1]{1,0:T(4,128)S(1)} %copy.7.flags_ref, s32[2,1]{1,0:T(2,128)S(1)} %copy.8.width_ref), custom_call_target="tpu_custom_call" | custom-call | flops 5898240 | bytes 3932160 | tf_op jit(solution)/shard_map/pallas_call | solution.py:240
Async XLA Ops:
  0.0 10.9 %copy-start = (f32[1,24,8192]{2,1,0:T(8,128)S(1)}, f32[1,24,8192]{2,1,0:T(8,128)}, u32[]{:S(2)}) copy-start(f32[1,24,8192]{2,1,0:T(8,128)} %cube_ref.7) | copy-start | bytes 2359300
  0.0 10.9 %copy-start.1 = (f32[1,24,8192]{2,1,0:T(8,128)S(1)}, f32[1,24,8192]{2,1,0:T(8,128)}, u32[]{:S(2)}) copy-start(f32[1,24,8192]{2,1,0:T(8,128)} %weight_ref.7) | copy-start | bytes 2359300
  1.4 12.4 %collective-permute-start = (f32[2,8,8320]{2,1,0:T(8,128)S(1)}, f32[2,8,8320]{2,1,0:T(8,128)S(1)}, u32[]{:S(2)}, u32[]{:S(2)}) collective-permute-start(f32[2,8,8320]{2,1,0:T(8,128)S(1)} %get-tuple-element.9), channel_id=1, source_target_pairs={{16,32},{48,64},{80,96},{112,128},{144,160},{176,192},{208,224},{2... | collective-permute-start | bytes 1597448 | tf_op jit(solution)/shard_map/ppermute | solution.py:265
  6.8 5.6 %collective-permute-start.1 = (f32[2,8,8192]{2,1,0:T(8,128)S(1)}, f32[2,8,8192]{2,1,0:T(8,128)S(1)}, u32[]{:S(2)}, u32[]{:S(2)}) collective-permute-start(f32[2,8,8192]{2,1,0:T(8,128)S(1)} %get-tuple-element.12), channel_id=1, source_target_pairs={{0,16},{16,0},{32,48},{48,32},{64,80},{80,64},{96,112},{112,96},{1... | collective-permute-start | bytes 1572872 | tf_op jit(solution)/shard_map/ppermute | solution.py:266
  13.7 9.2 %copy-start.5 = (s32[2,1]{0,1:T(1,128)S(1)}, s32[2,1]{0,1:T(1,128)}, u32[]{:S(2)}) copy-start(s32[2,1]{0,1:T(1,128)} %param.11) | copy-start | bytes 28
  13.7 9.3 %copy-start.4 = (s32[3,1]{0,1:T(1,128)S(1)}, s32[3,1]{0,1:T(1,128)}, u32[]{:S(2)}) copy-start(s32[3,1]{0,1:T(1,128)} %param.10) | copy-start | bytes 40
  13.7 34.3 %copy-start.2 = (f32[8,24,512]{2,1,0:T(8,128)S(1)}, f32[8,24,512]{2,1,0:T(8,128)}, u32[]{:S(2)}) copy-start(f32[8,24,512]{2,1,0:T(8,128)} %halo_ref.1) | copy-start | bytes 1179652
  13.7 34.3 %copy-start.3 = (s32[24,512]{1,0:T(8,128)S(1)}, s32[24,512]{1,0:T(8,128)}, u32[]{:S(2)}) copy-start(s32[24,512]{1,0:T(8,128)} %mask_ref.1) | copy-start | bytes 147460
  15.9 32.2 %all-to-all-start = ((f32[16,24,512]{2,1,0:T(8,128)}), f32[16,24,512]{2,1,0:T(8,128)S(1)}, u32[]{:S(2)}, u32[]{:S(2)}) async-start(f32[16,24,512]{2,1,0:T(8,128)} %shard_map.67), calls=%async_computation | async-start | bytes 1572864 | tf_op jit(solution)/shard_map/all_to_all | solution.py:271

commit v9 on v8

--- a/solution.py
+++ b/solution.py
@@ -42,14 +42,15 @@
         low_ref[rows] = (band - high.astype(jnp.float32)).astype(jnp.bfloat16)
 
 
-def smooth_kernel(kind, side_ref, cube_ref, weight_ref, *rest):
+def smooth_kernel(kind, cube_ref, weight_ref, *rest):
     if kind == "middle":
         high_ref, low_ref, out_ref, split, lines = rest
     elif kind == "near":
         halo_ref, high_ref, low_ref, out_ref, split, lines = rest
     else:
         halo_ref, high_ref, low_ref, middle_ref, near_ref, out_hbm, out_ref, sent, split, lines = rest
-    side = 1 - side_ref[0] if kind == "near" else side_ref[0]
+    side = lax.axis_index("sky") & 1
+    side = 1 - side if kind == "near" else side
     top = side == 0
     blocks = cube_ref.shape[2] // BLK
     copies = []
@@ -124,8 +125,8 @@
         copy.wait()
 
 
-def edge_kernel(side_ref, cube_ref, weight_ref, far_ref, near_ref, high_ref, low_ref, done):
-    side = side_ref[0]
+def edge_kernel(cube_ref, weight_ref, far_ref, near_ref, high_ref, low_ref, done):
+    side = lax.axis_index("sky") & 1
     columns = cube_ref.shape[2]
     last = cube_ref.shape[1] - TILE_R
     copies = []
@@ -142,7 +143,7 @@
         copy.wait()
 
 
-def edge_rows(side, cube, weight):
+def edge_rows(cube, weight):
     columns = cube.shape[2]
     edges = [pltpu.VMEM((2, TILE_R, columns + extra), cube.dtype) for extra in (LANES, 0)]
     band = pltpu.VMEM((2 * BLK, BLK), jnp.bfloat16)
@@ -150,17 +151,17 @@
     return pl.pallas_call(
         edge_kernel,
         out_shape=edges + [band, band],
-        in_specs=[pl.BlockSpec(memory_space=pltpu.SMEM)] + [pl.BlockSpec(memory_space=pl.ANY)] * 2,
+        in_specs=[pl.BlockSpec(memory_space=pl.ANY)] * 2,
         out_specs=[whole] * 4,
         scratch_shapes=[pltpu.SemaphoreType.DMA((4,))],
         compiler_params=pltpu.CompilerParams(vmem_limit_bytes=8 * 1024 * 1024),
         cost_estimate=pl.CostEstimate(
             flops=10**11, bytes_accessed=64 * TILE_R * columns, transcendentals=0
         ),
-    )(side, cube, weight)
-
-
-def smooth_rows(kind, side, cube, weight, *rest):
+    )(cube, weight)
+
+
+def smooth_rows(kind, cube, weight, *rest):
     columns = cube.shape[2]
     tiles = columns // TILE_C
     whole = pl.BlockSpec(memory_space=pltpu.VMEM)
@@ -173,7 +174,7 @@
     return pl.pallas_call(
         functools.partial(smooth_kernel, kind),
         out_shape=out_shape,
-        in_specs=[pl.BlockSpec(memory_space=pltpu.SMEM)] + [whole] * (2 + len(rest)),
+        in_specs=[whole] * (2 + len(rest)),
         out_specs=out_specs,
         scratch_shapes=scratch
         + [
@@ -182,7 +183,7 @@
         ],
         compiler_params=pltpu.CompilerParams(vmem_limit_bytes=24 * 1024 * 1024),
         cost_estimate=pl.CostEstimate(flops=0, bytes_accessed=0, transcendentals=0),
-    )(side, cube, weight, *rest)
+    )(cube, weight, *rest)
 
 
 def norm_kernel(smooth_ref, halo_ref, mask_ref, flags_ref, width_ref, out_hbm, out_ref, sent):
@@ -255,19 +256,17 @@
 
 def local(cube, noise_weight, spectral_halo, source_mask, tile_flags, halo_width):
     sky = lax.axis_size("sky")
-    side = lax.axis_index("sky") & 1
     near = [(i, i ^ 1) for i in range(sky)]
     far = [(i, i + 1) for i in range(1, sky - 1, 2)]
     far = far + [(target, source) for source, target in far]
-    sides = jnp.reshape(side, (1,))
     stay = [pltpu.with_memory_space_constraint(part, pltpu.HBM) for part in (cube, noise_weight)]
-    far_edge, near_edge, *band = edge_rows(sides, *stay)
+    far_edge, near_edge, *band = edge_rows(*stay)
     far_halo = lax.ppermute(far_edge, "sky", far)
     near_halo = lax.ppermute(near_edge, "sky", near)
-    middle = smooth_rows("middle", sides, cube, noise_weight, *band)
-    near_part = smooth_rows("near", sides, cube, noise_weight, near_halo, *band)
+    middle = smooth_rows("middle", cube, noise_weight, *band)
+    near_part = smooth_rows("near", cube, noise_weight, near_halo, *band)
     far_halo = pltpu.with_memory_space_constraint(far_halo, pltpu.VMEM)
-    smoothed = smooth_rows("far", sides, cube, noise_weight, far_halo, *band, middle, near_part)
+    smoothed = smooth_rows("far", cube, noise_weight, far_halo, *band, middle, near_part)
     smoothed = lax.all_to_all(smoothed, "chan", split_axis=0, concat_axis=0, tiled=True)
     return normalize(smoothed, spectral_halo, source_mask, tile_flags, halo_width)
 

time: 50.7 us -> 50.8 us (level)
  no operation moved by 1% of the time
where the time goes in v9:
time: 50.8 us; the launch traced here: 50.1 us
  waiting for transfers between devices  25.1 us (49%)
  starting transfers between devices  16.5 us (32%)
  Pallas kernels  8.12 us (16%)
    all_to_all x1, waiting for transfers between devices, local(): lax.all_to_all(smoothed, 'chan', split_axis=0, concat_axis=0, tiled=True)  24.9 us
    all_to_all x1, starting transfers between devices, local(): lax.all_to_all(smoothed, 'chan', split_axis=0, concat_axis=0, tiled=True)  7.06 us
    ppermute x1, starting transfers between devices, local(): far_halo = lax.ppermute(far_edge, 'sky', far)  5.39 us
    pallas_call x3, Pallas kernels, smooth_rows(): pl.pallas_call(functools.partial(smooth_kernel, kind), out_shape=out_shap...  4.77 us
    ppermute x1, starting transfers between devices, local(): near_halo = lax.ppermute(near_edge, 'sky', near)  4.09 us
    pallas_call x1, Pallas kernels, normalize(): pl.pallas_call(norm_kernel, out_shape=jax.ShapeDtypeStruct(out, jnp.float...  2.01 us
    pallas_call x1, Pallas kernels, edge_rows(): pl.pallas_call(edge_kernel, out_shape=edges + [band, band], in_specs=[pl....  1.35 us
  transfers between devices with their start and end apart: 3, of which 2 were waited for; matrix products, arithmetic and copies ran while one was open for 0% of the time, Pallas kernels for 5%

profile of v9, /device:TPU:1, one launch (start us, length us, event | category | flops | bytes accessed | tf_op | source)
XLA Modules:
  0.0 50.1 jit_solution(11418603222311770859)
XLA Ops:
  0.0 0.0 copy-start.1
  0.0 0.0 copy-start
  0.0 1.3 %shard_map.64 = (f32[2,8,8320]{2,1,0:T(8,128)S(1)}, f32[2,8,8192]{2,1,0:T(8,128)S(1)}, bf16[512,256]{1,0:T(8,128)(2,1)S(1)}, bf16[512,256]{1,0:T(8,128)(2,1)S(1)}) custom-call(f32[1,24,8192]{2,1,0:T(8,128)} %cube_ref.7, f32[1,24,8192]{2,1,0:T(8,128)} %weight_ref.7), custom_call_target="tpu_custom_call" | custom-call | flops 99999997952 | bytes 4194304 | tf_op jit(solution)/shard_map/pallas_call | solution.py:151
  1.4 5.4 %collective-permute-start = (f32[2,8,8320]{2,1,0:T(8,128)S(1)}, f32[2,8,8320]{2,1,0:T(8,128)S(1)}, u32[]{:S(2)}, u32[]{:S(2)}) collective-permute-start(f32[2,8,8320]{2,1,0:T(8,128)S(1)} %get-tuple-element.9), channel_id=1, source_target_pairs={{16,32},{48,64},{80,96},{112,128},{144,160},{176,192},{208,224},{2... | collective-permute-start | bytes 1597448 | tf_op jit(solution)/shard_map/ppermute | solution.py:264
  6.8 4.1 %collective-permute-start.1 = (f32[2,8,8192]{2,1,0:T(8,128)S(1)}, f32[2,8,8192]{2,1,0:T(8,128)S(1)}, u32[]{:S(2)}, u32[]{:S(2)}) collective-permute-start(f32[2,8,8192]{2,1,0:T(8,128)S(1)} %get-tuple-element.12), channel_id=1, source_target_pairs={{0,16},{16,0},{32,48},{48,32},{64,80},{80,64},{96,112},{112,96},{1... | collective-permute-start | bytes 1572872 | tf_op jit(solution)/shard_map/ppermute | solution.py:265
  10.9 0.0 copy-done.1
  10.9 0.0 copy-done
  10.9 1.3 %shard_map.65.rest_3_ = f32[16,8,512]{2,1,0:T(8,128)S(1)} custom-call(f32[1,24,8192]{2,1,0:T(8,128)S(1)} %copy-done, f32[1,24,8192]{2,1,0:T(8,128)S(1)} %copy-done.1, bf16[512,256]{1,0:T(8,128)(2,1)S(1)} %get-tuple-element.10.rest_0_.rest_1_, bf16[512,256]{1,0:T(8,128)(2,1)S(1)} %get-tuple-element.11.rest_1_.rest_2_), custom_call_target="tpu_custom_call" | custom-call | tf_op jit(solution)/shard_map/pallas_call | solution.py:174
  12.2 0.2 collective-permute-done.1.rest_0_
  12.4 1.4 %shard_map.66.rest_4_ = f32[16,8,512]{2,1,0:T(8,128)S(1)} custom-call(f32[1,24,8192]{2,1,0:T(8,128)S(1)} %copy-done, f32[1,24,8192]{2,1,0:T(8,128)S(1)} %copy-done.1, f32[2,8,8192]{2,1,0:T(8,128)S(1)} %collective-permute-done.1.rest_0_, bf16[512,256]{1,0:T(8,128)(2,1)S(1)} %get-tuple-element.10.rest_0_.rest_1_, ...), custom_call_target="tpu_custom_call" | custom-call | tf_op jit(solution)/shard_map/pallas_call | solution.py:174
  13.7 0.0 copy-start.5
  13.7 0.0 copy-start.4
  13.8 0.0 copy-start.2
  13.8 0.0 copy-start.3
  13.8 0.0 collective-permute-done.rest_0_
  13.8 2.1 %shard_map.67 = f32[16,24,512]{2,1,0:T(8,128)} custom-call(f32[1,24,8192]{2,1,0:T(8,128)S(1)} %copy-done, f32[1,24,8192]{2,1,0:T(8,128)S(1)} %copy-done.1, f32[2,8,8320]{2,1,0:T(8,128)S(1)} %collective-permute-done.rest_0_, bf16[512,256]{1,0:T(8,128)(2,1)S(1)} %get-tuple-element.10.rest_0_.rest_1_, bf16[512,256]{1,0:T(8,128)(2,1)S(1)} %get-tuple-element.11.rest_1_.rest_2_, ...), custom_call_target="tpu_custom_call" | custom-call | tf_op jit(solution)/shard_map/pallas_call | solution.py:174
  15.9 7.1 %all-to-all-start = ((f32[16,24,512]{2,1,0:T(8,128)}), f32[16,24,512]{2,1,0:T(8,128)S(1)}, u32[]{:S(2)}, u32[]{:S(2)}) async-start(f32[16,24,512]{2,1,0:T(8,128)} %shard_map.67), calls=%async_computation | async-start | bytes 1572864 | tf_op jit(solution)/shard_map/all_to_all | solution.py:270
  23.0 0.0 copy-done.5
  23.0 0.1 copy.8.width_ref
  23.1 0.0 copy-done.4
  23.1 0.1 copy.7.flags_ref
  23.2 24.9 %all-to-all-done.smooth_ref = f32[16,24,512]{2,1,0:T(8,128)S(1)} async-done(((f32[16,24,512]{2,1,0:T(8,128)}), f32[16,24,512]{2,1,0:T(8,128)S(1)}, u32[]{:S(2)}, u32[]{:S(2)}) %all-to-all-start) | async-done | bytes 786464 | tf_op jit(solution)/shard_map/all_to_all | solution.py:270
  48.1 0.0 copy-done.2
  48.1 0.0 copy-done.3
  48.1 2.0 %shard_map.68 = f32[3,16,24,512]{3,2,1,0:T(8,128)} custom-call(f32[16,24,512]{2,1,0:T(8,128)S(1)} %all-to-all-done.smooth_ref, f32[8,24,512]{2,1,0:T(8,128)S(1)} %copy-done.2, s32[24,512]{1,0:T(8,128)S(1)} %copy-done.3, s32[3,1]{1,0:T(4,128)S(1)} %copy.7.flags_ref, s32[2,1]{1,0:T(2,128)S(1)} %copy.8.width_ref), custom_call_target="tpu_custom_call" | custom-call | flops 5898240 | bytes 3932160 | tf_op jit(solution)/shard_map/pallas_call | solution.py:241
Async XLA Ops:
  0.0 10.9 %copy-start.1 = (f32[1,24,8192]{2,1,0:T(8,128)S(1)}, f32[1,24,8192]{2,1,0:T(8,128)}, u32[]{:S(2)}) copy-start(f32[1,24,8192]{2,1,0:T(8,128)} %weight_ref.7) | copy-start | bytes 2359300
  0.0 10.9 %copy-start = (f32[1,24,8192]{2,1,0:T(8,128)S(1)}, f32[1,24,8192]{2,1,0:T(8,128)}, u32[]{:S(2)}) copy-start(f32[1,24,8192]{2,1,0:T(8,128)} %cube_ref.7) | copy-start | bytes 2359300
  1.4 12.4 %collective-permute-start = (f32[2,8,8320]{2,1,0:T(8,128)S(1)}, f32[2,8,8320]{2,1,0:T(8,128)S(1)}, u32[]{:S(2)}, u32[]{:S(2)}) collective-permute-start(f32[2,8,8320]{2,1,0:T(8,128)S(1)} %get-tuple-element.9), channel_id=1, source_target_pairs={{16,32},{48,64},{80,96},{112,128},{144,160},{176,192},{208,224},{2... | collective-permute-start | bytes 1597448 | tf_op jit(solution)/shard_map/ppermute | solution.py:264
  6.8 5.6 %collective-permute-start.1 = (f32[2,8,8192]{2,1,0:T(8,128)S(1)}, f32[2,8,8192]{2,1,0:T(8,128)S(1)}, u32[]{:S(2)}, u32[]{:S(2)}) collective-permute-start(f32[2,8,8192]{2,1,0:T(8,128)S(1)} %get-tuple-element.12), channel_id=1, source_target_pairs={{0,16},{16,0},{32,48},{48,32},{64,80},{80,64},{96,112},{112,96},{1... | collective-permute-start | bytes 1572872 | tf_op jit(solution)/shard_map/ppermute | solution.py:265
  13.7 9.2 %copy-start.5 = (s32[2,1]{0,1:T(1,128)S(1)}, s32[2,1]{0,1:T(1,128)}, u32[]{:S(2)}) copy-start(s32[2,1]{0,1:T(1,128)} %param.11) | copy-start | bytes 28
  13.7 9.3 %copy-start.4 = (s32[3,1]{0,1:T(1,128)S(1)}, s32[3,1]{0,1:T(1,128)}, u32[]{:S(2)}) copy-start(s32[3,1]{0,1:T(1,128)} %param.10) | copy-start | bytes 40
  13.8 34.3 %copy-start.2 = (f32[8,24,512]{2,1,0:T(8,128)S(1)}, f32[8,24,512]{2,1,0:T(8,128)}, u32[]{:S(2)}) copy-start(f32[8,24,512]{2,1,0:T(8,128)} %halo_ref.1) | copy-start | bytes 1179652
  13.8 34.3 %copy-start.3 = (s32[24,512]{1,0:T(8,128)S(1)}, s32[24,512]{1,0:T(8,128)}, u32[]{:S(2)}) copy-start(s32[24,512]{1,0:T(8,128)} %mask_ref.1) | copy-start | bytes 147460
  15.9 32.2 %all-to-all-start = ((f32[16,24,512]{2,1,0:T(8,128)}), f32[16,24,512]{2,1,0:T(8,128)S(1)}, u32[]{:S(2)}, u32[]{:S(2)}) async-start(f32[16,24,512]{2,1,0:T(8,128)} %shard_map.67), calls=%async_computation | async-start | bytes 1572864 | tf_op jit(solution)/shard_map/all_to_all | solution.py:270
